TPU v7x, 32 devices: a whole 2x2x4 slice. The times are simulated.
32 devices in a mesh: ctx: 8 (over z, x), tp: 4 (over y, core).
Axes of the slice: x: 2, y: 2, z: 4, core: 2. Of those that a mesh axis runs over, the one named last changes fastest.
Arguments:
- features: bfloat16 [4096, 3, 4096], P(('ctx', 'tp')), may hold values from -6 to 6
- residual: bfloat16 [4096, 4096], P(('ctx', 'tp')), may hold values from -6 to 6
- short_weight: float32 [7, 3, 4096], P(None, None, 'tp'), may hold values from -2 to 2
- rates: float32 [256, 16], P('tp'), may hold values from 0.00012207031 to 0.06
- residues: float32 [256, 16], P('tp'), may hold values from -1.5 to 1.5
- out_weight: bfloat16 [4096, 4096], P('tp'), may hold values from -0.09375 to 0.09375
Outputs:
- mixed: bfloat16 [4096, 4096], P(('ctx', 'tp'))
All inputs are finite; a program needn't handle non-finite values.
Results may differ from a plain program's by a relative error of at most 0.023.
Values may be sent and summed in bfloat16 or wider, within the bound.
No kernel may reach another device: no remote copies, remote signals or barrier semaphores. Data moves between devices by JAX's collectives and lax.ppermute only.
A program may use at most 128 MiB of HBM per device.

v0:
```python
import jax
import jax.numpy as jnp
from jax import lax
from jax.sharding import PartitionSpec as P

ORDER = 16
GROUP_CH = 16


precise_mode = lax.Precision.HIGHEST


def from_behind(value, axis, by):
    devices = lax.axis_size(axis)
    pairs = [(i, i + by) for i in range(devices) if 0 <= i + by < devices]
    return lax.ppermute(value, axis, pairs)


def local_terms(product, rates, coefs):
    block_len = product.shape[0]
    steps_idx = jnp.arange(block_len, dtype=jnp.int32)
    valid = steps_idx[:, None] >= steps_idx[None, :]
    position = steps_idx.astype(jnp.float32)
    falling = coefs[:, :, None] * jnp.exp(-rates[:, :, None] * position)
    rising = jnp.exp(rates[:, :, None] * position)
    matrix = jnp.einsum("gnt,gns->gts", falling, rising, precision=precise_mode)
    matrix = jnp.where(valid[None], matrix, 0.0)
    local = jnp.einsum("gts,sgc->gtc", matrix, product, precision=precise_mode)
    outof = jnp.exp(-rates[:, :, None] * (block_len - 1.0 - position))
    state_here = jnp.einsum("gnt,tgc->ngc", outof, product, precision=precise_mode)
    return (local, state_here)


def carry_terms(rates, coefs, state_in, block_len):
    position = jnp.arange(block_len, dtype=jnp.int32).astype(jnp.float32)
    into = coefs[:, :, None] * jnp.exp(-rates[:, :, None] * (position + 1.0))
    return jnp.einsum("gnt,ngc->gtc", into, state_in, precision=precise_mode)


def body(features, residual, short_weight, rates, residues, out_weight):
    block = lax.all_to_all(features, "tp", split_axis=2, concat_axis=0, tiled=True)
    edge_rows = from_behind(block[-6:], "ctx", 1)
    padded = jnp.concatenate([edge_rows, block], 0)
    padded = padded.astype(jnp.float32)
    block_len = padded.shape[0] - 6
    short = short_weight[0] * padded[6:]
    for tap_index in range(1, 7):
        short = short + short_weight[tap_index] * padded[6 - tap_index : 6 - tap_index + block_len]
    query = short[:, 0]
    groups = rates.shape[0]
    product = (short[:, 1] * short[:, 2]).reshape(block_len, groups, GROUP_CH)
    coefs = residues * jnp.sqrt(1.0 - jnp.exp(-2.0 * rates))
    local, state_here = local_terms(product, rates, coefs)
    state_flat = state_here.reshape(ORDER, groups * GROUP_CH)
    decay = jnp.repeat(jnp.exp(-jnp.transpose(rates) * block_len), GROUP_CH, axis=1)

    def relay(turn, incoming):
        return from_behind(decay * incoming + state_flat, "ctx", 1)

    incoming = lax.fori_loop(0, lax.axis_size("ctx") - 1, relay, jnp.zeros_like(state_flat))
    carried = carry_terms(rates, coefs, incoming.reshape(ORDER, groups, GROUP_CH), block_len)
    long_out = jnp.transpose(local + carried, (1, 0, 2)).reshape(block_len, groups * GROUP_CH)
    gated = (query * long_out).astype(jnp.bfloat16)
    summed = lax.psum_scatter(
        jnp.dot(gated, out_weight, preferred_element_type=jnp.float32).astype(jnp.bfloat16),
        "tp",
        scatter_dimension=0,
        tiled=True,
    ).astype(jnp.float32)
    return (residual.astype(jnp.float32) + summed).astype(jnp.bfloat16)


def solution(mesh):
    in_specs = (
        P(("ctx", "tp"), None, None),
        P(("ctx", "tp"), None),
        P(None, None, "tp"),
        P("tp", None),
        P("tp", None),
        P("tp", None),
    )
    out_specs = P(("ctx", "tp"), None)
    return jax.shard_map(body, mesh=mesh, in_specs=in_specs, out_specs=out_specs, check_vma=False)
```

profile of v0, /device:TPU:0, one launch (start us, length us, event | category | flops | bytes accessed | tf_op | source)
XLA Modules:
  0.0 312.6 jit_solution(80744568132802990)
XLA Ops:
  6.5 7.2 %copy.29 = bf16[128,3,4096]{0,1,2:T(4,128)(2,1)} copy(bf16[128,3,4096]{2,0,1:T(8,128)(2,1)} %param.8) | data formatting | bytes 6291456 | tf_op args[0]
  13.8 5.0 %all-to-all-start = ((bf16[128,3,4096]{0,1,2:T(4,128)(2,1)}), bf16[128,3,4096]{0,1,2:T(4,128)(2,1)}, u32[]{:S(2)}, u32[]{:S(2)}) async-start(bf16[128,3,4096]{0,1,2:T(4,128)(2,1)} %copy.29), calls=%async_computation | async-start | bytes 8388608 | tf_op jit(solution)/shard_map/all_to_all | solution.py:41
  19.3 60.2 %fusion.21 = f32[64,512,512]{2,1,0:T(8,128)} fusion(f32[64,16]{1,0:T(8,128)S(1)} %copy.35, f32[512]{0:T(512)S(1)} %iota_convert_fusion, f32[64,16]{1,0:T(8,128)S(1)} %copy.34, f32[64,16]{1,0:T(8,128)S(1)} %copy.33), kind=kOutput, calls=%fused_computation.34 | convolution fusion | flops 3222798336 | bytes 67123200 | tf_op jit(solution)/shard_map/gnt,gns->gts/dot_general | solution.py:26
  79.5 6.8 %copy.54 = bf16[128,3,4,1024]{0,2,3,1:T(4,128)(2,1)} copy(bf16[128,3,4,1024]{0,1,3,2:T(4,128)(2,1)} %bitcast) | data formatting | bytes 6291456 | tf_op jit(solution)/shard_map/all_to_all | solution.py:41
  86.3 5.7 %all_to_all.16 = bf16[512,3,1024]{0,2,1:T(8,128)(2,1)} reshape(bf16[4,128,3,1024]{1,0,3,2:T(4,128)(2,1)} %bitcast.45) | data formatting | bytes 6291456 | tf_op jit(solution)/shard_map/all_to_all | solution.py:41
  92.0 1.4 slice.72
  93.7 5.0 %collective-permute-start.1 = (bf16[6,3,1024]{2,0,1:T(8,128)(2,1)S(1)}, bf16[6,3,1024]{2,0,1:T(8,128)(2,1)S(1)}, u32[]{:S(2)}, u32[]{:S(2)}) collective-permute-start(bf16[6,3,1024]{2,0,1:T(8,128)(2,1)S(1)} %copy.31), channel_id=1, source_target_pairs={{0,4},{4,8},{8,12},{12,16},{16,20},{20,24},{24,28},{1,5},{5,9},{9,... | collective-permute-start | bytes 110600 | tf_op jit(solution)/shard_map/ppermute | solution.py:16
  98.8 1.7 collective-permute-done.1
  100.9 3.6 %maximum_convert_fusion = f32[518,3,1024]{0,2,1:T(8,128)S(1)} fusion(bf16[512,3,1024]{0,2,1:T(8,128)(2,1)} %all_to_all.16, bf16[6,3,1024]{0,2,1:T(8,128)(2,1)S(1)} %copy.32), kind=kLoop, calls=%fused_computation.20 | loop fusion | flops 6365184 | bytes 9547776 | tf_op jit(solution)/shard_map/convert_element_type | solution.py:44
  104.5 14.1 %fusion.6 = f32[512,3,1024]{0,2,1:T(8,128)S(1)} fusion(f32[518,3,1024]{0,2,1:T(8,128)S(1)} %maximum_convert_fusion, f32[3,1024]{1,0:T(4,128)S(1)} %get-tuple-element.73, f32[3,1024]{1,0:T(4,128)S(1)} %get-tuple-element.74, f32[3,1024]{1,0:T(4,128)S(1)} %get-tuple-element.75, f32[3,1024]{1,0:T(4,128)S(1)} %get-tuple-element.76, ...), kind=kLoop, calls=%fused_computation.7 | loop fusion | flops 20447232 | bytes 50417664 | tf_op jit(solution)/shard_map/add | solution.py:48
  119.1 2.6 fusion.14
  121.8 51.7 %while.11 = (s32[]{:T(128)}, f32[16,1024]{1,0:T(8,128)S(1)}, f32[16,1024]{1,0:T(8,128)S(1)}, f32[16,64]{1,0:T(8,128)S(1)}, s32[]{:T(128)}) while((s32[]{:T(128)}, f32[16,1024]{1,0:T(8,128)S(1)}, f32[16,1024]{1,0:T(8,128)S(1)}, f32[16,64]{1,0:T(8,128)S(1)}, s32[]{:T(128)}) %tuple.36), condition=%wide.region_1.2_spmd.clone, body=%wide.region_0.1_spmd.clone.sunk | while | flops 32770 | bytes 725093 | solution.py:60
  122.3 4.2 %collective-permute-start = (f32[16,1024]{1,0:T(8,128)S(1)}, f32[16,1024]{1,0:T(8,128)S(1)}, u32[]{:S(2)}, u32[]{:S(2)}) collective-permute-start(f32[16,1024]{1,0:T(8,128)S(1)} %multiply_add_fusion.2), channel_id=1, source_target_pairs={{0,4},{4,8},{8,12},{12,16},{16,20},{20,24},{24,28},{1,5},{5,9},{9,... | collective-permute-start | bytes 196616 | tf_op jit(solution)/shard_map/while/body/eval_jaxpr/ppermute | solution.py:16
  126.6 1.9 collective-permute-done
  129.0 4.3 %collective-permute-start = (f32[16,1024]{1,0:T(8,128)S(1)}, f32[16,1024]{1,0:T(8,128)S(1)}, u32[]{:S(2)}, u32[]{:S(2)}) collective-permute-start(f32[16,1024]{1,0:T(8,128)S(1)} %multiply_add_fusion.2), channel_id=1, source_target_pairs={{0,4},{4,8},{8,12},{12,16},{16,20},{20,24},{24,28},{1,5},{5,9},{9,... | collective-permute-start | bytes 196616 | tf_op jit(solution)/shard_map/while/body/eval_jaxpr/ppermute | solution.py:16
  133.3 1.9 collective-permute-done
  135.7 5.2 %collective-permute-start = (f32[16,1024]{1,0:T(8,128)S(1)}, f32[16,1024]{1,0:T(8,128)S(1)}, u32[]{:S(2)}, u32[]{:S(2)}) collective-permute-start(f32[16,1024]{1,0:T(8,128)S(1)} %multiply_add_fusion.2), channel_id=1, source_target_pairs={{0,4},{4,8},{8,12},{12,16},{16,20},{20,24},{24,28},{1,5},{5,9},{9,... | collective-permute-start | bytes 196616 | tf_op jit(solution)/shard_map/while/body/eval_jaxpr/ppermute | solution.py:16
  140.9 1.9 collective-permute-done
  143.2 5.2 %collective-permute-start = (f32[16,1024]{1,0:T(8,128)S(1)}, f32[16,1024]{1,0:T(8,128)S(1)}, u32[]{:S(2)}, u32[]{:S(2)}) collective-permute-start(f32[16,1024]{1,0:T(8,128)S(1)} %multiply_add_fusion.2), channel_id=1, source_target_pairs={{0,4},{4,8},{8,12},{12,16},{16,20},{20,24},{24,28},{1,5},{5,9},{9,... | collective-permute-start | bytes 196616 | tf_op jit(solution)/shard_map/while/body/eval_jaxpr/ppermute | solution.py:16
  148.4 1.9 collective-permute-done
  150.8 5.2 %collective-permute-start = (f32[16,1024]{1,0:T(8,128)S(1)}, f32[16,1024]{1,0:T(8,128)S(1)}, u32[]{:S(2)}, u32[]{:S(2)}) collective-permute-start(f32[16,1024]{1,0:T(8,128)S(1)} %multiply_add_fusion.2), channel_id=1, source_target_pairs={{0,4},{4,8},{8,12},{12,16},{16,20},{20,24},{24,28},{1,5},{5,9},{9,... | collective-permute-start | bytes 196616 | tf_op jit(solution)/shard_map/while/body/eval_jaxpr/ppermute | solution.py:16
  156.0 2.1 collective-permute-done
  158.6 5.4 %collective-permute-start = (f32[16,1024]{1,0:T(8,128)S(1)}, f32[16,1024]{1,0:T(8,128)S(1)}, u32[]{:S(2)}, u32[]{:S(2)}) collective-permute-start(f32[16,1024]{1,0:T(8,128)S(1)} %multiply_add_fusion.2), channel_id=1, source_target_pairs={{0,4},{4,8},{8,12},{12,16},{16,20},{20,24},{24,28},{1,5},{5,9},{9,... | collective-permute-start | bytes 196616 | tf_op jit(solution)/shard_map/while/body/eval_jaxpr/ppermute | solution.py:16
  164.0 1.9 collective-permute-done
  166.4 5.3 %collective-permute-start = (f32[16,1024]{1,0:T(8,128)S(1)}, f32[16,1024]{1,0:T(8,128)S(1)}, u32[]{:S(2)}, u32[]{:S(2)}) collective-permute-start(f32[16,1024]{1,0:T(8,128)S(1)} %multiply_add_fusion.2), channel_id=1, source_target_pairs={{0,4},{4,8},{8,12},{12,16},{16,20},{20,24},{24,28},{1,5},{5,9},{9,... | collective-permute-start | bytes 196616 | tf_op jit(solution)/shard_map/while/body/eval_jaxpr/ppermute | solution.py:16
  171.7 1.9 collective-permute-done
  173.7 65.3 %fusion.2 = f32[64,512,16]{1,2,0:T(8,128)} fusion(f32[512,64,16]{0,2,1:T(8,128)S(1)} %bitcast.44, f32[64,512,512]{2,1,0:T(8,128)} %fusion.21, pred[512,512]{1,0:T(8,128)(4,1)S(1)} %iota_compare_fusion), kind=kOutput, calls=%fused_computation.2 | convolution fusion | flops 3238002688 | bytes 71565312 | tf_op jit(solution)/shard_map/gts,sgc->gtc/dot_general | solution.py:28
  239.1 3.8 %fusion.27 = f32[64,512,16]{1,2,0:T(8,128)S(1)} fusion(f32[64,512,16]{1,2,0:T(8,128)} %fusion.2, f32[16,64,16]{0,2,1:T(8,128)S(1)} %bitcast.46, f32[512]{0:T(512)S(1)} %fusion.40, f32[64,16]{1,0:T(8,128)S(1)} %copy.34, f32[64,16]{1,0:T(8,128)S(1)} %copy.33), kind=kOutput, calls=%fused_computation.40 | convolution fusion | flops 102236160 | bytes 4270080 | tf_op jit(solution)/shard_map/gnt,ngc->gtc/dot_general | solution.py:37
  242.9 2.0 fusion.13
  245.0 9.5 %convolution_convert_fusion = bf16[512,4096]{1,0:T(8,128)(2,1)} fusion(bf16[512,1024]{0,1:T(8,128)(2,1)S(1)} %fusion.13, bf16[1024,4096]{1,0:T(8,128)(2,1)} %param.13), kind=kOutput, calls=%fused_computation.19 | convolution fusion | flops 4297064448 | bytes 13631488 | tf_op jit(solution)/shard_map/dot_general | solution.py:65
  254.5 48.8 %reduce-scatter.2.cloned.1.call-done = bf16[128,4096]{1,0:T(8,128)(2,1)} async-done(((bf16[512,4096]{1,0:T(8,128)(2,1)}), bf16[128,4096]{1,0:T(8,128)(2,1)}) %reduce-scatter.2.cloned.1.call-update) | async-done | bytes 1048592 | tf_op jit(solution)/shard_map/reduce_scatter | solution.py:64
  303.3 2.4 add_convert_fusion
  (53 shorter events, 5.4 us)
Async XLA Ops:
  13.7 5.2 %copy-start.2 = (f32[7,3,1024]{2,0,1:T(8,128)S(1)}, f32[7,3,1024]{2,0,1:T(8,128)}, u32[]{:S(2)}) copy-start(f32[7,3,1024]{2,0,1:T(8,128)} %param.10) | copy-start | bytes 258052
  13.8 5.2 %copy-start.3 = (f32[64,16]{0,1:T(8,128)S(1)}, f32[64,16]{0,1:T(8,128)}, u32[]{:S(2)}) copy-start(f32[64,16]{0,1:T(8,128)} %param.11) | copy-start | bytes 12292
  13.8 5.3 %copy-start.4 = (f32[64,16]{0,1:T(8,128)S(1)}, f32[64,16]{0,1:T(8,128)}, u32[]{:S(2)}) copy-start(f32[64,16]{0,1:T(8,128)} %param.12) | copy-start | bytes 12292
  13.8 65.7 %all-to-all-start = ((bf16[128,3,4096]{0,1,2:T(4,128)(2,1)}), bf16[128,3,4096]{0,1,2:T(4,128)(2,1)}, u32[]{:S(2)}, u32[]{:S(2)}) async-start(bf16[128,3,4096]{0,1,2:T(4,128)(2,1)} %copy.29), calls=%async_computation | async-start | bytes 8388608 | tf_op jit(solution)/shard_map/all_to_all | solution.py:41
  18.7 284.6 %reduce-scatter.2.cloned.1.call-start = ((), (), s32[]{:S(2)}) async-start(), calls=%async_computation.2 | async-start | bytes 5242880 | tf_op jit(solution)/shard_map/reduce_scatter | solution.py:64
  93.7 6.8 %collective-permute-start.1 = (bf16[6,3,1024]{2,0,1:T(8,128)(2,1)S(1)}, bf16[6,3,1024]{2,0,1:T(8,128)(2,1)S(1)}, u32[]{:S(2)}, u32[]{:S(2)}) collective-permute-start(bf16[6,3,1024]{2,0,1:T(8,128)(2,1)S(1)} %copy.31), channel_id=1, source_target_pairs={{0,4},{4,8},{8,12},{12,16},{16,20},{20,24},{24,28},{1,5},{5,9},{9,... | collective-permute-start | bytes 110600 | tf_op jit(solution)/shard_map/ppermute | solution.py:16
  118.6 3.1 copy-start
  122.3 6.1 %collective-permute-start = (f32[16,1024]{1,0:T(8,128)S(1)}, f32[16,1024]{1,0:T(8,128)S(1)}, u32[]{:S(2)}, u32[]{:S(2)}) collective-permute-start(f32[16,1024]{1,0:T(8,128)S(1)} %multiply_add_fusion.2), channel_id=1, source_target_pairs={{0,4},{4,8},{8,12},{12,16},{16,20},{20,24},{24,28},{1,5},{5,9},{9,... | collective-permute-start | bytes 196616 | tf_op jit(solution)/shard_map/while/body/eval_jaxpr/ppermute | solution.py:16
  129.0 6.2 %collective-permute-start = (f32[16,1024]{1,0:T(8,128)S(1)}, f32[16,1024]{1,0:T(8,128)S(1)}, u32[]{:S(2)}, u32[]{:S(2)}) collective-permute-start(f32[16,1024]{1,0:T(8,128)S(1)} %multiply_add_fusion.2), channel_id=1, source_target_pairs={{0,4},{4,8},{8,12},{12,16},{16,20},{20,24},{24,28},{1,5},{5,9},{9,... | collective-permute-start | bytes 196616 | tf_op jit(solution)/shard_map/while/body/eval_jaxpr/ppermute | solution.py:16
  135.7 7.1 %collective-permute-start = (f32[16,1024]{1,0:T(8,128)S(1)}, f32[16,1024]{1,0:T(8,128)S(1)}, u32[]{:S(2)}, u32[]{:S(2)}) collective-permute-start(f32[16,1024]{1,0:T(8,128)S(1)} %multiply_add_fusion.2), channel_id=1, source_target_pairs={{0,4},{4,8},{8,12},{12,16},{16,20},{20,24},{24,28},{1,5},{5,9},{9,... | collective-permute-start | bytes 196616 | tf_op jit(solution)/shard_map/while/body/eval_jaxpr/ppermute | solution.py:16
  143.2 7.1 %collective-permute-start = (f32[16,1024]{1,0:T(8,128)S(1)}, f32[16,1024]{1,0:T(8,128)S(1)}, u32[]{:S(2)}, u32[]{:S(2)}) collective-permute-start(f32[16,1024]{1,0:T(8,128)S(1)} %multiply_add_fusion.2), channel_id=1, source_target_pairs={{0,4},{4,8},{8,12},{12,16},{16,20},{20,24},{24,28},{1,5},{5,9},{9,... | collective-permute-start | bytes 196616 | tf_op jit(solution)/shard_map/while/body/eval_jaxpr/ppermute | solution.py:16
  150.8 7.3 %collective-permute-start = (f32[16,1024]{1,0:T(8,128)S(1)}, f32[16,1024]{1,0:T(8,128)S(1)}, u32[]{:S(2)}, u32[]{:S(2)}) collective-permute-start(f32[16,1024]{1,0:T(8,128)S(1)} %multiply_add_fusion.2), channel_id=1, source_target_pairs={{0,4},{4,8},{8,12},{12,16},{16,20},{20,24},{24,28},{1,5},{5,9},{9,... | collective-permute-start | bytes 196616 | tf_op jit(solution)/shard_map/while/body/eval_jaxpr/ppermute | solution.py:16
  158.6 7.3 %collective-permute-start = (f32[16,1024]{1,0:T(8,128)S(1)}, f32[16,1024]{1,0:T(8,128)S(1)}, u32[]{:S(2)}, u32[]{:S(2)}) collective-permute-start(f32[16,1024]{1,0:T(8,128)S(1)} %multiply_add_fusion.2), channel_id=1, source_target_pairs={{0,4},{4,8},{8,12},{12,16},{16,20},{20,24},{24,28},{1,5},{5,9},{9,... | collective-permute-start | bytes 196616 | tf_op jit(solution)/shard_map/while/body/eval_jaxpr/ppermute | solution.py:16
  166.4 7.2 %collective-permute-start = (f32[16,1024]{1,0:T(8,128)S(1)}, f32[16,1024]{1,0:T(8,128)S(1)}, u32[]{:S(2)}, u32[]{:S(2)}) collective-permute-start(f32[16,1024]{1,0:T(8,128)S(1)} %multiply_add_fusion.2), channel_id=1, source_target_pairs={{0,4},{4,8},{8,12},{12,16},{16,20},{20,24},{24,28},{1,5},{5,9},{9,... | collective-permute-start | bytes 196616 | tf_op jit(solution)/shard_map/while/body/eval_jaxpr/ppermute | solution.py:16
  254.5 48.9 %copy-start.1 = (bf16[128,4096]{1,0:T(8,128)(2,1)S(1)}, bf16[128,4096]{1,0:T(8,128)(2,1)}, u32[]{:S(2)}) copy-start(bf16[128,4096]{1,0:T(8,128)(2,1)} %param.9) | copy-start | bytes 3145732
Sparse Core Ops, SparseCore 0:
  254.6 48.6 reduce-scatter.1
where the time goes:
time: 314 us; the launch traced here: 313 us
  matrix products  141 us (45%)
  waiting for transfers between devices  64 us (20%)
  starting transfers between devices  44.8 us (14%)
  local copies, waits for them, and re-layouts  25.8 us (8%)
  other arithmetic  22.8 us (7%)
  between operations  13.6 us (4%)
    dot_general x1, matrix products, local_terms(): local = jnp.einsum('gts,sgc->gtc', matrix, product, precision=precise_mode)  65.3 us
    dot_general x1, matrix products, local_terms(): matrix = jnp.einsum('gnt,gns->gts', falling, rising, precision=precise_mode)  60.2 us
    reduce_scatter x1, waiting for transfers between devices, body(): lax.psum_scatter(jnp.dot(gated, out_weight, preferred_element_type=jnp.fl...  48.8 us
    ppermute x8, starting transfers between devices, from_behind(): return lax.ppermute(value, axis, pairs)  39.8 us
    ppermute x8, waiting for transfers between devices, from_behind(): return lax.ppermute(value, axis, pairs)  15.1 us
    add x1, other arithmetic, body(): short + short_weight[tap_index] * padded[6 - tap_index:6 - tap_index + bl...  14.1 us
    all_to_all x2, local copies, waits for them, and re-layouts, body(): lax.all_to_all(features, 'tp', split_axis=2, concat_axis=0, tiled=True)  12.5 us
    dot_general x1, matrix products, body(): jnp.dot(gated, out_weight, preferred_element_type=jnp.float32)  9.51 us
  transfers between devices with their start and end apart: 10, of which 9 were waited for; matrix products, arithmetic and copies ran while one was open for 19% of the time, Pallas kernels for 0%

commit v1 on v0

v1 whole, which is shorter than its diff:
```python
import functools

import jax
import jax.numpy as jnp
from jax import lax
from jax.experimental import pallas as pl
from jax.experimental.pallas import tpu as pltpu
from jax.sharding import PartitionSpec as P

ORDER = 16
GROUP_CH = 16
LANES = 128
TAPS = 7
EDGE = 8
F32 = jnp.float32
BF16 = jnp.bfloat16
PER_TILE = LANES // GROUP_CH


def halves(value):
    high = value.astype(BF16)
    return high, (value - high.astype(F32)).astype(BF16)


def dot(a, b):
    return jnp.dot(a, b, preferred_element_type=F32)


def iota(shape, dim):
    return lax.broadcasted_iota(jnp.int32, shape, dim)


def own_group():
    return iota((LANES, LANES), 0) // ORDER == iota((LANES, LANES), 1) // GROUP_CH


def first_kernel(places, chips, info, feats, taps, rates, residues, kv_out, edge0, edge1, kv_taps, rate_row, coef_row, wide, *rest):
    q_outs, (last, sems) = rest[:places], rest[places:]
    rows, width = q_outs[0].shape
    core, chip = info[0] % 2, info[0] // 2
    copies = []
    for j in range(chips):
        start = pl.multiple_of((2 * j + 1 - core) * width, LANES)
        for branch in range(2):
            copies.append((feats.at[branch + 1, :, pl.ds(start, width)], kv_out.at[branch, :, pl.ds(j * width, width)]))
    copies.append((feats.at[:, pl.ds(rows - 2 * EDGE, 2 * EDGE), :], last))
    for out, (dy, dc) in zip(q_outs, moves(chips)):
        start = pl.multiple_of((2 * ((chip + dy) % chips) + (core + dc) % 2) * width, LANES)
        copies.append((feats.at[0, :, pl.ds(start, width)], out))
    copies = [pltpu.make_async_copy(source, target, sems.at[i]) for i, (source, target) in enumerate(copies)]
    for copy in copies:
        copy.start()

    rate, residue = rates[...], residues[...]
    coef = residue * jnp.sqrt(1.0 - jnp.exp(-2.0 * rate))
    lane_group = iota((ORDER, LANES), 1) // GROUP_CH
    diagonal = iota((ORDER, LANES), 1) % ORDER == iota((ORDER, LANES), 0)

    def spread(values, tile):
        out = jnp.broadcast_to(values[:, tile * PER_TILE : tile * PER_TILE + 1], (ORDER, LANES))
        for g in range(1, PER_TILE):
            at = tile * PER_TILE + g
            out = jnp.where(lane_group == g, jnp.broadcast_to(values[:, at : at + 1], (ORDER, LANES)), out)
        return out

    for b in range(2):
        kv_taps[b, 0:TAPS, :] = taps[b + 1]
    for tile in range(width // LANES):
        lanes = slice(tile * LANES, (tile + 1) * LANES)
        wide_rate = spread(rate, tile)
        wide[:, lanes] = wide_rate
        row = jnp.sum(jnp.where(diagonal, wide_rate, 0.0), axis=0, keepdims=True)
        rate_row[:, lanes] = row
        coef_row[:, lanes] = jnp.sum(jnp.where(diagonal, spread(coef, tile), 0.0), axis=0, keepdims=True)
        for b in range(2):
            kv_taps[b, TAPS : TAPS + 1, lanes] = row
    for copy in copies:
        copy.wait()
    for c, out in ((0, edge0), (1, edge1)):
        for j in range(chips):
            cols = slice((2 * j + c) * width, (2 * j + c + 1) * width)
            for branch in range(3):
                tail = last[branch, :, cols].astype(F32)[EDGE:]
                out[branch, :, j * width : (j + 1) * width] = tail.astype(BF16)


def moves(chips):
    return [(dy, dc) for dy in range(chips) for dc in range(2) if dy or dc]


def first(info, feats, taps, rates, residues, chips):
    _, rows, depth = feats.shape
    width = taps.shape[2]
    places = 2 * chips - 1
    vmem = pl.BlockSpec(memory_space=pltpu.VMEM)
    return pl.pallas_call(
        functools.partial(first_kernel, places, chips),
        out_shape=[
            jax.ShapeDtypeStruct((2, rows, chips * width), BF16),
            jax.ShapeDtypeStruct((3, EDGE, chips * width), BF16),
            jax.ShapeDtypeStruct((3, EDGE, chips * width), BF16),
            jax.ShapeDtypeStruct((2, TAPS + 1, width), F32),
            jax.ShapeDtypeStruct((1, width), F32),
            jax.ShapeDtypeStruct((1, width), F32),
            jax.ShapeDtypeStruct((ORDER, width), F32),
        ]
        + [jax.ShapeDtypeStruct((rows, width), BF16)] * places,
        in_specs=[pl.BlockSpec(memory_space=pltpu.SMEM), pl.BlockSpec(memory_space=pl.ANY), vmem, vmem, vmem],
        out_specs=[vmem] * (7 + places),
        scratch_shapes=[pltpu.VMEM((3, 2 * EDGE, depth), BF16), pltpu.SemaphoreType.DMA((2 * chips + 1 + places,))],
        compiler_params=pltpu.CompilerParams(vmem_limit_bytes=32 << 20),
    )(info, feats, taps, rates, residues)


def fold(product, mask):
    kept = jnp.where(mask, product, 0.0)
    return jnp.sum(kept.reshape(PER_TILE, ORDER, LANES), axis=0)


def convolve(padded, taps, start, count):
    total = taps[0:1] * padded[EDGE + start : EDGE + start + count]
    for j in range(1, TAPS):
        total = total + taps[j : j + 1] * padded[EDGE - j + start : EDGE - j + start + count]
    return total


def front_kernel(chunk, info, k_own, v_own, kv_in, edge0, edge1, taps, near, far, state, pad_k, pad_v, prod):
    rows, width = k_own.shape[1:]
    core = info[0] % 2
    chip_rows = 2 * rows
    chunks = chip_rows // chunk
    mine = pl.multiple_of(EDGE + core * rows, 8)
    other = pl.multiple_of(EDGE + (1 - core) * rows, 8)
    step = min(64, chip_rows)
    mask = own_group()
    age = (chunk - 1 - iota((LANES, chunk), 1)).astype(F32)
    for w in range(width // LANES):
        lanes = slice(w * LANES, (w + 1) * LANES)
        for b, own, pad in ((0, k_own, pad_k), (1, v_own, pad_v)):
            pad[0:EDGE, :] = edge0[b + 1, :, lanes].astype(F32) + edge1[b + 1, :, lanes].astype(F32)
            pad[pl.ds(mine, rows), :] = own[0, :, lanes].astype(F32)
            pad[pl.ds(other, rows), :] = kv_in[b, :, lanes].astype(F32)
        tap_k, tap_v = taps[0, :, lanes], taps[1, :, lanes]
        for start in range(0, chip_rows, step):
            value = convolve(pad_k, tap_k, start, step) * convolve(pad_v, tap_v, start, step)
            prod[start : start + step, :] = value.astype(BF16)
        near[0:rows, lanes] = prod[pl.ds(pl.multiple_of((1 - core) * rows, rows), rows), :]
        far[:, lanes] = prod[pl.ds(pl.multiple_of(core * rows, rows), rows), :]
        rate = jnp.broadcast_to(tap_k[TAPS : TAPS + 1], (LANES, LANES)).T
        high, low = halves(jnp.exp(-rate[:, :chunk] * age))
        beside = jnp.concatenate([prod[i * chunk : (i + 1) * chunk, :] for i in range(chunks)], axis=1)
        reached = dot(high, beside) + dot(low, beside)
        fade = jnp.exp(-rate * float(chunk))
        total = reached[:, :LANES]
        for i in range(1, chunks):
            at = rows + 2 * ORDER * (i - 1)
            inner_high, inner_low = halves(fold(total, mask))
            near[at : at + ORDER, lanes] = inner_high
            near[at + ORDER : at + 2 * ORDER, lanes] = inner_low
            total = fade * total + reached[:, i * LANES : (i + 1) * LANES]
        state[0:ORDER, lanes] = fold(total, mask)
        state[ORDER : ORDER + EDGE, lanes] = edge0[0, :, lanes].astype(F32) + edge1[0, :, lanes].astype(F32)


def front(info, d, chips, feats, kv_in, edge0, edge1, taps, chunk):
    rows = feats.shape[1]
    width = taps.shape[2]
    block = min(512, width)
    per = width // block
    chip_rows = 2 * rows
    stored = rows + 2 * ORDER * (chip_rows // chunk - 1)

    def target(info):
        return (info[0] // 2 + d) % chips

    def own(branch):
        return pl.BlockSpec((1, rows, block), lambda i, info: (branch, 0, (2 * target(info) + info[0] % 2) * per + i))

    return pl.pallas_call(
        functools.partial(front_kernel, chunk),
        grid_spec=pltpu.PrefetchScalarGridSpec(
            num_scalar_prefetch=1,
            grid=(per,),
            in_specs=[
                own(1),
                own(2),
                pl.BlockSpec((2, rows, block), lambda i, info: (0, 0, target(info) * per + i)),
                pl.BlockSpec((3, EDGE, block), lambda i, info: (0, 0, target(info) * per + i)),
                pl.BlockSpec((3, EDGE, block), lambda i, info: (0, 0, target(info) * per + i)),
                pl.BlockSpec((2, TAPS + 1, block), lambda i, info: (0, 0, i)),
            ],
            out_specs=[
                pl.BlockSpec((stored, block), lambda i, info: (0, i)),
                pl.BlockSpec((rows, block), lambda i, info: (0, i)),
                pl.BlockSpec((ORDER + EDGE, block), lambda i, info: (0, i)),
            ],
            scratch_shapes=[pltpu.VMEM((EDGE + chip_rows, LANES), F32)] * 2 + [pltpu.VMEM((chip_rows, LANES), BF16)],
        ),
        out_shape=[
            jax.ShapeDtypeStruct((stored, width), BF16),
            jax.ShapeDtypeStruct((rows, width), BF16),
            jax.ShapeDtypeStruct((ORDER + EDGE, width), F32),
        ],
        compiler_params=pltpu.CompilerParams(vmem_limit_bytes=32 << 20),
    )(info, feats, feats, kv_in, edge0, edge1, taps)


def query_kernel(chips, info, own, *rest):
    places = 2 * chips - 1
    pieces, (edge, taps, out, pad) = rest[:places], rest[places:]
    rows, width = own.shape[1:]
    total_rows = out.shape[0]
    step = min(64, total_rows)
    core, chip = info[0] % 2, info[0] // 2
    for w in range(width // LANES):
        lanes = slice(w * LANES, (w + 1) * LANES)
        pad[0:EDGE, :] = edge[:, lanes]
        pad[pl.ds(pl.multiple_of(EDGE + info[0] * rows, 8), rows), :] = own[0, :, lanes].astype(F32)
        for piece, (dy, dc) in zip(pieces, moves(chips)):
            source = 2 * ((chip + chips - dy) % chips) + (core + dc) % 2
            pad[pl.ds(pl.multiple_of(EDGE + source * rows, 8), rows), :] = piece[:, lanes].astype(F32)
        tap = taps[0, :, lanes]
        for start in range(0, total_rows, step):
            out[start : start + step, lanes] = convolve(pad, tap, start, step)


def query(info, chips, feats, pieces, edge, taps):
    rows, width = pieces[0].shape
    places = len(pieces)
    block = min(512, width)
    per = width // block
    total_rows = rows * (places + 1)
    return pl.pallas_call(
        functools.partial(query_kernel, chips),
        grid_spec=pltpu.PrefetchScalarGridSpec(
            num_scalar_prefetch=1,
            grid=(per,),
            in_specs=[pl.BlockSpec((1, rows, block), lambda i, info: (0, 0, info[0] * per + i))]
            + [pl.BlockSpec((rows, block), lambda i, info: (0, i))] * places
            + [
                pl.BlockSpec((EDGE, block), lambda i, info: (0, i)),
                pl.BlockSpec((1, TAPS, block), lambda i, info: (0, 0, i)),
            ],
            out_specs=pl.BlockSpec((total_rows, block), lambda i, info: (0, i)),
            scratch_shapes=[pltpu.VMEM((EDGE + total_rows, LANES), F32)],
        ),
        out_shape=jax.ShapeDtypeStruct((total_rows, width), F32),
        compiler_params=pltpu.CompilerParams(vmem_limit_bytes=32 << 20),
    )(info, feats, *pieces, edge, taps)


def toeplitz_kernel(chunk, rate_row, coef_row, out):
    lag = (LANES - 1 - iota((LANES, LANES), 1)).astype(F32)
    rate = jnp.broadcast_to(rate_row[...], (LANES, LANES)).T
    coef = jnp.broadcast_to(coef_row[...], (LANES, LANES)).T
    taps = jnp.sum((coef * jnp.exp(-rate * lag)).reshape(PER_TILE, ORDER, LANES), axis=1)
    valid = iota((LANES, LANES), 1) <= iota((LANES, LANES), 0)
    for g in range(PER_TILE):
        spread = jnp.broadcast_to(taps[g : g + 1], (LANES, LANES))
        block = jnp.where(valid, pltpu.roll(spread, 1, 1, stride=1, stride_axis=0), 0.0)
        out[g * chunk : (g + 1) * chunk, :] = block[:chunk, :chunk].astype(BF16)


def toeplitz(rate_row, coef_row, chunk):
    tiles = rate_row.shape[1] // LANES
    return pl.pallas_call(
        functools.partial(toeplitz_kernel, chunk),
        grid=(tiles,),
        in_specs=[pl.BlockSpec((1, LANES), lambda i: (0, i))] * 2,
        out_specs=pl.BlockSpec((PER_TILE * chunk, chunk), lambda i: (i, 0)),
        out_shape=jax.ShapeDtypeStruct((tiles * PER_TILE * chunk, chunk), BF16),
    )(rate_row, coef_row)


def gate_kernel(chunk, theirs, info, prod, inner, toep, q, start_state, wide_rates, rate_row, coef_row, out):
    rows, width = q.shape
    chunks = rows // chunk
    core = info[0] % 2
    half = 1 - core if theirs else core
    mask = own_group()
    lane_group = iota((chunk, LANES), 1) // GROUP_CH
    later = (iota((chunk, LANES), 0) + 1).astype(F32)
    for w in range(width // LANES):
        lanes = slice(w * LANES, (w + 1) * LANES)
        beside = jnp.concatenate([prod[i * chunk : (i + 1) * chunk, lanes] for i in range(chunks)], axis=1)
        blocks = toep[w * PER_TILE * chunk : (w + 1) * PER_TILE * chunk, :]
        local = dot(blocks, beside)
        into_high, into_low = halves(coef_row[:, lanes] * jnp.exp(-rate_row[:, lanes] * later))
        entering = []
        for i in range(chunks):
            place = half * chunks + i
            at = pl.multiple_of(rows + 2 * ORDER * jnp.maximum(place - 1, 0), ORDER)
            kept = inner[pl.ds(at, ORDER), lanes].astype(F32) + inner[pl.ds(at + ORDER, ORDER), lanes].astype(F32)
            state = jnp.exp(-wide_rates[:, lanes] * (place * chunk).astype(F32)) * start_state[:, lanes]
            state = state + jnp.where(place > 0, kept, 0.0)
            entering.append(jnp.where(mask, jnp.concatenate([state] * PER_TILE, axis=0), 0.0))
        state_high, state_low = halves(jnp.concatenate(entering, axis=1))
        carried = dot(into_high, state_high) + dot(into_high, state_low) + dot(into_low, state_high)
        for i in range(chunks):
            cols = slice(i * LANES, (i + 1) * LANES)
            kept = local[:chunk, cols]
            for g in range(1, PER_TILE):
                kept = jnp.where(lane_group == g, local[g * chunk : (g + 1) * chunk, cols], kept)
            gated = q[i * chunk : (i + 1) * chunk, lanes] * (kept + carried[:, cols])
            out[i * chunk : (i + 1) * chunk, lanes] = gated.astype(BF16)


def gate(info, d, chips, theirs, prod, inner, toep, q, start_state, wide_rates, rate_row, coef_row, chunk):
    rows = q.shape[0] // (2 * chips)
    width = q.shape[1]
    block = min(512, width)

    def place(info):
        core = info[0] % 2
        return 2 * ((info[0] // 2 + chips - d) % chips) + (1 - core if theirs else core)

    return pl.pallas_call(
        functools.partial(gate_kernel, chunk, theirs),
        grid_spec=pltpu.PrefetchScalarGridSpec(
            num_scalar_prefetch=1,
            grid=(width // block,),
            in_specs=[
                pl.BlockSpec((rows, block), lambda i, info: (0, i)),
                pl.BlockSpec((inner.shape[0], block), lambda i, info: (0, i)),
                pl.BlockSpec((block // GROUP_CH * chunk, chunk), lambda i, info: (i, 0)),
                pl.BlockSpec((rows, block), lambda i, info: (place(info), i)),
                pl.BlockSpec((ORDER, block), lambda i, info: (0, i)),
                pl.BlockSpec((ORDER, block), lambda i, info: (0, i)),
                pl.BlockSpec((1, block), lambda i, info: (0, i)),
                pl.BlockSpec((1, block), lambda i, info: (0, i)),
            ],
            out_specs=pl.BlockSpec((rows, block), lambda i, info: (0, i)),
        ),
        out_shape=jax.ShapeDtypeStruct((rows, width), BF16),
        compiler_params=pltpu.CompilerParams(vmem_limit_bytes=32 << 20),
    )(info, prod, inner, toep, q, start_state, wide_rates, rate_row, coef_row)


def body(chips, contexts, features, residual, short_weight, rates, residues, out_weight):
    rows, _, depth = features.shape
    chip_rows = 2 * rows
    context_rows = chips * chip_rows
    chunk = min(LANES, rows)
    tp, ctx = lax.axis_index("tp"), lax.axis_index("ctx")
    chip = tp // 2
    info = tp.astype(jnp.int32).reshape(1)

    def along_y(value, by):
        return lax.ppermute(value, "tp", [(i, (i + 2 * by) % (2 * chips)) for i in range(2 * chips)])

    def across(value):
        return lax.ppermute(value, "tp", [(i, i ^ 1) for i in range(2 * chips)])

    def with_context(value, bit):
        return lax.ppermute(value, "ctx", [(i, i ^ bit) for i in range(contexts)])

    feats = jnp.transpose(features, (1, 0, 2))
    taps = jnp.transpose(short_weight, (1, 0, 2))
    sent = first(info, feats, taps, jnp.transpose(rates), jnp.transpose(residues), chips)
    kv_out, edge0, edge1, kv_taps, rate_row, coef_row, wide_rates = sent[:7]

    kv_taps = [kv_taps] + [along_y(kv_taps, -d) for d in range(1, chips)]

    order = [(x, y) for x in range(contexts) for y in range(chips)]
    edges = []
    for c, part in ((0, edge0), (1, edge1)):
        pairs = [
            ((x * chips + y) * 2 + 1, (nx * chips + ny) * 2 + c) for (x, y), (nx, ny) in zip(order[:-1], order[1:])
        ]
        edges.append(lax.ppermute(part, ("ctx", "tp"), pairs))

    kv_in = across(kv_out)
    pieces = []
    for (dy, dc), part in zip(moves(chips), sent[7:]):
        pairs = [(2 * y + c, 2 * ((y + dy) % chips) + (c + dc) % 2) for y in range(chips) for c in range(2)]
        pieces.append(lax.ppermute(part, "tp", pairs))

    nears, fars, states = [None] * chips, [None] * chips, [None] * chips
    for d in list(range(1, chips)) + [0]:
        near, far, state = front(info, d, chips, feats, kv_in, edges[0], edges[1], kv_taps[d], chunk)
        if d > 0:
            state = along_y(state, d)
            near = along_y(near, d)
            far = along_y(far, d)
        nears[d], fars[d], states[d] = near, far, state

    toep_rates, _ = lax.optimization_barrier((rate_row, states[0]))
    toep = toeplitz(toep_rates, coef_row, chunk)

    def of_chip(values, y):
        return sum(jnp.where((chip - d) % chips == y, value, 0.0) for d, value in enumerate(values))

    by_chip = [of_chip(states, y) for y in range(chips)]
    chip_fade = jnp.exp(-wide_rates * float(chip_rows))
    total = by_chip[0][:ORDER]
    for y in range(1, chips):
        total = chip_fade * total + by_chip[y][:ORDER]

    before = jnp.zeros_like(total)
    bit = 1
    while bit < contexts:
        got = with_context(total, bit)
        upper = (ctx & bit) != 0
        place = (ctx & (bit - 1)).astype(F32)
        before = before + jnp.where(upper, jnp.exp(-wide_rates * (place * context_rows)) * got, 0.0)
        fade = jnp.exp(-wide_rates * float(bit * context_rows))
        total = jnp.where(upper, fade * got + total, fade * total + got)
        bit *= 2
    entering = [before]
    for y in range(chips - 1):
        entering.append(chip_fade * entering[-1] + by_chip[y][:ORDER])

    q = query(info, chips, feats, pieces, by_chip[0][ORDER:], taps)

    parts = 2
    cols = depth // parts
    sums = [residual[:, p * cols : (p + 1) * cols].astype(F32) for p in range(parts)]
    for d in list(range(1, chips)) + [0]:
        y = (chip - d) % chips
        start_state = sum(jnp.where(y == i, value, 0.0) for i, value in enumerate(entering))
        gated = [
            gate(info, d, chips, theirs, prod, nears[d], toep, q, start_state, wide_rates, rate_row, coef_row, chunk)
            for theirs, prod in ((True, nears[d]), (False, fars[d]))
        ]
        for p in range(parts):
            weights = out_weight[:, p * cols : (p + 1) * cols]
            theirs = across(dot(gated[0], weights).astype(BF16))
            mine = dot(gated[1], weights) + theirs.astype(F32)
            if d > 0:
                mine = along_y(mine.astype(BF16), -d).astype(F32)
            sums[p] = sums[p] + mine
    return jnp.concatenate([value.astype(BF16) for value in sums], axis=1)


def solution(mesh):
    chips, contexts = mesh.shape["tp"] // 2, mesh.shape["ctx"]
    in_specs = (
        P(("ctx", "tp"), None, None),
        P(("ctx", "tp"), None),
        P(None, None, "tp"),
        P("tp", None),
        P("tp", None),
        P("tp", None),
    )
    return jax.shard_map(
        functools.partial(body, chips, contexts),
        mesh=mesh,
        in_specs=in_specs,
        out_specs=P(("ctx", "tp"), None),
        check_vma=False,
    )
```

time: 314 us -> 108 us (0.34)
  matrix products: 141 us -> 14.7 us
  waiting for transfers between devices: 64 us -> 24.7 us
  starting transfers between devices: 44.8 us -> 22.4 us
  Pallas kernels: 0 us -> 20.9 us
  other arithmetic: 22.8 us -> 6.64 us
  between operations: 13.6 us -> 0.34 us
  local copies, waits for them, and re-layouts: 25.8 us -> 17.2 us
    dot_general x5 -> x8, matrix products: 141 us -> 14.7 us  [dot(): return jnp.dot(a, b, preferred_element_type=F32)]
    reduce_scatter x1 -> x0, waiting for transfers between devices: 48.8 us -> none  [body(): lax.psum_scatter(jnp.dot(gated, out_weight, preferred_element_type=jnp.fl...]
    pallas_call x0 -> x9, Pallas kernels: none -> 20.9 us  [the longest x2 6.32 us: front(): pl.pallas_call(functools.partial(front_kernel, chunk), grid_spec=pltpu.Pr...]
    ppermute x8 -> x19, starting transfers between devices: 39.8 us -> 22.4 us  [the longest x6 9.74 us: along_y(): lax.ppermute(value, 'tp', [(i, (i + 2 * by) % (2 * chips)) for i in range...]
    all_to_all x2 -> x0, local copies, waits for them, and re-layouts: 12.5 us -> none  [body(): lax.all_to_all(features, 'tp', split_axis=2, concat_axis=0, tiled=True)]
    add x9 -> x3, other arithmetic: 14.1 us -> 3.58 us  [the longest x1 1.98 us: body(): sum((jnp.where(y == i, value, 0.0) for i, value in enumerate(entering)))]
    ppermute x8 -> x19, waiting for transfers between devices: 15.1 us -> 24.7 us  [the longest x6 21.2 us: along_y(): lax.ppermute(value, 'tp', [(i, (i + 2 * by) % (2 * chips)) for i in range...]
    unnamed x17 -> x70, local copies, waits for them, and re-layouts: 7.52 us -> 16.3 us
  transfers between devices with their start and end apart: 10 -> 19, of which waited for: 9 -> 6; matrix products, arithmetic and copies ran while one was open for 19% -> 14% of each run, Pallas kernels for 0% -> 16%
where the time goes in v1:
time: 108 us; the launch traced here: 107 us
  waiting for transfers between devices  24.7 us (23%)
  starting transfers between devices  22.4 us (21%)
  Pallas kernels  20.9 us (19%)
  local copies, waits for them, and re-layouts  17.2 us (16%)
  matrix products  14.7 us (14%)
  other arithmetic  6.64 us (6%)
    ppermute x6, waiting for transfers between devices, along_y(): lax.ppermute(value, 'tp', [(i, (i + 2 * by) % (2 * chips)) for i in range...  21.2 us
    unnamed x70, local copies, waits for them, and re-layouts  16.3 us
    dot_general x8, matrix products, dot(): return jnp.dot(a, b, preferred_element_type=F32)  14.7 us
    ppermute x6, starting transfers between devices, along_y(): lax.ppermute(value, 'tp', [(i, (i + 2 * by) % (2 * chips)) for i in range...  9.74 us
    pallas_call x2, Pallas kernels, front(): pl.pallas_call(functools.partial(front_kernel, chunk), grid_spec=pltpu.Pr...  6.32 us
    pallas_call x4, Pallas kernels, gate(): pl.pallas_call(functools.partial(gate_kernel, chunk, theirs), grid_spec=p...  6.09 us
    ppermute x3, starting transfers between devices, with_context(): return lax.ppermute(value, 'ctx', [(i, i ^ bit) for i in range(contexts)])  5.65 us
    pallas_call x1, Pallas kernels, toeplitz(): pl.pallas_call(functools.partial(toeplitz_kernel, chunk), grid=(tiles,),...  5.2 us
  transfers between devices with their start and end apart: 19, of which 6 were waited for; matrix products, arithmetic and copies ran while one was open for 14% of the time, Pallas kernels for 16%

profile of v1, /device:TPU:0, one launch (start us, length us, event | category | flops | bytes accessed | tf_op | source)
XLA Modules:
  0.0 106.9 jit_solution(1619482720126366134)
XLA Ops:
  0.0 1.9 %copy-done = bf16[128,3,4096]{2,0,1:T(8,128)(2,1)S(1)} copy-done((bf16[128,3,4096]{2,0,1:T(8,128)(2,1)S(1)}, bf16[128,3,4096]{2,0,1:T(8,128)(2,1)}, u32[]{:S(2)}) %copy-start) | copy-done | bytes 3145752
  9.6 3.3 %collective-permute-start.3 = (f32[2,8,1024]{2,1,0:T(8,128)S(1)}, f32[2,8,1024]{2,1,0:T(8,128)S(1)}, u32[]{:S(2)}, u32[]{:S(2)}) collective-permute-start(f32[2,8,1024]{2,1,0:T(8,128)S(1)} %get-tuple-element.25.taps), channel_id=1, source_target_pairs={{0,2},{1,3},{2,0},{3,1},{4,6},{5,7},{6,4},{7,5},{8,10},{9,11},{10,... | collective-permute-start | bytes 196616 | tf_op jit(solution)/shard_map/ppermute | solution.py:349
  13.6 1.6 %collective-permute-done.3.taps = f32[2,8,1024]{2,1,0:T(8,128)S(1)} collective-permute-done((f32[2,8,1024]{2,1,0:T(8,128)S(1)}, f32[2,8,1024]{2,1,0:T(8,128)S(1)}, u32[]{:S(2)}, u32[]{:S(2)}) %collective-permute-start.3) | collective-permute-done | bytes 65568 | tf_op jit(solution)/shard_map/ppermute | solution.py:349
  15.3 3.5 %shard_map.65 = (bf16[160,1024]{1,0:T(8,128)(2,1)S(1)}, bf16[128,1024]{1,0:T(8,128)(2,1)S(1)}, f32[24,1024]{1,0:T(8,128)}) custom-call(s32[1]{0:T(128)} %bitcast.info, bf16[3,128,4096]{2,1,0:T(8,128)(2,1)S(1)} %bitcast.14, bf16[3,128,4096]{2,1,0:T(8,128)(2,1)S(1)} %bitcast.15, bf16[2,128,2048]{2,1,0:T(8,128)(2,1)S(1)} %collective-permute-done.kv_in, ...), custom_call_target="tpu_custom_call" | custom-call | tf_op jit(solution)/shard_map/pallas_call | solution.py:179
  20.2 2.4 %collective-permute-start.9 = (f32[24,1024]{1,0:T(8,128)}, f32[24,1024]{1,0:T(8,128)}, u32[]{:S(2)}, u32[]{:S(2)}) collective-permute-start(f32[24,1024]{1,0:T(8,128)} %get-tuple-element.35), channel_id=1, source_target_pairs={{0,2},{1,3},{2,0},{3,1},{4,6},{5,7},{6,4},{7,5},{8,10},{9,11},{10,... | collective-permute-start | bytes 294920 | tf_op jit(solution)/shard_map/ppermute | solution.py:349
  26.4 2.9 %shard_map.66 = (bf16[160,1024]{1,0:T(8,128)(2,1)S(1)}, bf16[128,1024]{1,0:T(8,128)(2,1)S(1)}, f32[24,1024]{1,0:T(8,128)S(1)}) custom-call(s32[1]{0:T(128)} %bitcast.info, bf16[3,128,4096]{2,1,0:T(8,128)(2,1)S(1)} %bitcast.16, bf16[3,128,4096]{2,1,0:T(8,128)(2,1)S(1)} %bitcast.17, bf16[2,128,2048]{2,1,0:T(8,128)(2,1)S(1)} %copy-done.7, ...), custom_call_target="tpu_custom_call" | custom-call | tf_op jit(solution)/shard_map/pallas_call | solution.py:179
  29.3 1.6 %fusion.47 = f32[16,1024]{1,0:T(8,128)} fusion(f32[24,1024]{1,0:T(8,128)} %collective-permute-done.9, f32[24,1024]{1,0:T(8,128)S(1)} %get-tuple-element.29, f32[24,1024]{1,0:T(8,128)S(1)} %select_add_fusion, f32[16,1024]{1,0:T(8,128)S(1)} %get-tuple-element.36.wide_rates, pred[]{:T(512)S(6)} %eq.26, pred[]{:T(512)S(6)} %eq.25), kind=kLoop, calls=%fused_computation.32 | loop fusion | flops 114688 | bytes 327682 | tf_op jit(solution)/shard_map/add | solution.py:397
  30.9 1.5 %collective-permute-start.10 = (f32[16,1024]{1,0:T(8,128)}, f32[16,1024]{1,0:T(8,128)}, u32[]{:S(2)}, u32[]{:S(2)}) collective-permute-start(f32[16,1024]{1,0:T(8,128)} %fusion.47), channel_id=1, source_target_pairs={{0,4},{4,0},{8,12},{12,8},{16,20},{20,16},{24,28},{28,24},{1,5},{5... | collective-permute-start | bytes 196616 | tf_op jit(solution)/shard_map/ppermute | solution.py:355
  32.4 3.1 %collective-permute-done.10 = f32[16,1024]{1,0:T(8,128)} collective-permute-done((f32[16,1024]{1,0:T(8,128)}, f32[16,1024]{1,0:T(8,128)}, u32[]{:S(2)}, u32[]{:S(2)}) %collective-permute-start.10) | collective-permute-done | bytes 65568 | tf_op jit(solution)/shard_map/ppermute | solution.py:355
  35.5 1.5 %add_select_fusion.1 = f32[16,1024]{1,0:T(8,128)} fusion(f32[16,1024]{1,0:T(8,128)} %collective-permute-done.10, f32[16,1024]{1,0:T(8,128)} %fusion.47, f32[16,1024]{1,0:T(8,128)S(1)} %get-tuple-element.36.wide_rates, pred[]{:T(512)S(6)} %ne.39), kind=kLoop, calls=%fused_computation.39 | loop fusion | flops 114688 | bytes 262145 | tf_op jit(solution)/shard_map/jit(_where)/select_n | solution.py:407
  37.0 1.6 %collective-permute-start.11 = (f32[16,1024]{1,0:T(8,128)}, f32[16,1024]{1,0:T(8,128)}, u32[]{:S(2)}, u32[]{:S(2)}) collective-permute-start(f32[16,1024]{1,0:T(8,128)} %add_select_fusion.1), channel_id=1, source_target_pairs={{0,8},{4,12},{8,0},{12,4},{16,24},{20,28},{24,16},{28,20},{1,9},{5... | collective-permute-start | bytes 196616 | tf_op jit(solution)/shard_map/ppermute | solution.py:355
  38.6 1.5 %collective-permute-start.6 = (bf16[128,1024]{1,0:T(8,128)(2,1)}, bf16[128,1024]{1,0:T(8,128)(2,1)}, u32[]{:S(2)}, u32[]{:S(2)}) collective-permute-start(bf16[128,1024]{1,0:T(8,128)(2,1)} %copy-done.28), channel_id=1, source_target_pairs={{0,1},{1,0},{2,3},{3,2},{4,5},{5,4},{6,7},{7,6},{8,9},{9,8},{10,11... | collective-permute-start | bytes 786440 | tf_op jit(solution)/shard_map/ppermute | solution.py:376
  40.1 2.5 %collective-permute-start.7 = (bf16[128,1024]{1,0:T(8,128)(2,1)}, bf16[128,1024]{1,0:T(8,128)(2,1)}, u32[]{:S(2)}, u32[]{:S(2)}) collective-permute-start(bf16[128,1024]{1,0:T(8,128)(2,1)} %copy-done.27), channel_id=1, source_target_pairs={{0,2},{1,3},{2,0},{3,1},{4,6},{5,7},{6,4},{7,5},{8,10},{9,11},{10,... | collective-permute-start | bytes 786440 | tf_op jit(solution)/shard_map/ppermute | solution.py:376
  42.6 1.5 %add_select_fusion = f32[16,1024]{1,0:T(8,128)} fusion(f32[16,1024]{1,0:T(8,128)} %collective-permute-done.11, f32[16,1024]{1,0:T(8,128)} %add_select_fusion.1, f32[16,1024]{1,0:T(8,128)S(1)} %get-tuple-element.36.wide_rates, pred[]{:T(512)S(6)} %ne.40), kind=kLoop, calls=%fused_computation.38 | loop fusion | flops 114688 | bytes 262145 | tf_op jit(solution)/shard_map/jit(_where)/select_n | solution.py:407
  44.1 2.6 %collective-permute-start.12 = (f32[16,1024]{1,0:T(8,128)}, f32[16,1024]{1,0:T(8,128)}, u32[]{:S(2)}, u32[]{:S(2)}) collective-permute-start(f32[16,1024]{1,0:T(8,128)} %add_select_fusion), channel_id=1, source_target_pairs={{0,16},{4,20},{8,24},{12,28},{16,0},{20,4},{24,8},{28,12},{1,17},{... | collective-permute-start | bytes 196616 | tf_op jit(solution)/shard_map/ppermute | solution.py:355
  46.7 1.6 %collective-permute-start.4 = (bf16[128,1024]{1,0:T(8,128)(2,1)}, bf16[128,1024]{1,0:T(8,128)(2,1)}, u32[]{:S(2)}, u32[]{:S(2)}) collective-permute-start(bf16[128,1024]{1,0:T(8,128)(2,1)} %copy-done.25), channel_id=1, source_target_pairs={{0,2},{1,3},{2,0},{3,1},{4,6},{5,7},{6,4},{7,5},{8,10},{9,11},{10,... | collective-permute-start | bytes 786440 | tf_op jit(solution)/shard_map/ppermute | solution.py:349
  48.3 5.2 %shard_map.67.toep = bf16[8192,128]{1,0:T(8,128)(2,1)} custom-call(f32[1,1024]{1,0:T(1,128)} %copy-done.16, f32[1,1024]{1,0:T(1,128)} %copy-done.18), custom_call_target="tpu_custom_call" | custom-call | tf_op jit(solution)/shard_map/pallas_call | solution.py:266
  56.1 2.5 %shard_map.68.q = f32[512,1024]{1,0:T(8,128)S(1)} custom-call(s32[1]{0:T(128)} %bitcast.info, bf16[3,128,4096]{2,1,0:T(8,128)(2,1)S(1)} %bitcast.18, bf16[128,1024]{1,0:T(8,128)(2,1)} %collective-permute-done.6.rest_0_, bf16[128,1024]{1,0:T(8,128)(2,1)} %collective-permute-done.7.rest_1_, bf16[128,1024]{1,0:T(8,128)(2,1)} %collective-permute-done.8.rest_2_, ...), custom_call_target="tpu_custom_call" | custom-call | tf_op jit(solution)/shard_map/pallas_call | solution.py:233
  58.6 2.0 %select_add_fusion.2 = (f32[16,1024]{1,0:T(8,128)S(1)}, f32[16,1024]{1,0:T(8,128)S(1)}) fusion(f32[24,1024]{1,0:T(8,128)S(1)} %copy-done.30, f32[16,1024]{1,0:T(8,128)S(1)} %get-tuple-element.36.wide_rates, pred[]{:T(512)S(6)} %eq.26, pred[]{:T(512)S(6)} %eq.24, f32[16,1024]{1,0:T(8,128)} %collective-permute-done.12, f32[]{:T(128)S(6)} %mul.83, pred[]{:T(512)S(6)} %ne.41, ...), kind=kLoop, calls=%fused_computation.35 | loop fusion | flops 344064 | bytes 458767 | tf_op jit(solution)/shard_map/add | solution.py:420
  60.6 1.4 %shard_map.72 = bf16[128,1024]{1,0:T(8,128)(2,1)S(1)} custom-call(s32[1]{0:T(128)} %bitcast.info, bf16[160,1024]{1,0:T(8,128)(2,1)S(1)} %get-tuple-element.38.inner.prod, bf16[160,1024]{1,0:T(8,128)(2,1)S(1)} %get-tuple-element.38.inner.prod, bf16[8192,128]{1,0:T(8,128)(2,1)S(1)} %copy-done.2, f32[512,1024]{1,0:T(8,128)S(1)} %shard_map.68.q, ...), custom_call_target="tpu_custom_call" | custom-call | tf_op jit(solution)/shard_map/pallas_call | solution.py:317
  62.0 1.5 %fusion.43 = bf16[128,2048]{1,0:T(8,128)(2,1)} fusion(bf16[128,1024]{1,0:T(8,128)(2,1)S(1)} %shard_map.72, bf16[1024,4096]{1,0:T(8,128)(2,1)S(1)} %copy-done.31), kind=kOutput, calls=%fused_computation.25 | convolution fusion | flops 537133056 | bytes 4980736 | tf_op jit(solution)/shard_map/dot_general | solution.py:26
  63.5 4.0 %collective-permute-done.5.inner.prod = bf16[160,1024]{1,0:T(8,128)(2,1)S(1)} collective-permute-done((bf16[160,1024]{1,0:T(8,128)(2,1)}, bf16[160,1024]{1,0:T(8,128)(2,1)S(1)}, u32[]{:S(2)}, u32[]{:S(2)}) %collective-permute-start.5) | collective-permute-done | bytes 327712 | tf_op jit(solution)/shard_map/ppermute | solution.py:349
  71.0 1.5 %fusion.37 = bf16[128,2048]{1,0:T(8,128)(2,1)} fusion(bf16[128,1024]{1,0:T(8,128)(2,1)S(1)} %shard_map.72, bf16[1024,4096]{1,0:T(8,128)(2,1)S(1)} %copy-done.31), kind=kOutput, calls=%fused_computation.23 | convolution fusion | flops 537133056 | bytes 4980736 | tf_op jit(solution)/shard_map/dot_general | solution.py:26
  73.0 2.1 %shard_map.69 = bf16[128,1024]{1,0:T(8,128)(2,1)S(1)} custom-call(s32[1]{0:T(128)} %bitcast.info, bf16[128,1024]{1,0:T(8,128)(2,1)} %collective-permute-done.4.prod, bf16[160,1024]{1,0:T(8,128)(2,1)S(1)} %collective-permute-done.5.inner.prod, bf16[8192,128]{1,0:T(8,128)(2,1)S(1)} %copy-done.2, f32[512,1024]{1,0:T(8,128)S(1)} %shard_map.68.q, ...), custom_call_target="tpu_custom_call" | custom-call | tf_op jit(solution)/shard_map/pallas_call | solution.py:317
  75.1 1.6 %fusion.31 = bf16[128,2048]{1,0:T(8,128)(2,1)} fusion(bf16[128,1024]{1,0:T(8,128)(2,1)S(1)} %shard_map.69, bf16[1024,4096]{1,0:T(8,128)(2,1)S(1)} %copy-done.31, bf16[128,2048]{1,0:T(8,128)(2,1)S(1)} %collective-permute-done.13), kind=kOutput, calls=%fused_computation.21 | convolution fusion | flops 537657344 | bytes 5505024 | tf_op jit(solution)/shard_map/dot_general | solution.py:26
  76.8 1.7 %collective-permute-start.14 = (bf16[128,2048]{1,0:T(8,128)(2,1)}, bf16[128,2048]{1,0:T(8,128)(2,1)}, u32[]{:S(2)}, u32[]{:S(2)}) collective-permute-start(bf16[128,2048]{1,0:T(8,128)(2,1)} %fusion.31), channel_id=1, source_target_pairs={{0,2},{1,3},{2,0},{3,1},{4,6},{5,7},{6,4},{7,5},{8,10},{9,11},{10,... | collective-permute-start | bytes 1572872 | tf_op jit(solution)/shard_map/ppermute | solution.py:349
  78.5 1.6 %fusion.28 = bf16[128,2048]{1,0:T(8,128)(2,1)} fusion(bf16[128,1024]{1,0:T(8,128)(2,1)S(1)} %shard_map.69, bf16[1024,4096]{1,0:T(8,128)(2,1)S(1)} %copy-done.31, bf16[128,2048]{1,0:T(8,128)(2,1)S(1)} %collective-permute-done.16), kind=kOutput, calls=%fused_computation.20 | convolution fusion | flops 537657344 | bytes 5505024 | tf_op jit(solution)/shard_map/dot_general | solution.py:26
  80.4 1.6 %copy-done.5 = f32[512,1024]{1,0:T(8,128)S(1)} copy-done((f32[512,1024]{1,0:T(8,128)S(1)}, f32[512,1024]{1,0:T(8,128)}, u32[]{:S(2)}) %copy-start.5) | copy-done | bytes 2097176
  83.4 3.2 %fusion.25 = f32[128,2048]{1,0:T(8,128)S(1)} fusion(bf16[128,1024]{1,0:T(8,128)(2,1)S(1)} %shard_map.71, bf16[1024,4096]{1,0:T(8,128)(2,1)} %param.11, bf16[128,2048]{1,0:T(8,128)(2,1)} %collective-permute-done.18), kind=kOutput, calls=%fused_computation.19 | convolution fusion | flops 537395200 | bytes 6029312 | tf_op jit(solution)/shard_map/dot_general | solution.py:26
  86.6 5.3 %collective-permute-done.14 = bf16[128,2048]{1,0:T(8,128)(2,1)} collective-permute-done((bf16[128,2048]{1,0:T(8,128)(2,1)}, bf16[128,2048]{1,0:T(8,128)(2,1)}, u32[]{:S(2)}, u32[]{:S(2)}) %collective-permute-start.14) | collective-permute-done | bytes 524320 | tf_op jit(solution)/shard_map/ppermute | solution.py:349
  91.9 10.3 %collective-permute-done.17 = bf16[128,2048]{1,0:T(8,128)(2,1)} collective-permute-done((bf16[128,2048]{1,0:T(8,128)(2,1)}, bf16[128,2048]{1,0:T(8,128)(2,1)}, u32[]{:S(2)}, u32[]{:S(2)}) %collective-permute-start.17) | collective-permute-done | bytes 524320 | tf_op jit(solution)/shard_map/ppermute | solution.py:349
  102.2 3.7 %add_convert_fusion.1 = (bf16[128,4096]{1,0:T(8,128)(2,1)S(1)}, bf16[128,4096]{1,0:T(8,128)(2,1)S(1)}) fusion(bf16[128,2048]{1,0:T(8,128)(2,1)} %collective-permute-done.14, bf16[128,4096]{1,0:T(8,128)(2,1)S(1)} %copy-done.32, f32[128,2048]{1,0:T(8,128)S(1)} %fusion.25, ...), kind=kOutput, output_to_operand_aliasing={{0}: (7, {}), {1}: (7, {})}, calls=%fused_computation.28 | convolution fusion | flops 540016640 | bytes 9175040 | tf_op jit(solution)/shard_map/dot_general | solution.py:26
  (100 shorter events, 22.9 us)
Async XLA Ops:
  7.7 7.5 %copy-start.16 = (f32[1,1024]{1,0:T(1,128)}, f32[1,1024]{1,0:T(1,128)S(1)}, u32[]{:S(2)}) copy-start(f32[1,1024]{1,0:T(1,128)S(1)} %get-tuple-element.30.rate_row) | copy-start | bytes 12292
  7.7 14.8 %copy-start.1 = (bf16[128,3,4096]{2,0,1:T(8,128)(2,1)S(1)}, bf16[128,3,4096]{2,0,1:T(8,128)(2,1)}, u32[]{:S(2)}) copy-start(bf16[128,3,4096]{2,0,1:T(8,128)(2,1)} %param.6) | copy-start | bytes 9437188
  7.7 7.5 %collective-permute-start = (bf16[2,128,2048]{2,1,0:T(8,128)(2,1)S(1)}, bf16[2,128,2048]{2,1,0:T(8,128)(2,1)S(1)}, u32[]{:S(2)}, u32[]{:S(2)}) collective-permute-start(bf16[2,128,2048]{2,1,0:T(8,128)(2,1)S(1)} %get-tuple-element.22), channel_id=1, source_target_pairs={{0,1},{1,0},{2,3},{3,2},{4,5},{5,4},{6,7},{7,6},{8,9},{9,8},{10,11... | collective-permute-start | bytes 3145736 | tf_op jit(solution)/shard_map/ppermute | solution.py:352
  8.2 7.1 %collective-permute-start.1 = (bf16[3,8,2048]{2,1,0:T(8,128)(2,1)S(1)}, bf16[3,8,2048]{2,1,0:T(8,128)(2,1)S(1)}, u32[]{:S(2)}, u32[]{:S(2)}) collective-permute-start(bf16[3,8,2048]{2,1,0:T(8,128)(2,1)S(1)} %get-tuple-element.23), channel_id=1, source_target_pairs={{1,2},{3,4},{5,6},{7,8},{9,10},{11,12},{13,14},{15,16},{17,18},{19... | collective-permute-start | bytes 294920 | tf_op jit(solution)/shard_map/ppermute | solution.py:370
  9.0 6.3 %collective-permute-start.2 = (bf16[3,8,2048]{2,1,0:T(8,128)(2,1)S(1)}, bf16[3,8,2048]{2,1,0:T(8,128)(2,1)S(1)}, u32[]{:S(2)}, u32[]{:S(2)}) collective-permute-start(bf16[3,8,2048]{2,1,0:T(8,128)(2,1)S(1)} %get-tuple-element.24), channel_id=1, source_target_pairs={{1,3},{3,5},{5,7},{7,9},{9,11},{11,13},{13,15},{15,17},{17,19},{19... | collective-permute-start | bytes 294920 | tf_op jit(solution)/shard_map/ppermute | solution.py:370
  9.6 5.6 %collective-permute-start.3 = (f32[2,8,1024]{2,1,0:T(8,128)S(1)}, f32[2,8,1024]{2,1,0:T(8,128)S(1)}, u32[]{:S(2)}, u32[]{:S(2)}) collective-permute-start(f32[2,8,1024]{2,1,0:T(8,128)S(1)} %get-tuple-element.25.taps), channel_id=1, source_target_pairs={{0,2},{1,3},{2,0},{3,1},{4,6},{5,7},{6,4},{7,5},{8,10},{9,11},{10,... | collective-permute-start | bytes 196616 | tf_op jit(solution)/shard_map/ppermute | solution.py:349
  15.2 5.0 %copy-start.8 = (bf16[3,8,2048]{2,1,0:T(8,128)(2,1)}, bf16[3,8,2048]{2,1,0:T(8,128)(2,1)S(1)}, u32[]{:S(2)}) copy-start(bf16[3,8,2048]{2,1,0:T(8,128)(2,1)S(1)} %collective-permute-done.1.edge0) | copy-start | bytes 294916
  15.3 5.0 %copy-start.10 = (bf16[3,8,2048]{2,1,0:T(8,128)(2,1)}, bf16[3,8,2048]{2,1,0:T(8,128)(2,1)S(1)}, u32[]{:S(2)}) copy-start(bf16[3,8,2048]{2,1,0:T(8,128)(2,1)S(1)} %collective-permute-done.2.edge1) | copy-start | bytes 294916
  20.2 9.1 %collective-permute-start.9 = (f32[24,1024]{1,0:T(8,128)}, f32[24,1024]{1,0:T(8,128)}, u32[]{:S(2)}, u32[]{:S(2)}) collective-permute-start(f32[24,1024]{1,0:T(8,128)} %get-tuple-element.35), channel_id=1, source_target_pairs={{0,2},{1,3},{2,0},{3,1},{4,6},{5,7},{6,4},{7,5},{8,10},{9,11},{10,... | collective-permute-start | bytes 294920 | tf_op jit(solution)/shard_map/ppermute | solution.py:349
  30.9 4.6 %collective-permute-start.10 = (f32[16,1024]{1,0:T(8,128)}, f32[16,1024]{1,0:T(8,128)}, u32[]{:S(2)}, u32[]{:S(2)}) collective-permute-start(f32[16,1024]{1,0:T(8,128)} %fusion.47), channel_id=1, source_target_pairs={{0,4},{4,0},{8,12},{12,8},{16,20},{20,16},{24,28},{28,24},{1,5},{5... | collective-permute-start | bytes 196616 | tf_op jit(solution)/shard_map/ppermute | solution.py:355
  37.0 5.5 %collective-permute-start.11 = (f32[16,1024]{1,0:T(8,128)}, f32[16,1024]{1,0:T(8,128)}, u32[]{:S(2)}, u32[]{:S(2)}) collective-permute-start(f32[16,1024]{1,0:T(8,128)} %add_select_fusion.1), channel_id=1, source_target_pairs={{0,8},{4,12},{8,0},{12,4},{16,24},{20,28},{24,16},{28,20},{1,9},{5... | collective-permute-start | bytes 196616 | tf_op jit(solution)/shard_map/ppermute | solution.py:355
  38.6 15.8 %collective-permute-start.6 = (bf16[128,1024]{1,0:T(8,128)(2,1)}, bf16[128,1024]{1,0:T(8,128)(2,1)}, u32[]{:S(2)}, u32[]{:S(2)}) collective-permute-start(bf16[128,1024]{1,0:T(8,128)(2,1)} %copy-done.28), channel_id=1, source_target_pairs={{0,1},{1,0},{2,3},{3,2},{4,5},{5,4},{6,7},{7,6},{8,9},{9,8},{10,11... | collective-permute-start | bytes 786440 | tf_op jit(solution)/shard_map/ppermute | solution.py:376
  40.1 14.8 %collective-permute-start.7 = (bf16[128,1024]{1,0:T(8,128)(2,1)}, bf16[128,1024]{1,0:T(8,128)(2,1)}, u32[]{:S(2)}, u32[]{:S(2)}) collective-permute-start(bf16[128,1024]{1,0:T(8,128)(2,1)} %copy-done.27), channel_id=1, source_target_pairs={{0,2},{1,3},{2,0},{3,1},{4,6},{5,7},{6,4},{7,5},{8,10},{9,11},{10,... | collective-permute-start | bytes 786440 | tf_op jit(solution)/shard_map/ppermute | solution.py:376
  42.6 12.6 %collective-permute-start.8 = (bf16[128,1024]{1,0:T(8,128)(2,1)}, bf16[128,1024]{1,0:T(8,128)(2,1)}, u32[]{:S(2)}, u32[]{:S(2)}) collective-permute-start(bf16[128,1024]{1,0:T(8,128)(2,1)} %copy-done.26), channel_id=1, source_target_pairs={{0,3},{1,2},{2,1},{3,0},{4,7},{5,6},{6,5},{7,4},{8,11},{9,10},{10,... | collective-permute-start | bytes 786440 | tf_op jit(solution)/shard_map/ppermute | solution.py:376
  44.1 14.5 %collective-permute-start.12 = (f32[16,1024]{1,0:T(8,128)}, f32[16,1024]{1,0:T(8,128)}, u32[]{:S(2)}, u32[]{:S(2)}) collective-permute-start(f32[16,1024]{1,0:T(8,128)} %add_select_fusion), channel_id=1, source_target_pairs={{0,16},{4,20},{8,24},{12,28},{16,0},{20,4},{24,8},{28,12},{1,17},{... | collective-permute-start | bytes 196616 | tf_op jit(solution)/shard_map/ppermute | solution.py:355
  46.7 26.3 %collective-permute-start.4 = (bf16[128,1024]{1,0:T(8,128)(2,1)}, bf16[128,1024]{1,0:T(8,128)(2,1)}, u32[]{:S(2)}, u32[]{:S(2)}) collective-permute-start(bf16[128,1024]{1,0:T(8,128)(2,1)} %copy-done.25), channel_id=1, source_target_pairs={{0,2},{1,3},{2,0},{3,1},{4,6},{5,7},{6,4},{7,5},{8,10},{9,11},{10,... | collective-permute-start | bytes 786440 | tf_op jit(solution)/shard_map/ppermute | solution.py:349
  48.3 12.3 %copy-start.17 = (f32[1,1024]{1,0:T(1,128)S(1)}, f32[1,1024]{1,0:T(1,128)}, u32[]{:S(2)}) copy-start(f32[1,1024]{1,0:T(1,128)} %copy-done.16) | copy-start | bytes 12292
  48.3 12.3 %copy-start.19 = (f32[1,1024]{1,0:T(1,128)S(1)}, f32[1,1024]{1,0:T(1,128)}, u32[]{:S(2)}) copy-start(f32[1,1024]{1,0:T(1,128)} %copy-done.18) | copy-start | bytes 12292
  53.5 7.1 %copy-start.2 = (bf16[8192,128]{1,0:T(8,128)(2,1)S(1)}, bf16[8192,128]{1,0:T(8,128)(2,1)}, u32[]{:S(2)}) copy-start(bf16[8192,128]{1,0:T(8,128)(2,1)} %shard_map.67.toep) | copy-start | bytes 6291460
  54.4 13.1 %collective-permute-start.5 = (bf16[160,1024]{1,0:T(8,128)(2,1)}, bf16[160,1024]{1,0:T(8,128)(2,1)S(1)}, u32[]{:S(2)}, u32[]{:S(2)}) collective-permute-start(bf16[160,1024]{1,0:T(8,128)(2,1)} %copy-done.24), channel_id=1, source_target_pairs={{0,2},{1,3},{2,0},{3,1},{4,6},{5,7},{6,4},{7,5},{8,10},{9,11},{10,... | collective-permute-start | bytes 983048 | tf_op jit(solution)/shard_map/ppermute | solution.py:349
  56.1 5.9 %copy-start.31 = (bf16[1024,4096]{1,0:T(8,128)(2,1)S(1)}, bf16[1024,4096]{1,0:T(8,128)(2,1)}, u32[]{:S(2)}) copy-start(bf16[1024,4096]{1,0:T(8,128)(2,1)} %param.11) | copy-start | bytes 25165828
  58.6 14.5 %copy-start.4 = (f32[512,1024]{1,0:T(8,128)}, f32[512,1024]{1,0:T(8,128)S(1)}, u32[]{:S(2)}) copy-start(f32[512,1024]{1,0:T(8,128)S(1)} %shard_map.68.q) | copy-start | bytes 6291460
  69.6 5.5 %collective-permute-start.13 = (bf16[128,2048]{1,0:T(8,128)(2,1)S(1)}, bf16[128,2048]{1,0:T(8,128)(2,1)S(1)}, u32[]{:S(2)}, u32[]{:S(2)}) collective-permute-start(bf16[128,2048]{1,0:T(8,128)(2,1)S(1)} %fusion.34), channel_id=1, source_target_pairs={{0,1},{1,0},{2,3},{3,2},{4,5},{5,4},{6,7},{7,6},{8,9},{9,8},{10,11... | collective-permute-start | bytes 1572872 | tf_op jit(solution)/shard_map/ppermute | solution.py:352
  70.4 8.1 %collective-permute-start.16 = (bf16[128,2048]{1,0:T(8,128)(2,1)S(1)}, bf16[128,2048]{1,0:T(8,128)(2,1)S(1)}, u32[]{:S(2)}, u32[]{:S(2)}) collective-permute-start(bf16[128,2048]{1,0:T(8,128)(2,1)S(1)} %fusion.40), channel_id=1, source_target_pairs={{0,1},{1,0},{2,3},{3,2},{4,5},{5,4},{6,7},{7,6},{8,9},{9,8},{10,11... | collective-permute-start | bytes 1572872 | tf_op jit(solution)/shard_map/ppermute | solution.py:352
  72.5 10.8 %collective-permute-start.18 = (bf16[128,2048]{1,0:T(8,128)(2,1)}, bf16[128,2048]{1,0:T(8,128)(2,1)}, u32[]{:S(2)}, u32[]{:S(2)}) collective-permute-start(bf16[128,2048]{1,0:T(8,128)(2,1)} %fusion.43), channel_id=1, source_target_pairs={{0,1},{1,0},{2,3},{3,2},{4,5},{5,4},{6,7},{7,6},{8,9},{9,8},{10,11... | collective-permute-start | bytes 1572872 | tf_op jit(solution)/shard_map/ppermute | solution.py:352
  72.5 14.0 %collective-permute-start.15 = (bf16[128,2048]{1,0:T(8,128)(2,1)}, bf16[128,2048]{1,0:T(8,128)(2,1)}, u32[]{:S(2)}, u32[]{:S(2)}) collective-permute-start(bf16[128,2048]{1,0:T(8,128)(2,1)} %fusion.37), channel_id=1, source_target_pairs={{0,1},{1,0},{2,3},{3,2},{4,5},{5,4},{6,7},{7,6},{8,9},{9,8},{10,11... | collective-permute-start | bytes 1572872 | tf_op jit(solution)/shard_map/ppermute | solution.py:352
  76.8 3.6 %copy-start.3 = (bf16[8192,128]{1,0:T(8,128)(2,1)S(1)}, bf16[8192,128]{1,0:T(8,128)(2,1)}, u32[]{:S(2)}) copy-start(bf16[8192,128]{1,0:T(8,128)(2,1)} %shard_map.67.toep) | copy-start | bytes 6291460
  76.8 3.6 %copy-start.15 = (bf16[128,1024]{1,0:T(8,128)(2,1)S(1)}, bf16[128,1024]{1,0:T(8,128)(2,1)}, u32[]{:S(2)}) copy-start(bf16[128,1024]{1,0:T(8,128)(2,1)} %copy-done.14) | copy-start | bytes 786436
  76.8 15.1 %collective-permute-start.14 = (bf16[128,2048]{1,0:T(8,128)(2,1)}, bf16[128,2048]{1,0:T(8,128)(2,1)}, u32[]{:S(2)}, u32[]{:S(2)}) collective-permute-start(bf16[128,2048]{1,0:T(8,128)(2,1)} %fusion.31), channel_id=1, source_target_pairs={{0,2},{1,3},{2,0},{3,1},{4,6},{5,7},{6,4},{7,5},{8,10},{9,11},{10,... | collective-permute-start | bytes 1572872 | tf_op jit(solution)/shard_map/ppermute | solution.py:349
  80.1 22.1 %collective-permute-start.17 = (bf16[128,2048]{1,0:T(8,128)(2,1)}, bf16[128,2048]{1,0:T(8,128)(2,1)}, u32[]{:S(2)}, u32[]{:S(2)}) collective-permute-start(bf16[128,2048]{1,0:T(8,128)(2,1)} %fusion.28), channel_id=1, source_target_pairs={{0,2},{1,3},{2,0},{3,1},{4,6},{5,7},{6,4},{7,5},{8,10},{9,11},{10,... | collective-permute-start | bytes 1572872 | tf_op jit(solution)/shard_map/ppermute | solution.py:349
  83.3 18.8 %copy-start.32 = (bf16[128,4096]{1,0:T(8,128)(2,1)S(1)}, bf16[128,4096]{1,0:T(8,128)(2,1)}, u32[]{:S(2)}) copy-start(bf16[128,4096]{1,0:T(8,128)(2,1)} %param.7) | copy-start | bytes 3145732
  83.3 18.8 %copy-start.33 = (bf16[128,4096]{1,0:T(8,128)(2,1)S(1)}, bf16[128,4096]{1,0:T(8,128)(2,1)}, u32[]{:S(2)}) copy-start(bf16[128,4096]{1,0:T(8,128)(2,1)} %custom-call) | copy-start | bytes 3145732
  (22 other events, 25.5 us)

commit v2 on v0

v2 whole, which is shorter than its diff:
```python
import functools

import jax
import jax.numpy as jnp
from jax import lax
from jax.experimental import pallas as pl
from jax.experimental.pallas import tpu as pltpu
from jax.sharding import PartitionSpec as P

ORDER = 16
GROUP_CH = 16
LANES = 128
TAPS = 7
EDGE = 8
F32 = jnp.float32
BF16 = jnp.bfloat16
PER_TILE = LANES // GROUP_CH
BRIEF = pl.CostEstimate(flops=1, bytes_accessed=1, transcendentals=0)


def halves(value):
    high = value.astype(BF16)
    return high, (value - high.astype(F32)).astype(BF16)


def dot(a, b):
    return jnp.dot(a, b, preferred_element_type=F32)


def iota(shape, dim):
    return lax.broadcasted_iota(jnp.int32, shape, dim)


def own_group():
    return iota((LANES, LANES), 0) // ORDER == iota((LANES, LANES), 1) // GROUP_CH


def target(position, e, chips):
    return 2 * ((position // 2 + e // 2) % chips) + (position % 2 + e % 2) % 2


def source(position, e, chips):
    return 2 * ((position // 2 + chips - e // 2) % chips) + (position % 2 + e % 2) % 2


def fold(product, mask):
    kept = jnp.where(mask, product, 0.0)
    return jnp.sum(kept.reshape(PER_TILE, ORDER, LANES), axis=0)


def convolve(padded, taps, start, count):
    total = taps[0:1] * padded[EDGE + start : EDGE + start + count]
    for j in range(1, TAPS):
        total = total + taps[j : j + 1] * padded[EDGE - j + start : EDGE - j + start + count]
    return total


def first_kernel(chips, info, feats, taps_in, rates_in, residues_in, kv_out, edge0, edge1, kv_taps, rate_row, coef_row, wide, *rest):
    steps = 2 * chips
    pieces, (last, taps, rates, residues, sems) = rest[: steps - 1], rest[steps - 1 :]
    rows, width = pieces[0].shape
    core = info[0] % 2
    copies = [(rates_in, rates), (residues_in, residues), (taps_in, taps), (feats.at[:, pl.ds(rows - 2 * EDGE, 2 * EDGE), :], last)]
    for j in range(chips):
        start = pl.multiple_of((2 * j + 1 - core) * width, LANES)
        for branch in range(2):
            copies.append((feats.at[branch + 1, :, pl.ds(start, width)], kv_out.at[branch, :, pl.ds(j * width, width)]))
    for e, piece in enumerate(pieces, 1):
        start = pl.multiple_of(target(info[0], e, chips) * width, LANES)
        copies.append((feats.at[0, :, pl.ds(start, width)], piece))
    copies = [pltpu.make_async_copy(*ends, sems.at[i]) for i, ends in enumerate(copies)]
    for copy in copies:
        copy.start()
    for copy in copies[:3]:
        copy.wait()

    rate, residue = rates[...], residues[...]
    coef = residue * jnp.sqrt(1.0 - jnp.exp(-2.0 * rate))
    lane_group = iota((ORDER, LANES), 1) // GROUP_CH
    diagonal = iota((ORDER, LANES), 1) % ORDER == iota((ORDER, LANES), 0)

    def spread(values, tile):
        out = jnp.broadcast_to(values[:, tile * PER_TILE : tile * PER_TILE + 1], (ORDER, LANES))
        for g in range(1, PER_TILE):
            at = tile * PER_TILE + g
            out = jnp.where(lane_group == g, jnp.broadcast_to(values[:, at : at + 1], (ORDER, LANES)), out)
        return out

    for b in range(2):
        kv_taps[b, 0:TAPS, :] = taps[b + 1]
    for tile in range(width // LANES):
        lanes = slice(tile * LANES, (tile + 1) * LANES)
        wide_rate = spread(rate, tile)
        wide[:, lanes] = wide_rate
        row = jnp.sum(jnp.where(diagonal, wide_rate, 0.0), axis=0, keepdims=True)
        rate_row[:, lanes] = row
        coef_row[:, lanes] = jnp.sum(jnp.where(diagonal, spread(coef, tile), 0.0), axis=0, keepdims=True)
        for b in range(2):
            kv_taps[b, TAPS : TAPS + 1, lanes] = row
    for copy in copies[3:]:
        copy.wait()
    for c, out in ((0, edge0), (1, edge1)):
        for j in range(chips):
            cols = slice((2 * j + c) * width, (2 * j + c + 1) * width)
            for branch in range(3):
                out[branch, :, j * width : (j + 1) * width] = last[branch, :, cols].astype(F32)[EDGE:].astype(BF16)


def first(info, feats, taps, rates, residues, chips):
    _, rows, depth = feats.shape
    width = taps.shape[2]
    others = 2 * chips - 1
    vmem = pl.BlockSpec(memory_space=pltpu.VMEM)
    return pl.pallas_call(
        functools.partial(first_kernel, chips),
        out_shape=[
            jax.ShapeDtypeStruct((2, rows, chips * width), BF16),
            jax.ShapeDtypeStruct((3, EDGE, chips * width), BF16),
            jax.ShapeDtypeStruct((3, EDGE, chips * width), BF16),
            jax.ShapeDtypeStruct((2, TAPS + 1, width), F32),
            jax.ShapeDtypeStruct((1, width), F32),
            jax.ShapeDtypeStruct((1, width), F32),
            jax.ShapeDtypeStruct((ORDER, width), F32),
        ]
        + [jax.ShapeDtypeStruct((rows, width), BF16)] * others,
        in_specs=[pl.BlockSpec(memory_space=pltpu.SMEM)] + [pl.BlockSpec(memory_space=pltpu.HBM)] * 4,
        out_specs=[vmem] * (7 + others),
        scratch_shapes=[
            pltpu.VMEM((3, 2 * EDGE, depth), BF16),
            pltpu.VMEM(taps.shape, F32),
            pltpu.VMEM(rates.shape, F32),
            pltpu.VMEM(residues.shape, F32),
            pltpu.SemaphoreType.DMA((4 + 2 * chips + others,)),
        ],
        compiler_params=pltpu.CompilerParams(vmem_limit_bytes=12 << 20),
        cost_estimate=BRIEF,
    )(info, feats, taps, rates, residues)


def front_kernel(info, k_own, v_own, kv_in, edge0, edge1, taps, prod, state, pad_k, pad_v):
    rows, width = k_own.shape[1:]
    core = info[0] % 2
    chip_rows = 2 * rows
    mine = pl.multiple_of(EDGE + core * rows, 8)
    other = pl.multiple_of(EDGE + (1 - core) * rows, 8)
    step = min(64, chip_rows)
    mask = own_group()
    age = (rows - 1 - iota((LANES, rows), 1)).astype(F32)
    for w in range(width // LANES):
        lanes = slice(w * LANES, (w + 1) * LANES)
        for b, own, pad in ((0, k_own, pad_k), (1, v_own, pad_v)):
            pad[w, 0:EDGE, :] = edge0[b + 1, :, lanes].astype(F32) + edge1[b + 1, :, lanes].astype(F32)
            pad[w, pl.ds(mine, rows), :] = own[0, :, lanes].astype(F32)
            pad[w, pl.ds(other, rows), :] = kv_in[b, :, lanes].astype(F32)
        tap_k, tap_v = taps[0, :, lanes], taps[1, :, lanes]
        for start in range(0, chip_rows, step):
            value = convolve(pad_k.at[w], tap_k, start, step) * convolve(pad_v.at[w], tap_v, start, step)
            prod[start : start + step, lanes] = value.astype(BF16)
        rate = jnp.broadcast_to(tap_k[TAPS : TAPS + 1], (LANES, LANES)).T
        high, low = halves(jnp.exp(-rate[:, :rows] * age))
        beside = jnp.concatenate([prod[0:rows, lanes], prod[rows:chip_rows, lanes]], axis=1)
        reached = dot(jnp.concatenate([high, low], axis=0), beside)
        reached = reached[:LANES] + reached[LANES:]
        inner_high, inner_low = halves(fold(reached[:, :LANES], mask))
        prod[chip_rows : chip_rows + ORDER, lanes] = inner_high
        prod[chip_rows + ORDER : chip_rows + 2 * ORDER, lanes] = inner_low
        state[0:ORDER, lanes] = fold(jnp.exp(-rate * float(rows)) * reached[:, :LANES] + reached[:, LANES:], mask)
        state[ORDER : ORDER + EDGE, lanes] = edge0[0, :, lanes].astype(F32) + edge1[0, :, lanes].astype(F32)


def front(info, d, chips, feats, kv_in, edge0, edge1, taps):
    rows = feats.shape[1]
    width = taps.shape[2]
    block = min(512, width)
    per = width // block
    stored = 2 * rows + 2 * ORDER

    def chip(info):
        return (info[0] // 2 + d) % chips

    def own(branch):
        return pl.BlockSpec((1, rows, block), lambda i, info: (branch, 0, (2 * chip(info) + info[0] % 2) * per + i))

    def of_chip(*shape):
        return pl.BlockSpec(shape + (block,), lambda i, info: (0,) * len(shape) + (chip(info) * per + i,))

    def spec(*shape):
        return pl.BlockSpec(shape + (block,), lambda i, info: (0,) * len(shape) + (i,))

    return pl.pallas_call(
        front_kernel,
        grid_spec=pltpu.PrefetchScalarGridSpec(
            num_scalar_prefetch=1,
            grid=(per,),
            in_specs=[own(1), own(2), of_chip(2, rows), of_chip(3, EDGE), of_chip(3, EDGE), spec(2, TAPS + 1)],
            out_specs=[spec(stored), spec(ORDER + EDGE)],
            scratch_shapes=[pltpu.VMEM((block // LANES, EDGE + 2 * rows, LANES), F32)] * 2,
        ),
        out_shape=[jax.ShapeDtypeStruct((stored, width), BF16), jax.ShapeDtypeStruct((ORDER + EDGE, width), F32)],
        compiler_params=pltpu.CompilerParams(vmem_limit_bytes=12 << 20),
        cost_estimate=BRIEF,
    )(info, feats, feats, kv_in, edge0, edge1, taps)


def toeplitz_kernel(chunk, rate_row, coef_row, *rest):
    out = rest[-1]
    lag = (LANES - 1 - iota((LANES, LANES), 1)).astype(F32)
    rate = jnp.broadcast_to(rate_row[...], (LANES, LANES)).T
    coef = jnp.broadcast_to(coef_row[...], (LANES, LANES)).T
    taps = jnp.sum((coef * jnp.exp(-rate * lag)).reshape(PER_TILE, ORDER, LANES), axis=1)
    valid = iota((LANES, LANES), 1) <= iota((LANES, LANES), 0)
    for g in range(PER_TILE):
        spread = jnp.broadcast_to(taps[g : g + 1], (8, LANES))
        top = pltpu.roll(spread, 1, 1, stride=1, stride_axis=0)
        block = jnp.concatenate([top] + [pltpu.roll(top, at, 1) for at in range(8, chunk, 8)], axis=0)
        block = jnp.where(valid[:chunk], block, 0.0)
        out[g * chunk : (g + 1) * chunk, :] = block[:, :chunk].astype(BF16)


def toeplitz(rate_row, coef_row, chunk, first_tile, tiles, made=None):
    made = [] if made is None else [made]
    return pl.pallas_call(
        functools.partial(toeplitz_kernel, chunk),
        grid=(tiles,),
        in_specs=[pl.BlockSpec((1, LANES), lambda i: (0, first_tile + i))] * 2 + [pl.BlockSpec(memory_space=pl.ANY)] * len(made),
        out_specs=pl.BlockSpec((PER_TILE * chunk, chunk), lambda i: (first_tile + i, 0)),
        out_shape=jax.ShapeDtypeStruct((rate_row.shape[1] // GROUP_CH * chunk, chunk), BF16),
        input_output_aliases={2: 0} if made else {},
        cost_estimate=BRIEF,
    )(rate_row, coef_row, *made)


def local_kernel(prod, toep, out):
    rows, width = out.shape[0] // 2, out.shape[1]
    lane_group = iota((rows, LANES), 1) // GROUP_CH
    for w in range(width // LANES):
        lanes = slice(w * LANES, (w + 1) * LANES)
        beside = jnp.concatenate([prod[:rows, lanes], prod[rows : 2 * rows, lanes]], axis=1)
        local = dot(toep[w * PER_TILE * rows : (w + 1) * PER_TILE * rows, :], beside)
        for i in range(2):
            cols = slice(i * LANES, (i + 1) * LANES)
            kept = local[:rows, cols]
            for g in range(1, PER_TILE):
                kept = jnp.where(lane_group == g, local[g * rows : (g + 1) * rows, cols], kept)
            out[i * rows : (i + 1) * rows, lanes] = kept


def local(prod, toep):
    rows, width = toep.shape[1], prod.shape[1]
    block = min(512, width)
    return pl.pallas_call(
        local_kernel,
        grid=(width // block,),
        in_specs=[
            pl.BlockSpec((prod.shape[0], block), lambda i: (0, i)),
            pl.BlockSpec((block // GROUP_CH * rows, rows), lambda i: (i, 0)),
        ],
        out_specs=pl.BlockSpec((2 * rows, block), lambda i: (0, i)),
        out_shape=jax.ShapeDtypeStruct((2 * rows, width), F32),
        compiler_params=pltpu.CompilerParams(vmem_limit_bytes=12 << 20),
        cost_estimate=BRIEF,
    )(prod, toep)


def weight_copies(weights, part, cols, held, sems):
    share = held.shape[2]
    return [
        pltpu.make_async_copy(weights.at[:, pl.ds(part * cols + j * share, share)], held.at[j], sems.at[j])
        for j in range(held.shape[0])
    ]


def multiply(gated, copies, held, theirs, mine):
    rows, share = theirs.shape[0], held.shape[2]
    for j, copy in enumerate(copies):
        copy.wait()
        product = dot(gated, held[j])
        theirs[:, j * share : (j + 1) * share] = product[:rows].astype(BF16)
        mine[:, j * share : (j + 1) * share] = product[rows:].astype(BF16)


def gate_kernel(d, chips, info, local, inner, q0, q1, *rest):
    steps = 2 * chips
    ends, states, rest = rest[:steps], rest[steps : steps + chips], rest[steps + chips :]
    taps, before, wide_rates, rate_row, coef_row, weights, out, theirs, mine, pad, gated, held, sems = rest
    rows, width = q0.shape[-2:]
    cols = theirs.shape[1]
    step = min(64, rows)
    mask = own_group()
    later = (iota((rows, LANES), 0) + 1).astype(F32)
    places = [source(info[0], 2 * d + 1, chips), source(info[0], 2 * d, chips)]
    turn = pl.program_id(0)
    copies = weight_copies(weights, 0, cols, held, sems)

    @pl.when(turn == 0)
    def _():
        for copy in copies:
            copy.start()

    for w in range(width // LANES):
        lanes = slice(w * LANES, (w + 1) * LANES)
        into_high, into_low = halves(coef_row[:, lanes] * jnp.exp(-rate_row[:, lanes] * later))
        by_chip = []
        for y in range(chips):
            value = states[0][:, lanes]
            for i in range(1, chips):
                value = jnp.where((info[0] // 2 + chips - i) % chips == y, states[i][:, lanes], value)
            by_chip.append(value)
        rate = wide_rates[:, lanes]
        fade = jnp.exp(-rate * float(2 * rows))
        state = before[:, lanes]
        for y in range(chips - 1):
            state = jnp.where(y < places[0] // 2, fade * state + by_chip[y][:ORDER], state)
        halfway = inner[0:ORDER, lanes].astype(F32) + inner[ORDER:, lanes].astype(F32)
        halfway = jnp.exp(-rate * float(rows)) * state + halfway
        entering = [jnp.where(place % 2 == 0, state, halfway) for place in places]
        entering = [jnp.where(mask, jnp.concatenate([value] * PER_TILE, axis=0), 0.0) for value in entering]
        state_high, state_low = halves(jnp.concatenate(entering, axis=1))
        carried = dot(into_high, state_high) + dot(into_high, state_low) + dot(into_low, state_high)
        tap = taps[0, :, lanes]
        for i, (q, place) in enumerate(zip((q0, q1), places)):
            tail = by_chip[0][ORDER:]
            for e, end in enumerate(ends):
                rows_before = (end[0, :, lanes] if e == 0 else end[:, lanes]).astype(F32)[EDGE:]
                tail = jnp.where(source(info[0], e, chips) == place - 1, rows_before, tail)
            pad[w, i, 0:EDGE, :] = tail
            pad[w, i, EDGE:, :] = (q[0, :, lanes] if d == 0 and i == 1 else q[:, lanes]).astype(F32)
            base = pl.multiple_of((place % 2) * rows, rows)
            for start in range(0, rows, step):
                long = local[pl.ds(base + start, step), lanes] + carried[start : start + step, i * LANES : (i + 1) * LANES]
                value = convolve(pad.at[w, i], tap, start, step) * long
                at = i * rows + start
                gated[turn, at : at + step, lanes] = value.astype(BF16)

    @pl.when(turn == pl.num_programs(0) - 1)
    def _():
        whole = jnp.concatenate([gated[i] for i in range(gated.shape[0])], axis=1)
        out[...] = whole
        multiply(whole, copies, held, theirs, mine)


def gate(info, d, chips, local, prod, feats, pieces, states, taps, before, wide_rates, rate_row, coef_row, weights, parts):
    rows = feats.shape[1]
    width = taps.shape[2]
    steps = 2 * chips
    cols = weights.shape[1] // parts
    block = min(512, width)
    per = width // block
    share = min(512, cols)

    def spec(*shape):
        return pl.BlockSpec(shape + (block,), lambda i, info: (0,) * len(shape) + (i,))

    def of_own(count):
        at = rows // count - 1
        return pl.BlockSpec((1, count, block), lambda i, info: (0, at, info[0] * per + i))

    def of_piece(count):
        at = rows // count - 1
        return pl.BlockSpec((count, block), lambda i, info: (at, i))

    def whole(*shape):
        return pl.BlockSpec(shape, lambda i, info: (0,) * len(shape))

    pair = [pieces[2 * d], pieces[2 * d - 1]] if d > 0 else [pieces[0], feats]
    return pl.pallas_call(
        functools.partial(gate_kernel, d, chips),
        grid_spec=pltpu.PrefetchScalarGridSpec(
            num_scalar_prefetch=1,
            grid=(per,),
            in_specs=[spec(2 * rows), pl.BlockSpec((2 * ORDER, block), lambda i, info: (rows // ORDER, i))]
            + [of_piece(rows), of_piece(rows) if d > 0 else of_own(rows), of_own(2 * EDGE)]
            + [of_piece(2 * EDGE)] * (steps - 1)
            + [spec(ORDER + EDGE)] * chips
            + [spec(3, TAPS), spec(ORDER), spec(ORDER), spec(1), spec(1)]
            + [pl.BlockSpec(memory_space=pltpu.HBM)],
            out_specs=[whole(2 * rows, width), whole(rows, cols), whole(rows, cols)],
            scratch_shapes=[
                pltpu.VMEM((block // LANES, 2, EDGE + rows, LANES), F32),
                pltpu.VMEM((per, 2 * rows, block), BF16),
                pltpu.VMEM((cols // share, width, share), BF16),
                pltpu.SemaphoreType.DMA((cols // share,)),
            ],
        ),
        out_shape=[
            jax.ShapeDtypeStruct((2 * rows, width), BF16),
            jax.ShapeDtypeStruct((rows, cols), BF16),
            jax.ShapeDtypeStruct((rows, cols), BF16),
        ],
        compiler_params=pltpu.CompilerParams(vmem_limit_bytes=20 << 20),
        cost_estimate=BRIEF,
    )(info, local, prod, *pair, feats, *pieces, *states, taps, before, wide_rates, rate_row, coef_row, weights)


def project_kernel(part, gated, weights, theirs, mine, held, sems):
    copies = weight_copies(weights, part, theirs.shape[1], held, sems)
    for copy in copies:
        copy.start()
    multiply(gated[...], copies, held, theirs, mine)


def project(gated, weights, part, parts):
    rows, width = gated.shape[0] // 2, gated.shape[1]
    cols = weights.shape[1] // parts
    share = min(512, cols)
    vmem = pl.BlockSpec(memory_space=pltpu.VMEM)
    return pl.pallas_call(
        functools.partial(project_kernel, part),
        in_specs=[vmem, pl.BlockSpec(memory_space=pltpu.HBM)],
        out_specs=[vmem] * 2,
        out_shape=[jax.ShapeDtypeStruct((rows, cols), BF16)] * 2,
        scratch_shapes=[pltpu.VMEM((cols // share, width, share), BF16), pltpu.SemaphoreType.DMA((cols // share,))],
        compiler_params=pltpu.CompilerParams(vmem_limit_bytes=20 << 20),
        cost_estimate=BRIEF,
    )(gated, weights)


def finish_kernel(part, count, base, *rest):
    terms, (out, ready, sems) = rest[:count], rest[-3:]
    rows, cols = base.shape
    step = min(32, rows)
    copies = []
    for i in range(rows // step):
        span = slice(i * step, (i + 1) * step)
        total = base[span, :]
        for term in terms:
            total = total + term[span, :].astype(F32)
        ready[span, :] = total.astype(BF16)
        here = ready.at[pl.ds(i * step, step), :]
        copies.append(pltpu.make_async_copy(here, out.at[pl.ds(i * step, step), pl.ds(part * cols, cols)], sems.at[i]))
        copies[-1].start()
    for copy in copies:
        copy.wait()


def finish(part, parts, base, terms, out):
    rows, cols = base.shape
    before = [] if out is None else [out]
    vmem = pl.BlockSpec(memory_space=pltpu.VMEM)
    hbm = pl.BlockSpec(memory_space=pltpu.HBM)
    return pl.pallas_call(
        functools.partial(finish_kernel, part, len(terms)),
        in_specs=[vmem] * (1 + len(terms)) + [hbm] * len(before),
        out_specs=hbm,
        out_shape=jax.ShapeDtypeStruct((rows, cols * parts), BF16),
        scratch_shapes=[pltpu.VMEM((rows, cols), BF16), pltpu.SemaphoreType.DMA((rows // min(32, rows),))],
        input_output_aliases={1 + len(terms): 0} if before else {},
        compiler_params=pltpu.CompilerParams(vmem_limit_bytes=12 << 20),
        cost_estimate=BRIEF,
    )(base, *terms, *before)


def body(chips, contexts, features, residual, short_weight, rates, residues, out_weight):
    rows, _, depth = features.shape
    width = short_weight.shape[2]
    steps = 2 * chips
    chip_rows = 2 * rows
    context_rows = steps * rows
    tp, ctx = lax.axis_index("tp"), lax.axis_index("ctx")
    chip = tp // 2
    info = tp.astype(jnp.int32).reshape(1)
    always = tp < steps

    def send(value, e):
        return lax.ppermute(value, "tp", [(i, target(i, e, chips)) for i in range(steps)])

    def send_back(value, e):
        return lax.ppermute(value, "tp", [(i, source(i, e, chips)) for i in range(steps)])

    def with_context(value, bit):
        return lax.ppermute(value, "ctx", [(i, i ^ bit) for i in range(contexts)])

    def in_hbm(value):
        return pltpu.with_memory_space_constraint(value, pltpu.HBM)

    feats = in_hbm(jnp.transpose(features, (1, 0, 2)))
    taps = in_hbm(jnp.transpose(short_weight, (1, 0, 2)))
    poles = [in_hbm(jnp.transpose(value)) for value in (rates, residues)]
    kv_out, edge0, edge1, kv_taps, rate_row, coef_row, wide_rates, *pieces = first(info, feats, taps, *poles, chips)
    tiles = width // LANES
    early = tiles // 2
    toep = toeplitz(rate_row, coef_row, rows, 0, early)

    kv_taps = [kv_taps] + [send_back(kv_taps, 2 * d) for d in range(1, chips)]

    order = [(x * chips + y) * 2 for x in range(contexts) for y in range(chips)]
    edges = [
        lax.ppermute(part, ("ctx", "tp"), [(here + 1, after + c) for here, after in zip(order[:-1], order[1:])])
        for c, part in ((0, edge0), (1, edge1))
    ]

    kv_in = send(kv_out, 1)
    pieces[:chips] = [send(piece, e) for e, piece in enumerate(pieces[:chips], 1)]
    kv_in, edges, pieces[:chips], toep = lax.optimization_barrier((kv_in, edges, pieces[:chips], toep))

    prods, states = [None] * chips, [None] * chips
    for d in list(range(1, chips)) + [0]:
        prods[d], states[d] = front(info, d, chips, feats, kv_in, *edges, kv_taps[d])
        if d > 0:
            states[d] = send(states[d], 2 * d)
    states, prods, pieces[chips:] = lax.optimization_barrier((states, prods, pieces[chips:]))
    prods[1:] = [send(prods[d], 2 * d) for d in range(1, chips)]
    pieces[chips:] = [send(piece, e) for e, piece in enumerate(pieces[chips:], chips + 1)]

    def relay(states, prod, toep):
        by_chip = [
            sum(jnp.where((chip - d) % chips == y, state[:ORDER], 0.0) for d, state in enumerate(states))
            for y in range(chips)
        ]
        bits = [1 << i for i in range(contexts.bit_length() - 1)]
        fade = jnp.exp(-wide_rates * float(chip_rows))
        pasts = [jnp.exp(-wide_rates * float(bit * context_rows)) for bit in bits]
        places = [
            jnp.where((ctx & bit) != 0, jnp.exp(-wide_rates * ((ctx & (bit - 1)).astype(F32) * context_rows)), 0.0)
            for bit in bits
        ]
        total = by_chip[0]
        for y in range(1, chips):
            total = fade * total + by_chip[y]
        total, pasts, places = lax.optimization_barrier((total, pasts, places))
        before = jnp.zeros_like(total)
        for i, bit in enumerate(bits):
            got = with_context(total, bit)
            before = before + places[i] * got
            total = jnp.where((ctx & bit) != 0, pasts[i] * got + total, pasts[i] * total + got)
            if i == 0:
                toep = toeplitz(rate_row, coef_row, rows, early, tiles - early, toep)
                total, toep = lax.optimization_barrier((total, toep))
            if i == 1:
                near = local(prod, toep)
                total, near = lax.optimization_barrier((total, near))
        return before, near, toep

    def no_relay(states, prod, toep):
        return wide_rates, jnp.zeros((chip_rows, width), F32), toep

    before, near, toep = lax.cond(always, relay, no_relay, states, prods[0], toep)

    parts = 2
    cols = depth // parts
    weights = in_hbm(out_weight)

    def projected(d):
        inside = local(prods[d], toep) if d > 0 else near
        gated, theirs, mine = gate(
            info, d, chips, inside, prods[d], feats, pieces, states, taps, before, wide_rates, rate_row, coef_row,
            weights, parts,
        )
        sums = []
        for p in range(parts):
            if p > 0:
                theirs, mine = project(gated, weights, p, parts)
            sums.append(mine.astype(F32) + send(theirs, 1).astype(F32))
        return sums

    arriving = [[] for _ in range(parts)]
    for d in range(1, chips):
        for p, value in enumerate(projected(d)):
            arriving[p].append(send_back(value.astype(BF16), 2 * d))

    def own():
        return [
            value + residual[:, p * cols : (p + 1) * cols].astype(F32) for p, value in enumerate(projected(0))
        ]

    bases = lax.cond(always, own, lambda: [jnp.zeros((rows, cols), F32)] * parts)
    out = None
    for p in range(parts):
        out = finish(p, parts, bases[p], arriving[p], out)
    return out


def solution(mesh):
    chips, contexts = mesh.shape["tp"] // 2, mesh.shape["ctx"]
    in_specs = (
        P(("ctx", "tp"), None, None),
        P(("ctx", "tp"), None),
        P(None, None, "tp"),
        P("tp", None),
        P("tp", None),
        P("tp", None),
    )
    return jax.shard_map(
        functools.partial(body, chips, contexts),
        mesh=mesh,
        in_specs=in_specs,
        out_specs=P(("ctx", "tp"), None),
        check_vma=False,
    )
```

time: 314 us -> 81.9 us (0.26)
  matrix products: 141 us -> 0 us
  waiting for transfers between devices: 64 us -> 18.6 us
  Pallas kernels: 0 us -> 36.3 us
  local copies, waits for them, and re-layouts: 25.8 us -> 0.03 us
  starting transfers between devices: 44.8 us -> 23.9 us
  other arithmetic: 22.8 us -> 2.49 us
  between operations: 13.6 us -> 0.2 us
    dot_general x5 -> x0, matrix products: 141 us -> none  [the longest x1 65.3 us: local_terms(): local = jnp.einsum('gts,sgc->gtc', matrix, product, precision=precise_mode)]
    reduce_scatter x1 -> x0, waiting for transfers between devices: 48.8 us -> none  [body(): lax.psum_scatter(jnp.dot(gated, out_weight, preferred_element_type=jnp.fl...]
    pallas_call x0 -> x13, Pallas kernels: none -> 36.3 us  [the longest x2 8.89 us: gate(): pl.pallas_call(functools.partial(gate_kernel, d, chips), grid_spec=pltpu....]
    ppermute x8 -> x18, starting transfers between devices: 39.8 us -> 23.9 us  [the longest x3 9.42 us: send_back(): lax.ppermute(value, 'tp', [(i, source(i, e, chips)) for i in range(steps)])]
    add x9 -> x2, other arithmetic: 14.1 us -> 0.53 us  [the longest x1 0.51 us: own(): value + residual[:, p * cols:(p + 1) * cols].astype(F32)]
    all_to_all x2 -> x0, local copies, waits for them, and re-layouts: 12.5 us -> none  [body(): lax.all_to_all(features, 'tp', split_axis=2, concat_axis=0, tiled=True)]
    unnamed x17 -> x12, local copies, waits for them, and re-layouts: 7.52 us -> 0.03 us
    convert_element_type x4 -> x2, other arithmetic: 8.09 us -> 1.85 us  [body(): arriving[p].append(send_back(value.astype(BF16), 2 * d))]
  transfers between devices with their start and end apart: 10 -> 18, of which waited for: 9 -> 8; matrix products, arithmetic and copies ran while one was open for 19% -> 3% of each run, Pallas kernels for 0% -> 32%
where the time goes in v2:
time: 81.9 us; the launch traced here: 81.6 us
  Pallas kernels  36.3 us (44%)
  starting transfers between devices  23.9 us (29%)
  waiting for transfers between devices  18.6 us (23%)
  other arithmetic  2.49 us (3%)
    ppermute x3, waiting for transfers between devices, send_back(): lax.ppermute(value, 'tp', [(i, source(i, e, chips)) for i in range(steps)])  10.9 us
    ppermute x3, starting transfers between devices, send_back(): lax.ppermute(value, 'tp', [(i, source(i, e, chips)) for i in range(steps)])  9.42 us
    pallas_call x2, Pallas kernels, gate(): pl.pallas_call(functools.partial(gate_kernel, d, chips), grid_spec=pltpu....  8.89 us
    pallas_call x2, Pallas kernels, front(): pl.pallas_call(front_kernel, grid_spec=pltpu.PrefetchScalarGridSpec(num_s...  7.57 us
    ppermute x10, starting transfers between devices, send(): lax.ppermute(value, 'tp', [(i, target(i, e, chips)) for i in range(steps)])  7.2 us
    pallas_call x2, Pallas kernels, project(): pl.pallas_call(functools.partial(project_kernel, part), in_specs=[vmem, p...  6.04 us
    ppermute x3, starting transfers between devices, with_context(): return lax.ppermute(value, 'ctx', [(i, i ^ bit) for i in range(contexts)])  5.98 us
    pallas_call x2, Pallas kernels, local(): pl.pallas_call(local_kernel, grid=(width // block,), in_specs=[pl.BlockSp...  5.79 us
  transfers between devices with their start and end apart: 18, of which 8 were waited for; matrix products, arithmetic and copies ran while one was open for 3% of the time, Pallas kernels for 32%

profile of v2, /device:TPU:0, one launch (start us, length us, event | category | flops | bytes accessed | tf_op | source)
XLA Modules:
  0.0 81.6 jit_solution(5430166889743789219)
XLA Ops:
  0.0 1.7 %shard_map.65 = (bf16[2,128,2048]{2,1,0:T(8,128)(2,1)S(1)}, bf16[3,8,2048]{2,1,0:T(8,128)(2,1)S(1)}, bf16[3,8,2048]{2,1,0:T(8,128)(2,1)S(1)}, f32[2,8,1024]{2,1,...) custom-call(s32[1]{0:T(128)} %bitcast.info, ...), custom_call_target="tpu_custom_call" | custom-call | flops 1 | bytes 1 | tf_op jit(solution)/shard_map/pallas_call | solution.py:114
  2.3 2.9 %collective-permute-start.9 = (bf16[128,1024]{1,0:T(8,128)(2,1)S(1)}, bf16[128,1024]{1,0:T(8,128)(2,1)}, u32[]{:S(2)}, u32[]{:S(2)}) collective-permute-start(bf16[128,1024]{1,0:T(8,128)(2,1)S(1)} %get-tuple-element.171), channel_id=1, source_target_pairs={{0,2},{1,3},{2,0},{3,1},{4,6},{5,7},{6,4},{7,5},{8,10},{9,11},{10,... | collective-permute-start | bytes 786440 | tf_op jit(solution)/shard_map/ppermute | solution.py:465
  5.3 0.7 collective-permute-start.6
  6.0 0.7 collective-permute-start.7
  6.6 8.0 %collective-permute-start.10 = (f32[2,8,1024]{2,1,0:T(8,128)S(1)}, f32[2,8,1024]{2,1,0:T(8,128)S(1)}, u32[]{:S(2)}, u32[]{:S(2)}) collective-permute-start(f32[2,8,1024]{2,1,0:T(8,128)S(1)} %get-tuple-element.178.taps), channel_id=1, source_target_pairs={{0,2},{1,3},{2,0},{3,1},{4,6},{5,7},{6,4},{7,5},{8,10},{9,11},{10,... | collective-permute-start | bytes 196616 | tf_op jit(solution)/shard_map/ppermute | solution.py:468
  14.6 2.3 %shard_map.66 = bf16[8192,128]{1,0:T(8,128)(2,1)} custom-call(f32[1,1024]{1,0:T(1,128)S(1)} %get-tuple-element.172.rate_row.rest_9_, f32[1,1024]{1,0:T(1,128)S(1)} %get-tuple-element.173.coef_row.rest_10_), custom_call_target="tpu_custom_call" | custom-call | flops 1 | bytes 1 | tf_op jit(solution)/shard_map/pallas_call | solution.py:222
  17.0 3.5 %shard_map.68 = (bf16[288,1024]{1,0:T(8,128)(2,1)S(1)}, f32[24,1024]{1,0:T(8,128)S(1)}) custom-call(s32[1]{0:T(128)} %bitcast.info, bf16[3,128,4096]{2,1,0:T(8,128)(2,1)} %bitcast.6, bf16[3,128,4096]{2,1,0:T(8,128)(2,1)} %bitcast.7, bf16[2,128,2048]{2,1,0:T(8,128)(2,1)S(1)} %collective-permute-done.5.kv_in, ...), custom_call_target="tpu_custom_call" | custom-call | flops 1 | bytes 1 | tf_op jit(solution)/shard_map/pallas_call | solution.py:190
  20.4 1.9 %collective-permute-start.11 = (f32[24,1024]{1,0:T(8,128)S(1)}, f32[24,1024]{1,0:T(8,128)S(1)}, u32[]{:S(2)}, u32[]{:S(2)}) collective-permute-start(f32[24,1024]{1,0:T(8,128)S(1)} %get-tuple-element.180), channel_id=1, source_target_pairs={{0,2},{1,3},{2,0},{3,1},{4,6},{5,7},{6,4},{7,5},{8,10},{9,11},{10,... | collective-permute-start | bytes 294920 | tf_op jit(solution)/shard_map/ppermute | solution.py:465
  22.4 4.1 %shard_map.67 = (bf16[288,1024]{1,0:T(8,128)(2,1)}, f32[24,1024]{1,0:T(8,128)S(1)}) custom-call(s32[1]{0:T(128)} %bitcast.info, bf16[3,128,4096]{2,1,0:T(8,128)(2,1)} %bitcast.8, bf16[3,128,4096]{2,1,0:T(8,128)(2,1)} %bitcast.9, bf16[2,128,2048]{2,1,0:T(8,128)(2,1)S(1)} %collective-permute-done.5.kv_in, ...), custom_call_target="tpu_custom_call" | custom-call | flops 1 | bytes 1 | tf_op jit(solution)/shard_map/pallas_call | solution.py:190
  27.0 16.1 %conditional.2 = (f32[16,1024]{1,0:T(8,128)S(1)}, f32[256,1024]{1,0:T(8,128)S(1)}, bf16[8192,128]{1,0:T(8,128)(2,1)}) conditional(s32[]{:T(128)} %convert_element_type.46, (f32[16,1024]{1,0:T(8,128)S(1)}, bf16[8192,128]{1,0:T(8,128)(2,1)}) %tuple.39, (f32[16,1024]{1,0:T(8,128)S(1)}, s32[]{:T(128)}, s32[]{:T(128)}, f32[24,1024]{1,0:T(8,128)S(1)}, ...), branch_computations={%region_0.1_spmd, %region_1.2_spmd} | conditional | flops 540727 | bytes 4719314 | solution.py:537
  27.1 1.6 %collective-permute-start = (f32[16,1024]{1,0:T(8,128)S(1)}, f32[16,1024]{1,0:T(8,128)S(1)}, u32[]{:S(2)}, u32[]{:S(2)}) collective-permute-start(f32[16,1024]{1,0:T(8,128)S(1)} %get-tuple-element.97), channel_id=1, source_target_pairs={{0,4},{4,0},{8,12},{12,8},{16,20},{20,16},{24,28},{28,24},{1,5},{5... | collective-permute-start | bytes 196616 | tf_op jit(solution)/shard_map/cond/branch_1_fun/ppermute | solution.py:471
  28.6 2.3 %branch_1_fun.4.toep = bf16[8192,128]{1,0:T(8,128)(2,1)} custom-call(f32[1,1024]{1,0:T(1,128)S(1)} %get-tuple-element.100.rate_row, f32[1,1024]{1,0:T(1,128)S(1)} %get-tuple-element.101.coef_row, bf16[8192,128]{1,0:T(8,128)(2,1)} %get-tuple-element.102.rest_0_), custom_call_target="tpu_custom_call", output_to_operand_aliasing={{}: (2, {})} | custom-call | flops 1 | bytes 1 | tf_op jit(solution)/shard_map/cond/branch_1_fun/pallas_call | solution.py:222
  31.4 1.8 %collective-permute-start.1 = (f32[16,1024]{1,0:T(8,128)S(1)}, f32[16,1024]{1,0:T(8,128)S(1)}, u32[]{:S(2)}, u32[]{:S(2)}) collective-permute-start(f32[16,1024]{1,0:T(8,128)S(1)} %add_select_fusion.1), channel_id=1, source_target_pairs={{0,8},{4,12},{8,0},{12,4},{16,24},{20,28},{24,16},{28,20},{1,9},{5... | collective-permute-start | bytes 196616 | tf_op jit(solution)/shard_map/cond/branch_1_fun/ppermute | solution.py:471
  33.2 2.7 %branch_1_fun.5 = f32[256,1024]{1,0:T(8,128)S(1)} custom-call(bf16[288,1024]{1,0:T(8,128)(2,1)S(1)} %copy-done.3, bf16[8192,128]{1,0:T(8,128)(2,1)} %branch_1_fun.4.toep), custom_call_target="tpu_custom_call" | custom-call | flops 1 | bytes 1 | tf_op jit(solution)/shard_map/cond/branch_1_fun/pallas_call | solution.py:251
  36.5 2.7 %collective-permute-start.2 = (f32[16,1024]{1,0:T(8,128)S(1)}, f32[16,1024]{1,0:T(8,128)S(1)}, u32[]{:S(2)}, u32[]{:S(2)}) collective-permute-start(f32[16,1024]{1,0:T(8,128)S(1)} %add_select_fusion), channel_id=1, source_target_pairs={{0,16},{4,20},{8,24},{12,28},{16,0},{20,4},{24,8},{28,12},{1,17},{... | collective-permute-start | bytes 196616 | tf_op jit(solution)/shard_map/cond/branch_1_fun/ppermute | solution.py:471
  39.1 4.0 %collective-permute-done.2 = f32[16,1024]{1,0:T(8,128)S(1)} collective-permute-done((f32[16,1024]{1,0:T(8,128)S(1)}, f32[16,1024]{1,0:T(8,128)S(1)}, u32[]{:S(2)}, u32[]{:S(2)}) %collective-permute-start.2) | collective-permute-done | bytes 65568 | tf_op jit(solution)/shard_map/cond/branch_1_fun/ppermute | solution.py:471
  43.1 3.1 %shard_map.69.local = f32[256,1024]{1,0:T(8,128)S(1)} custom-call(bf16[288,1024]{1,0:T(8,128)(2,1)S(1)} %collective-permute-done.13.prod.inner, bf16[8192,128]{1,0:T(8,128)(2,1)} %get-tuple-element.194.toep), custom_call_target="tpu_custom_call" | custom-call | flops 1 | bytes 1 | tf_op jit(solution)/shard_map/pallas_call | solution.py:251
  46.3 4.5 %shard_map.70 = (bf16[256,1024]{1,0:T(8,128)(2,1)S(1)}, bf16[128,2048]{1,0:T(8,128)(2,1)S(1)}, bf16[128,2048]{1,0:T(8,128)(2,1)S(1)}) custom-call(s32[1]{0:T(128)} %bitcast.info, f32[256,1024]{1,0:T(8,128)S(1)} %shard_map.69.local, bf16[288,1024]{1,0:T(8,128)(2,1)S(1)} %collective-permute-done.13.prod.inner, ...), custom_call_target="tpu_custom_call" | custom-call | flops 1 | bytes 1 | tf_op jit(solution)/shard_map/pallas_call | solution.py:366
  50.9 3.0 %shard_map.71 = (bf16[128,2048]{1,0:T(8,128)(2,1)S(1)}, bf16[128,2048]{1,0:T(8,128)(2,1)S(1)}) custom-call(bf16[256,1024]{1,0:T(8,128)(2,1)S(1)} %get-tuple-element.195.gated, bf16[1024,4096]{1,0:T(8,128)(2,1)} %weights.1), custom_call_target="tpu_custom_call" | custom-call | flops 1 | bytes 1 | tf_op jit(solution)/shard_map/pallas_call | solution.py:407
  54.5 0.9 %add_convert_fusion = bf16[128,2048]{1,0:T(8,128)(2,1)} fusion(bf16[128,2048]{1,0:T(8,128)(2,1)S(1)} %collective-permute-done.16, bf16[128,2048]{1,0:T(8,128)(2,1)S(1)} %get-tuple-element.199), kind=kLoop, calls=%fused_computation.11 | loop fusion | flops 1048576 | bytes 1572864 | tf_op jit(solution)/shard_map/convert_element_type | solution.py:559
  55.5 0.6 collective-permute-done.14
  56.1 0.9 %add_convert_fusion.1 = bf16[128,2048]{1,0:T(8,128)(2,1)} fusion(bf16[128,2048]{1,0:T(8,128)(2,1)S(1)} %collective-permute-done.14, bf16[128,2048]{1,0:T(8,128)(2,1)S(1)} %get-tuple-element.196), kind=kLoop, calls=%fused_computation.12 | loop fusion | flops 1048576 | bytes 1572864 | tf_op jit(solution)/shard_map/convert_element_type | solution.py:559
  57.0 1.4 %collective-permute-start.15 = (bf16[128,2048]{1,0:T(8,128)(2,1)}, bf16[128,2048]{1,0:T(8,128)(2,1)S(1)}, u32[]{:S(2)}, u32[]{:S(2)}) collective-permute-start(bf16[128,2048]{1,0:T(8,128)(2,1)} %add_convert_fusion.1), channel_id=1, source_target_pairs={{0,2},{1,3},{2,0},{3,1},{4,6},{5,7},{6,4},{7,5},{8,10},{9,11},{10,... | collective-permute-start | bytes 1572872 | tf_op jit(solution)/shard_map/ppermute | solution.py:468
  58.4 10.6 %conditional.3 = (f32[128,2048]{1,0:T(8,128)S(1)}, f32[128,2048]{1,0:T(8,128)S(1)}) conditional(s32[]{:T(128)} %convert_element_type.46, () %tuple.37, (s32[1]{0:T(128)}, f32[256,1024]{1,0:T(8,128)S(1)}, bf16[288,1024]{1,0:T(8,128)(2,1)S(1)}, bf16[128,1024]{1,0:T(8,128)(2,1)}, bf16[3,128,4096]{2,1,0:T(8,128)(2,1)}, ...), branch_computations={%region_2.3_spmd, %region_3.4_spmd} | conditional | flops 2621442 | bytes 9437282 | solution.py:566
  58.4 4.3 %branch_1_fun.6 = (bf16[256,1024]{1,0:T(8,128)(2,1)S(1)}, bf16[128,2048]{1,0:T(8,128)(2,1)S(1)}, bf16[128,2048]{1,0:T(8,128)(2,1)S(1)}) custom-call(s32[1]{0:T(128)} %get-tuple-element.110.info, f32[256,1024]{1,0:T(8,128)S(1)} %get-tuple-element.111.local, bf16[288,1024]{1,0:T(8,128)(2,1)S(1)} %get-tuple-element.112.inner, ...), custom_call_target="tpu_custom_call" | custom-call | flops 1 | bytes 1 | tf_op jit(solution)/shard_map/cond/branch_1_fun/pallas_call | solution.py:366
  62.8 3.0 %branch_1_fun.7 = (bf16[128,2048]{1,0:T(8,128)(2,1)S(1)}, bf16[128,2048]{1,0:T(8,128)(2,1)S(1)}) custom-call(bf16[256,1024]{1,0:T(8,128)(2,1)S(1)} %get-tuple-element.128.gated, bf16[1024,4096]{1,0:T(8,128)(2,1)} %get-tuple-element.124.rest_11_.weights), custom_call_target="tpu_custom_call" | custom-call | flops 1 | bytes 1 | tf_op jit(solution)/shard_map/cond/branch_1_fun/pallas_call | solution.py:407
  66.4 1.4 %collective-permute-done.4 = bf16[128,2048]{1,0:T(8,128)(2,1)S(1)} collective-permute-done((bf16[128,2048]{1,0:T(8,128)(2,1)S(1)}, bf16[128,2048]{1,0:T(8,128)(2,1)S(1)}, u32[]{:S(2)}, u32[]{:S(2)}) %collective-permute-start.4) | collective-permute-done | bytes 524320 | tf_op jit(solution)/shard_map/cond/branch_1_fun/ppermute | solution.py:465
  67.8 0.7 collective-permute-done.3
  69.0 1.4 %collective-permute-done.17.rest_0_ = bf16[128,2048]{1,0:T(8,128)(2,1)S(1)} collective-permute-done((bf16[128,2048]{1,0:T(8,128)(2,1)}, bf16[128,2048]{1,0:T(8,128)(2,1)S(1)}, u32[]{:S(2)}, u32[]{:S(2)}) %collective-permute-start.17) | collective-permute-done | bytes 524320 | tf_op jit(solution)/shard_map/ppermute | solution.py:468
  70.4 0.8 %shard_map.72.rest_1_ = bf16[128,4096]{1,0:T(8,128)(2,1)} custom-call(f32[128,2048]{1,0:T(8,128)S(1)} %get-tuple-element.198.base, bf16[128,2048]{1,0:T(8,128)(2,1)S(1)} %collective-permute-done.17.rest_0_), custom_call_target="tpu_custom_call" | custom-call | flops 1 | bytes 1 | tf_op jit(solution)/shard_map/pallas_call | solution.py:441
  71.3 9.5 %collective-permute-done.15.rest_0_ = bf16[128,2048]{1,0:T(8,128)(2,1)S(1)} collective-permute-done((bf16[128,2048]{1,0:T(8,128)(2,1)}, bf16[128,2048]{1,0:T(8,128)(2,1)S(1)}, u32[]{:S(2)}, u32[]{:S(2)}) %collective-permute-start.15) | collective-permute-done | bytes 524320 | tf_op jit(solution)/shard_map/ppermute | solution.py:468
  80.7 0.8 %shard_map.73 = bf16[128,4096]{1,0:T(8,128)(2,1)} custom-call(f32[128,2048]{1,0:T(8,128)S(1)} %get-tuple-element.192.base, bf16[128,2048]{1,0:T(8,128)(2,1)S(1)} %collective-permute-done.15.rest_0_, bf16[128,4096]{1,0:T(8,128)(2,1)} %shard_map.72.rest_1_), custom_call_target="tpu_custom_call", output_to_operand_aliasing={{}: (2, {})} | custom-call | flops 1 | bytes 1 | tf_op jit(solution)/shard_map/pallas_call | solution.py:441
  (40 shorter events, 4.0 us)
Async XLA Ops:
  1.7 15.2 %collective-permute-start.5 = (bf16[2,128,2048]{2,1,0:T(8,128)(2,1)S(1)}, bf16[2,128,2048]{2,1,0:T(8,128)(2,1)S(1)}, u32[]{:S(2)}, u32[]{:S(2)}) collective-permute-start(bf16[2,128,2048]{2,1,0:T(8,128)(2,1)S(1)} %get-tuple-element.167), channel_id=1, source_target_pairs={{0,1},{1,0},{2,3},{3,2},{4,5},{5,4},{6,7},{7,6},{8,9},{9,8},{10,11... | collective-permute-start | bytes 3145736 | tf_op jit(solution)/shard_map/ppermute | solution.py:465
  2.3 14.7 %collective-permute-start.8 = (bf16[128,1024]{1,0:T(8,128)(2,1)S(1)}, bf16[128,1024]{1,0:T(8,128)(2,1)}, u32[]{:S(2)}, u32[]{:S(2)}) collective-permute-start(bf16[128,1024]{1,0:T(8,128)(2,1)S(1)} %get-tuple-element.170), channel_id=1, source_target_pairs={{0,1},{1,0},{2,3},{3,2},{4,5},{5,4},{6,7},{7,6},{8,9},{9,8},{10,11... | collective-permute-start | bytes 786440 | tf_op jit(solution)/shard_map/ppermute | solution.py:465
  2.3 14.6 %collective-permute-start.9 = (bf16[128,1024]{1,0:T(8,128)(2,1)S(1)}, bf16[128,1024]{1,0:T(8,128)(2,1)}, u32[]{:S(2)}, u32[]{:S(2)}) collective-permute-start(bf16[128,1024]{1,0:T(8,128)(2,1)S(1)} %get-tuple-element.171), channel_id=1, source_target_pairs={{0,2},{1,3},{2,0},{3,1},{4,6},{5,7},{6,4},{7,5},{8,10},{9,11},{10,... | collective-permute-start | bytes 786440 | tf_op jit(solution)/shard_map/ppermute | solution.py:465
  5.3 1.3 %collective-permute-start.6 = (bf16[3,8,2048]{2,1,0:T(8,128)(2,1)S(1)}, bf16[3,8,2048]{2,1,0:T(8,128)(2,1)S(1)}, u32[]{:S(2)}, u32[]{:S(2)}) collective-permute-start(bf16[3,8,2048]{2,1,0:T(8,128)(2,1)S(1)} %get-tuple-element.168), channel_id=1, source_target_pairs={{1,2},{3,4},{5,6},{7,8},{9,10},{11,12},{13,14},{15,16},{17,18},{19... | collective-permute-start | bytes 294920 | tf_op jit(solution)/shard_map/ppermute | solution.py:488
  6.0 11.0 %collective-permute-start.7 = (bf16[3,8,2048]{2,1,0:T(8,128)(2,1)S(1)}, bf16[3,8,2048]{2,1,0:T(8,128)(2,1)S(1)}, u32[]{:S(2)}, u32[]{:S(2)}) collective-permute-start(bf16[3,8,2048]{2,1,0:T(8,128)(2,1)S(1)} %get-tuple-element.169), channel_id=1, source_target_pairs={{1,3},{3,5},{5,7},{7,9},{9,11},{11,13},{13,15},{15,17},{17,19},{19... | collective-permute-start | bytes 294920 | tf_op jit(solution)/shard_map/ppermute | solution.py:488
  6.6 10.3 %collective-permute-start.10 = (f32[2,8,1024]{2,1,0:T(8,128)S(1)}, f32[2,8,1024]{2,1,0:T(8,128)S(1)}, u32[]{:S(2)}, u32[]{:S(2)}) collective-permute-start(f32[2,8,1024]{2,1,0:T(8,128)S(1)} %get-tuple-element.178.taps), channel_id=1, source_target_pairs={{0,2},{1,3},{2,0},{3,1},{4,6},{5,7},{6,4},{7,5},{8,10},{9,11},{10,... | collective-permute-start | bytes 196616 | tf_op jit(solution)/shard_map/ppermute | solution.py:468
  20.4 6.0 %collective-permute-start.11 = (f32[24,1024]{1,0:T(8,128)S(1)}, f32[24,1024]{1,0:T(8,128)S(1)}, u32[]{:S(2)}, u32[]{:S(2)}) collective-permute-start(f32[24,1024]{1,0:T(8,128)S(1)} %get-tuple-element.180), channel_id=1, source_target_pairs={{0,2},{1,3},{2,0},{3,1},{4,6},{5,7},{6,4},{7,5},{8,10},{9,11},{10,... | collective-permute-start | bytes 294920 | tf_op jit(solution)/shard_map/ppermute | solution.py:465
  26.5 19.8 %copy-start.5 = (f32[24,1024]{1,0:T(8,128)}, f32[24,1024]{1,0:T(8,128)S(1)}, u32[]{:S(2)}) copy-start(f32[24,1024]{1,0:T(8,128)S(1)} %collective-permute-done.11.rest_5_) | copy-start | bytes 294916
  26.5 16.7 %collective-permute-start.13 = (bf16[288,1024]{1,0:T(8,128)(2,1)S(1)}, bf16[288,1024]{1,0:T(8,128)(2,1)S(1)}, u32[]{:S(2)}, u32[]{:S(2)}) collective-permute-start(bf16[288,1024]{1,0:T(8,128)(2,1)S(1)} %get-tuple-element.193), channel_id=1, source_target_pairs={{0,2},{1,3},{2,0},{3,1},{4,6},{5,7},{6,4},{7,5},{8,10},{9,11},{10,... | collective-permute-start | bytes 1769480 | tf_op jit(solution)/shard_map/ppermute | solution.py:465
  27.0 19.2 %collective-permute-start.12 = (bf16[128,1024]{1,0:T(8,128)(2,1)S(1)}, bf16[128,1024]{1,0:T(8,128)(2,1)S(1)}, u32[]{:S(2)}, u32[]{:S(2)}) collective-permute-start(bf16[128,1024]{1,0:T(8,128)(2,1)S(1)} %get-tuple-element.190), channel_id=1, source_target_pairs={{0,3},{1,2},{2,1},{3,0},{4,7},{5,6},{6,5},{7,4},{8,11},{9,10},{10,... | collective-permute-start | bytes 786440 | tf_op jit(solution)/shard_map/ppermute | solution.py:465
  27.1 4.3 %collective-permute-start = (f32[16,1024]{1,0:T(8,128)S(1)}, f32[16,1024]{1,0:T(8,128)S(1)}, u32[]{:S(2)}, u32[]{:S(2)}) collective-permute-start(f32[16,1024]{1,0:T(8,128)S(1)} %get-tuple-element.97), channel_id=1, source_target_pairs={{0,4},{4,0},{8,12},{12,8},{16,20},{20,16},{24,28},{28,24},{1,5},{5... | collective-permute-start | bytes 196616 | tf_op jit(solution)/shard_map/cond/branch_1_fun/ppermute | solution.py:471
  28.6 4.6 %copy-start.3 = (bf16[288,1024]{1,0:T(8,128)(2,1)S(1)}, bf16[288,1024]{1,0:T(8,128)(2,1)}, u32[]{:S(2)}) copy-start(bf16[288,1024]{1,0:T(8,128)(2,1)} %get-tuple-element.106.prod) | copy-start | bytes 1769476 | tf_op jit(solution)/shard_map/cond
  31.4 5.0 %collective-permute-start.1 = (f32[16,1024]{1,0:T(8,128)S(1)}, f32[16,1024]{1,0:T(8,128)S(1)}, u32[]{:S(2)}, u32[]{:S(2)}) collective-permute-start(f32[16,1024]{1,0:T(8,128)S(1)} %add_select_fusion.1), channel_id=1, source_target_pairs={{0,8},{4,12},{8,0},{12,4},{16,24},{20,28},{24,16},{28,20},{1,9},{5... | collective-permute-start | bytes 196616 | tf_op jit(solution)/shard_map/cond/branch_1_fun/ppermute | solution.py:471
  36.5 6.6 %collective-permute-start.2 = (f32[16,1024]{1,0:T(8,128)S(1)}, f32[16,1024]{1,0:T(8,128)S(1)}, u32[]{:S(2)}, u32[]{:S(2)}) collective-permute-start(f32[16,1024]{1,0:T(8,128)S(1)} %add_select_fusion), channel_id=1, source_target_pairs={{0,16},{4,20},{8,24},{12,28},{16,0},{20,4},{24,8},{28,12},{1,17},{... | collective-permute-start | bytes 196616 | tf_op jit(solution)/shard_map/cond/branch_1_fun/ppermute | solution.py:471
  43.1 3.1 %copy-start = (f32[256,1024]{1,0:T(8,128)}, f32[256,1024]{1,0:T(8,128)S(1)}, u32[]{:S(2)}) copy-start(f32[256,1024]{1,0:T(8,128)S(1)} %get-tuple-element.187) | copy-start | bytes 3145732
  50.8 3.7 %collective-permute-start.16 = (bf16[128,2048]{1,0:T(8,128)(2,1)S(1)}, bf16[128,2048]{1,0:T(8,128)(2,1)S(1)}, u32[]{:S(2)}, u32[]{:S(2)}) collective-permute-start(bf16[128,2048]{1,0:T(8,128)(2,1)S(1)} %get-tuple-element.200), channel_id=1, source_target_pairs={{0,1},{1,0},{2,3},{3,2},{4,5},{5,4},{6,7},{7,6},{8,9},{9,8},{10,11... | collective-permute-start | bytes 1572872 | tf_op jit(solution)/shard_map/ppermute | solution.py:465
  53.9 4.5 %copy-start.1 = (f32[256,1024]{1,0:T(8,128)S(1)}, f32[256,1024]{1,0:T(8,128)}, u32[]{:S(2)}) copy-start(f32[256,1024]{1,0:T(8,128)} %copy-done) | copy-start | bytes 3145732
  53.9 4.5 %copy-start.2 = (bf16[288,1024]{1,0:T(8,128)(2,1)S(1)}, bf16[288,1024]{1,0:T(8,128)(2,1)}, u32[]{:S(2)}) copy-start(bf16[288,1024]{1,0:T(8,128)(2,1)} %get-tuple-element.186) | copy-start | bytes 1769476
  53.9 4.5 %copy-start.4 = (bf16[128,4096]{1,0:T(8,128)(2,1)S(1)}, bf16[128,4096]{1,0:T(8,128)(2,1)}, u32[]{:S(2)}) copy-start(bf16[128,4096]{1,0:T(8,128)(2,1)} %param.11) | copy-start | bytes 3145732
  53.9 4.5 %copy-start.6 = (f32[24,1024]{1,0:T(8,128)S(1)}, f32[24,1024]{1,0:T(8,128)}, u32[]{:S(2)}) copy-start(f32[24,1024]{1,0:T(8,128)} %copy-done.5) | copy-start | bytes 294916
  54.0 2.1 %collective-permute-start.14 = (bf16[128,2048]{1,0:T(8,128)(2,1)S(1)}, bf16[128,2048]{1,0:T(8,128)(2,1)S(1)}, u32[]{:S(2)}, u32[]{:S(2)}) collective-permute-start(bf16[128,2048]{1,0:T(8,128)(2,1)S(1)} %get-tuple-element.197), channel_id=1, source_target_pairs={{0,1},{1,0},{2,3},{3,2},{4,5},{5,4},{6,7},{7,6},{8,9},{9,8},{10,11... | collective-permute-start | bytes 1572872 | tf_op jit(solution)/shard_map/ppermute | solution.py:465
  55.5 15.0 %collective-permute-start.17 = (bf16[128,2048]{1,0:T(8,128)(2,1)}, bf16[128,2048]{1,0:T(8,128)(2,1)S(1)}, u32[]{:S(2)}, u32[]{:S(2)}) collective-permute-start(bf16[128,2048]{1,0:T(8,128)(2,1)} %add_convert_fusion), channel_id=1, source_target_pairs={{0,2},{1,3},{2,0},{3,1},{4,6},{5,7},{6,4},{7,5},{8,10},{9,11},{10,... | collective-permute-start | bytes 1572872 | tf_op jit(solution)/shard_map/ppermute | solution.py:468
  57.0 23.8 %collective-permute-start.15 = (bf16[128,2048]{1,0:T(8,128)(2,1)}, bf16[128,2048]{1,0:T(8,128)(2,1)S(1)}, u32[]{:S(2)}, u32[]{:S(2)}) collective-permute-start(bf16[128,2048]{1,0:T(8,128)(2,1)} %add_convert_fusion.1), channel_id=1, source_target_pairs={{0,2},{1,3},{2,0},{3,1},{4,6},{5,7},{6,4},{7,5},{8,10},{9,11},{10,... | collective-permute-start | bytes 1572872 | tf_op jit(solution)/shard_map/ppermute | solution.py:468
  65.8 2.0 %collective-permute-start.4 = (bf16[128,2048]{1,0:T(8,128)(2,1)S(1)}, bf16[128,2048]{1,0:T(8,128)(2,1)S(1)}, u32[]{:S(2)}, u32[]{:S(2)}) collective-permute-start(bf16[128,2048]{1,0:T(8,128)(2,1)S(1)} %get-tuple-element.130), channel_id=1, source_target_pairs={{0,1},{1,0},{2,3},{3,2},{4,5},{5,4},{6,7},{7,6},{8,9},{9,8},{10,11... | collective-permute-start | bytes 1572872 | tf_op jit(solution)/shard_map/cond/branch_1_fun/ppermute | solution.py:465
  65.9 2.6 %collective-permute-start.3 = (bf16[128,2048]{1,0:T(8,128)(2,1)S(1)}, bf16[128,2048]{1,0:T(8,128)(2,1)S(1)}, u32[]{:S(2)}, u32[]{:S(2)}) collective-permute-start(bf16[128,2048]{1,0:T(8,128)(2,1)S(1)} %get-tuple-element.126), channel_id=1, source_target_pairs={{0,1},{1,0},{2,3},{3,2},{4,5},{5,4},{6,7},{7,6},{8,9},{9,8},{10,11... | collective-permute-start | bytes 1572872 | tf_op jit(solution)/shard_map/cond/branch_1_fun/ppermute | solution.py:465

commit v3 on v2

--- a/solution.py
+++ b/solution.py
@@ -1,4 +1,5 @@
 import functools
+import math
 
 import jax
 import jax.numpy as jnp
@@ -205,67 +206,39 @@
 def toeplitz_kernel(chunk, rate_row, coef_row, *rest):
     out = rest[-1]
     lag = (LANES - 1 - iota((LANES, LANES), 1)).astype(F32)
-    rate = jnp.broadcast_to(rate_row[...], (LANES, LANES)).T
-    coef = jnp.broadcast_to(coef_row[...], (LANES, LANES)).T
-    taps = jnp.sum((coef * jnp.exp(-rate * lag)).reshape(PER_TILE, ORDER, LANES), axis=1)
-    valid = iota((LANES, LANES), 1) <= iota((LANES, LANES), 0)
-    for g in range(PER_TILE):
-        spread = jnp.broadcast_to(taps[g : g + 1], (8, LANES))
-        top = pltpu.roll(spread, 1, 1, stride=1, stride_axis=0)
-        block = jnp.concatenate([top] + [pltpu.roll(top, at, 1) for at in range(8, chunk, 8)], axis=0)
-        block = jnp.where(valid[:chunk], block, 0.0)
-        out[g * chunk : (g + 1) * chunk, :] = block[:, :chunk].astype(BF16)
+    valid = iota((chunk, LANES), 1) <= iota((chunk, LANES), 0)
+    for w in range(rate_row.shape[1] // LANES):
+        lanes = slice(w * LANES, (w + 1) * LANES)
+        rate = jnp.broadcast_to(rate_row[:, lanes], (LANES, LANES)).T
+        coef = jnp.broadcast_to(coef_row[:, lanes], (LANES, LANES)).T
+        taps = jnp.sum((coef * jnp.exp(-rate * lag)).reshape(PER_TILE, ORDER, LANES), axis=1)
+        for g in range(PER_TILE):
+            spread = jnp.broadcast_to(taps[g : g + 1], (8, LANES))
+            top = pltpu.roll(spread, 1, 1, stride=1, stride_axis=0)
+            block = jnp.concatenate([top] + [pltpu.roll(top, at, 1) for at in range(8, chunk, 8)], axis=0)
+            at = (w * PER_TILE + g) * chunk
+            out[at : at + chunk, :] = jnp.where(valid, block, 0.0)[:, :chunk].astype(BF16)
 
 
 def toeplitz(rate_row, coef_row, chunk, first_tile, tiles, made=None):
     made = [] if made is None else [made]
+    together = 4 if tiles % 4 == 0 and first_tile % 4 == 0 else 1
+    at = first_tile // together
     return pl.pallas_call(
         functools.partial(toeplitz_kernel, chunk),
-        grid=(tiles,),
-        in_specs=[pl.BlockSpec((1, LANES), lambda i: (0, first_tile + i))] * 2 + [pl.BlockSpec(memory_space=pl.ANY)] * len(made),
-        out_specs=pl.BlockSpec((PER_TILE * chunk, chunk), lambda i: (first_tile + i, 0)),
+        grid=(tiles // together,),
+        in_specs=[pl.BlockSpec((1, together * LANES), lambda i: (0, at + i))] * 2 + [pl.BlockSpec(memory_space=pl.ANY)] * len(made),
+        out_specs=pl.BlockSpec((together * PER_TILE * chunk, chunk), lambda i: (at + i, 0)),
         out_shape=jax.ShapeDtypeStruct((rate_row.shape[1] // GROUP_CH * chunk, chunk), BF16),
         input_output_aliases={2: 0} if made else {},
         cost_estimate=BRIEF,
     )(rate_row, coef_row, *made)
 
 
-def local_kernel(prod, toep, out):
-    rows, width = out.shape[0] // 2, out.shape[1]
-    lane_group = iota((rows, LANES), 1) // GROUP_CH
-    for w in range(width // LANES):
-        lanes = slice(w * LANES, (w + 1) * LANES)
-        beside = jnp.concatenate([prod[:rows, lanes], prod[rows : 2 * rows, lanes]], axis=1)
-        local = dot(toep[w * PER_TILE * rows : (w + 1) * PER_TILE * rows, :], beside)
-        for i in range(2):
-            cols = slice(i * LANES, (i + 1) * LANES)
-            kept = local[:rows, cols]
-            for g in range(1, PER_TILE):
-                kept = jnp.where(lane_group == g, local[g * rows : (g + 1) * rows, cols], kept)
-            out[i * rows : (i + 1) * rows, lanes] = kept
-
-
-def local(prod, toep):
-    rows, width = toep.shape[1], prod.shape[1]
-    block = min(512, width)
-    return pl.pallas_call(
-        local_kernel,
-        grid=(width // block,),
-        in_specs=[
-            pl.BlockSpec((prod.shape[0], block), lambda i: (0, i)),
-            pl.BlockSpec((block // GROUP_CH * rows, rows), lambda i: (i, 0)),
-        ],
-        out_specs=pl.BlockSpec((2 * rows, block), lambda i: (0, i)),
-        out_shape=jax.ShapeDtypeStruct((2 * rows, width), F32),
-        compiler_params=pltpu.CompilerParams(vmem_limit_bytes=12 << 20),
-        cost_estimate=BRIEF,
-    )(prod, toep)
-
-
-def weight_copies(weights, part, cols, held, sems):
+def weight_copies(weights, first, held, sems):
     share = held.shape[2]
     return [
-        pltpu.make_async_copy(weights.at[:, pl.ds(part * cols + j * share, share)], held.at[j], sems.at[j])
+        pltpu.make_async_copy(weights.at[:, pl.ds(first + j * share, share)], held.at[j], sems.at[j])
         for j in range(held.shape[0])
     ]
 
@@ -279,18 +252,18 @@
         mine[:, j * share : (j + 1) * share] = product[rows:].astype(BF16)
 
 
-def gate_kernel(d, chips, info, local, inner, q0, q1, *rest):
-    steps = 2 * chips
-    ends, states, rest = rest[:steps], rest[steps : steps + chips], rest[steps + chips :]
+def gate_kernel(d, chips, info, prod, toep, q0, q1, *rest):
+    states, rest = rest[:chips], rest[chips:]
     taps, before, wide_rates, rate_row, coef_row, weights, out, theirs, mine, pad, gated, held, sems = rest
     rows, width = q0.shape[-2:]
-    cols = theirs.shape[1]
     step = min(64, rows)
     mask = own_group()
     later = (iota((rows, LANES), 0) + 1).astype(F32)
     places = [source(info[0], 2 * d + 1, chips), source(info[0], 2 * d, chips)]
+    begins = [pl.multiple_of((place % 2) * rows, rows) for place in places]
+    lane_group = iota((step, LANES), 1) // GROUP_CH
     turn = pl.program_id(0)
-    copies = weight_copies(weights, 0, cols, held, sems)
+    copies = weight_copies(weights, 0, held, sems)
 
     @pl.when(turn == 0)
     def _():
@@ -311,23 +284,27 @@
         state = before[:, lanes]
         for y in range(chips - 1):
             state = jnp.where(y < places[0] // 2, fade * state + by_chip[y][:ORDER], state)
-        halfway = inner[0:ORDER, lanes].astype(F32) + inner[ORDER:, lanes].astype(F32)
+        inner = prod[2 * rows :, lanes].astype(F32)
+        halfway = inner[:ORDER] + inner[ORDER:]
         halfway = jnp.exp(-rate * float(rows)) * state + halfway
         entering = [jnp.where(place % 2 == 0, state, halfway) for place in places]
         entering = [jnp.where(mask, jnp.concatenate([value] * PER_TILE, axis=0), 0.0) for value in entering]
         state_high, state_low = halves(jnp.concatenate(entering, axis=1))
         carried = dot(into_high, state_high) + dot(into_high, state_low) + dot(into_low, state_high)
+        beside = jnp.concatenate([prod[pl.ds(at, rows), lanes] for at in begins], axis=1)
+        local = dot(toep[w * PER_TILE * rows : (w + 1) * PER_TILE * rows, :], beside)
         tap = taps[0, :, lanes]
         for i, (q, place) in enumerate(zip((q0, q1), places)):
-            tail = by_chip[0][ORDER:]
-            for e, end in enumerate(ends):
-                rows_before = (end[0, :, lanes] if e == 0 else end[:, lanes]).astype(F32)[EDGE:]
-                tail = jnp.where(source(info[0], e, chips) == place - 1, rows_before, tail)
-            pad[w, i, 0:EDGE, :] = tail
+            other = (q1, q0)[i]
+            other = (other[0, rows - 2 * EDGE :, lanes] if d == 0 and i == 0 else other[rows - 2 * EDGE :, lanes]).astype(F32)
+            pad[w, i, 0:EDGE, :] = jnp.where(place % 2 == 0, states[d][ORDER:, lanes], other[EDGE:])
             pad[w, i, EDGE:, :] = (q[0, :, lanes] if d == 0 and i == 1 else q[:, lanes]).astype(F32)
-            base = pl.multiple_of((place % 2) * rows, rows)
+            cols_of = slice(i * LANES, (i + 1) * LANES)
             for start in range(0, rows, step):
-                long = local[pl.ds(base + start, step), lanes] + carried[start : start + step, i * LANES : (i + 1) * LANES]
+                long = local[start : start + step, cols_of]
+                for g in range(1, PER_TILE):
+                    long = jnp.where(lane_group == g, local[g * rows + start : g * rows + start + step, cols_of], long)
+                long = long + carried[start : start + step, cols_of]
                 value = convolve(pad.at[w, i], tap, start, step) * long
                 at = i * rows + start
                 gated[turn, at : at + step, lanes] = value.astype(BF16)
@@ -339,25 +316,15 @@
         multiply(whole, copies, held, theirs, mine)
 
 
-def gate(info, d, chips, local, prod, feats, pieces, states, taps, before, wide_rates, rate_row, coef_row, weights, parts):
+def gate(info, d, chips, prod, toep, feats, pieces, states, taps, before, wide_rates, rate_row, coef_row, weights, cols):
     rows = feats.shape[1]
     width = taps.shape[2]
-    steps = 2 * chips
-    cols = weights.shape[1] // parts
     block = min(512, width)
     per = width // block
     share = min(512, cols)
 
     def spec(*shape):
         return pl.BlockSpec(shape + (block,), lambda i, info: (0,) * len(shape) + (i,))
-
-    def of_own(count):
-        at = rows // count - 1
-        return pl.BlockSpec((1, count, block), lambda i, info: (0, at, info[0] * per + i))
-
-    def of_piece(count):
-        at = rows // count - 1
-        return pl.BlockSpec((count, block), lambda i, info: (at, i))
 
     def whole(*shape):
         return pl.BlockSpec(shape, lambda i, info: (0,) * len(shape))
@@ -368,9 +335,8 @@
         grid_spec=pltpu.PrefetchScalarGridSpec(
             num_scalar_prefetch=1,
             grid=(per,),
-            in_specs=[spec(2 * rows), pl.BlockSpec((2 * ORDER, block), lambda i, info: (rows // ORDER, i))]
-            + [of_piece(rows), of_piece(rows) if d > 0 else of_own(rows), of_own(2 * EDGE)]
-            + [of_piece(2 * EDGE)] * (steps - 1)
+            in_specs=[spec(2 * rows + 2 * ORDER), pl.BlockSpec((block // GROUP_CH * rows, rows), lambda i, info: (i, 0))]
+            + [spec(rows), spec(rows) if d > 0 else pl.BlockSpec((1, rows, block), lambda i, info: (0, 0, info[0] * per + i))]
             + [spec(ORDER + EDGE)] * chips
             + [spec(3, TAPS), spec(ORDER), spec(ORDER), spec(1), spec(1)]
             + [pl.BlockSpec(memory_space=pltpu.HBM)],
@@ -387,25 +353,24 @@
             jax.ShapeDtypeStruct((rows, cols), BF16),
             jax.ShapeDtypeStruct((rows, cols), BF16),
         ],
-        compiler_params=pltpu.CompilerParams(vmem_limit_bytes=20 << 20),
+        compiler_params=pltpu.CompilerParams(vmem_limit_bytes=24 << 20),
         cost_estimate=BRIEF,
-    )(info, local, prod, *pair, feats, *pieces, *states, taps, before, wide_rates, rate_row, coef_row, weights)
-
-
-def project_kernel(part, gated, weights, theirs, mine, held, sems):
-    copies = weight_copies(weights, part, theirs.shape[1], held, sems)
+    )(info, prod, toep, *pair, *states, taps, before, wide_rates, rate_row, coef_row, weights)
+
+
+def project_kernel(first, gated, weights, theirs, mine, held, sems):
+    copies = weight_copies(weights, first, held, sems)
     for copy in copies:
         copy.start()
     multiply(gated[...], copies, held, theirs, mine)
 
 
-def project(gated, weights, part, parts):
+def project(gated, weights, first, cols):
     rows, width = gated.shape[0] // 2, gated.shape[1]
-    cols = weights.shape[1] // parts
     share = min(512, cols)
     vmem = pl.BlockSpec(memory_space=pltpu.VMEM)
     return pl.pallas_call(
-        functools.partial(project_kernel, part),
+        functools.partial(project_kernel, first),
         in_specs=[vmem, pl.BlockSpec(memory_space=pltpu.HBM)],
         out_specs=[vmem] * 2,
         out_shape=[jax.ShapeDtypeStruct((rows, cols), BF16)] * 2,
@@ -415,39 +380,43 @@
     )(gated, weights)
 
 
-def finish_kernel(part, count, base, *rest):
-    terms, (out, ready, sems) = rest[:count], rest[-3:]
-    rows, cols = base.shape
+def finish_kernel(first, blocks, count, *rest):
+    bases, terms, (out, ready, sems) = rest[:blocks], rest[blocks : blocks + count], rest[-3:]
+    rows, cols = ready.shape
     step = min(32, rows)
     copies = []
     for i in range(rows // step):
         span = slice(i * step, (i + 1) * step)
-        total = base[span, :]
+        total = jnp.concatenate([base[span, :] for base in bases], axis=1)
         for term in terms:
             total = total + term[span, :].astype(F32)
         ready[span, :] = total.astype(BF16)
         here = ready.at[pl.ds(i * step, step), :]
-        copies.append(pltpu.make_async_copy(here, out.at[pl.ds(i * step, step), pl.ds(part * cols, cols)], sems.at[i]))
+        copies.append(pltpu.make_async_copy(here, out.at[pl.ds(i * step, step), pl.ds(first, cols)], sems.at[i]))
         copies[-1].start()
     for copy in copies:
         copy.wait()
 
 
-def finish(part, parts, base, terms, out):
-    rows, cols = base.shape
+def finish(first, cols, base, terms, out):
+    rows, depth = base.shape
     before = [] if out is None else [out]
+    block = math.gcd(first, cols)
     vmem = pl.BlockSpec(memory_space=pltpu.VMEM)
     hbm = pl.BlockSpec(memory_space=pltpu.HBM)
     return pl.pallas_call(
-        functools.partial(finish_kernel, part, len(terms)),
-        in_specs=[vmem] * (1 + len(terms)) + [hbm] * len(before),
+        functools.partial(finish_kernel, first, cols // block, len(terms)),
+        grid=(1,),
+        in_specs=[pl.BlockSpec((rows, block), lambda i, at=first // block + j: (0, at)) for j in range(cols // block)]
+        + [vmem] * len(terms)
+        + [hbm] * len(before),
         out_specs=hbm,
-        out_shape=jax.ShapeDtypeStruct((rows, cols * parts), BF16),
+        out_shape=jax.ShapeDtypeStruct((rows, depth), BF16),
         scratch_shapes=[pltpu.VMEM((rows, cols), BF16), pltpu.SemaphoreType.DMA((rows // min(32, rows),))],
-        input_output_aliases={1 + len(terms): 0} if before else {},
+        input_output_aliases={cols // block + len(terms): 0} if before else {},
         compiler_params=pltpu.CompilerParams(vmem_limit_bytes=12 << 20),
         cost_estimate=BRIEF,
-    )(base, *terms, *before)
+    )(*[base] * (cols // block), *terms, *before)
 
 
 def body(chips, contexts, features, residual, short_weight, rates, residues, out_weight):
@@ -479,7 +448,6 @@
     kv_out, edge0, edge1, kv_taps, rate_row, coef_row, wide_rates, *pieces = first(info, feats, taps, *poles, chips)
     tiles = width // LANES
     early = tiles // 2
-    toep = toeplitz(rate_row, coef_row, rows, 0, early)
 
     kv_taps = [kv_taps] + [send_back(kv_taps, 2 * d) for d in range(1, chips)]
 
@@ -490,19 +458,19 @@
     ]
 
     kv_in = send(kv_out, 1)
+    kv_in, edges, kv_taps, pieces = lax.optimization_barrier((kv_in, edges, kv_taps, pieces))
     pieces[:chips] = [send(piece, e) for e, piece in enumerate(pieces[:chips], 1)]
-    kv_in, edges, pieces[:chips], toep = lax.optimization_barrier((kv_in, edges, pieces[:chips], toep))
 
     prods, states = [None] * chips, [None] * chips
     for d in list(range(1, chips)) + [0]:
         prods[d], states[d] = front(info, d, chips, feats, kv_in, *edges, kv_taps[d])
         if d > 0:
             states[d] = send(states[d], 2 * d)
-    states, prods, pieces[chips:] = lax.optimization_barrier((states, prods, pieces[chips:]))
+    states, prods, pieces = lax.optimization_barrier((states, prods, pieces))
     prods[1:] = [send(prods[d], 2 * d) for d in range(1, chips)]
     pieces[chips:] = [send(piece, e) for e, piece in enumerate(pieces[chips:], chips + 1)]
 
-    def relay(states, prod, toep):
+    def relay(states):
         by_chip = [
             sum(jnp.where((chip - d) % chips == y, state[:ORDER], 0.0) for d, state in enumerate(states))
             for y in range(chips)
@@ -524,49 +492,59 @@
             before = before + places[i] * got
             total = jnp.where((ctx & bit) != 0, pasts[i] * got + total, pasts[i] * total + got)
             if i == 0:
+                toep = toeplitz(rate_row, coef_row, rows, 0, early)
+                total, toep = lax.optimization_barrier((total, toep))
+            if i == 1:
                 toep = toeplitz(rate_row, coef_row, rows, early, tiles - early, toep)
                 total, toep = lax.optimization_barrier((total, toep))
-            if i == 1:
-                near = local(prod, toep)
-                total, near = lax.optimization_barrier((total, near))
-        return before, near, toep
-
-    def no_relay(states, prod, toep):
-        return wide_rates, jnp.zeros((chip_rows, width), F32), toep
-
-    before, near, toep = lax.cond(always, relay, no_relay, states, prods[0], toep)
-
-    parts = 2
-    cols = depth // parts
+        return before, toep
+
+    def no_relay(states):
+        return wide_rates, jnp.zeros((width // GROUP_CH * rows, rows), BF16)
+
+    before, toep = lax.cond(always, relay, no_relay, states)
+
+    parts = [(0, depth // 4), (depth // 4, 3 * depth // 8), (5 * depth // 8, 3 * depth // 8)]
     weights = in_hbm(out_weight)
 
-    def projected(d):
-        inside = local(prods[d], toep) if d > 0 else near
-        gated, theirs, mine = gate(
-            info, d, chips, inside, prods[d], feats, pieces, states, taps, before, wide_rates, rate_row, coef_row,
-            weights, parts,
+    def gated_rows(d, prod, cols):
+        return gate(
+            info, d, chips, prod, toep, feats, pieces, states, taps, before, wide_rates, rate_row, coef_row,
+            weights, cols,
         )
-        sums = []
-        for p in range(parts):
-            if p > 0:
-                theirs, mine = project(gated, weights, p, parts)
-            sums.append(mine.astype(F32) + send(theirs, 1).astype(F32))
-        return sums
-
-    arriving = [[] for _ in range(parts)]
+
+    def summed(theirs, mine):
+        return mine.astype(F32) + send(theirs, 1).astype(F32)
+
+    def own(prod):
+        _, theirs, mine = gated_rows(0, prod, depth)
+        return residual.astype(F32) + summed(theirs, mine)
+
+    def no_own(prod):
+        return jnp.zeros((rows, depth), F32)
+
+    gateds, wholes, arriving = [], [], []
     for d in range(1, chips):
-        for p, value in enumerate(projected(d)):
-            arriving[p].append(send_back(value.astype(BF16), 2 * d))
-
-    def own():
-        return [
-            value + residual[:, p * cols : (p + 1) * cols].astype(F32) for p, value in enumerate(projected(0))
-        ]
-
-    bases = lax.cond(always, own, lambda: [jnp.zeros((rows, cols), F32)] * parts)
+        gated, *first_part = gated_rows(d, prods[d], parts[0][1])
+        gateds.append(gated)
+        wholes.append(summed(*first_part).astype(BF16))
+    for part in parts[1:]:
+
+        def others(gateds, part=part):
+            return [summed(*project(gated, weights, *part)).astype(BF16) for gated in gateds]
+
+        def no_others(gateds, part=part):
+            return [jnp.zeros((rows, part[1]), BF16) for _ in gateds]
+
+        gateds, wholes = lax.optimization_barrier((gateds, wholes))
+        arriving.append([send_back(whole, 2 * d) for d, whole in enumerate(wholes, 1)])
+        wholes = lax.cond(always, others, no_others, gateds)
+    prods[0], wholes, arriving[0] = lax.optimization_barrier((prods[0], wholes, arriving[0]))
+    arriving.append([send_back(whole, 2 * d) for d, whole in enumerate(wholes, 1)])
+    base = lax.cond(always, own, no_own, prods[0])
     out = None
-    for p in range(parts):
-        out = finish(p, parts, bases[p], arriving[p], out)
+    for (first_col, cols), terms in zip(parts, arriving):
+        out = finish(first_col, cols, base, terms, out)
     return out
 
 

time: 81.9 us -> 77.2 us (0.943)
  Pallas kernels: 36.3 us -> 33.6 us
  waiting for transfers between devices: 18.6 us -> 17.6 us
    ppermute x3 -> x4, waiting for transfers between devices: 10.9 us -> 2.25 us  [send_back(): lax.ppermute(value, 'tp', [(i, source(i, e, chips)) for i in range(steps)])]
    ppermute x10, waiting for transfers between devices: 2.77 us -> 9.59 us  [send(): lax.ppermute(value, 'tp', [(i, target(i, e, chips)) for i in range(steps)])]
    pallas_call x8 -> x7, Pallas kernels: 18.1 us -> 11.8 us  [the longest x2 5.13 us: project(): pl.pallas_call(functools.partial(project_kernel, first), in_specs=[vmem,...]
    pallas_call x2, Pallas kernels: 8.89 us -> 12.6 us  [gate(): pl.pallas_call(functools.partial(gate_kernel, d, chips), grid_spec=pltpu....]
    ppermute x3 -> x4, starting transfers between devices: 9.42 us -> 6.85 us  [send_back(): lax.ppermute(value, 'tp', [(i, source(i, e, chips)) for i in range(steps)])]
    ppermute x10, starting transfers between devices: 7.2 us -> 9.39 us  [send(): lax.ppermute(value, 'tp', [(i, target(i, e, chips)) for i in range(steps)])]
    convert_element_type x2 -> x3, other arithmetic: 1.85 us -> 1.72 us  [the longest x2 1.66 us: others(): summed(*project(gated, weights, *part)).astype(BF16)]
  transfers between devices with their start and end apart: 18 -> 19, of which waited for: 8 -> 10; matrix products, arithmetic and copies ran while one was open for 3% -> 3% of each run, Pallas kernels for 32% -> 35%
where the time goes in v3:
time: 77.2 us; the launch traced here: 77 us
  Pallas kernels  33.6 us (44%)
  starting transfers between devices  23.4 us (30%)
  waiting for transfers between devices  17.6 us (23%)
  other arithmetic  2.26 us (3%)
    pallas_call x2, Pallas kernels, gate(): pl.pallas_call(functools.partial(gate_kernel, d, chips), grid_spec=pltpu....  12.6 us
    ppermute x10, waiting for transfers between devices, send(): lax.ppermute(value, 'tp', [(i, target(i, e, chips)) for i in range(steps)])  9.59 us
    ppermute x10, starting transfers between devices, send(): lax.ppermute(value, 'tp', [(i, target(i, e, chips)) for i in range(steps)])  9.39 us
    pallas_call x2, Pallas kernels, front(): pl.pallas_call(front_kernel, grid_spec=pltpu.PrefetchScalarGridSpec(num_s...  7.46 us
    ppermute x4, starting transfers between devices, send_back(): lax.ppermute(value, 'tp', [(i, source(i, e, chips)) for i in range(steps)])  6.85 us
    ppermute x3, starting transfers between devices, with_context(): return lax.ppermute(value, 'ctx', [(i, i ^ bit) for i in range(contexts)])  5.82 us
    ppermute x3, waiting for transfers between devices, with_context(): return lax.ppermute(value, 'ctx', [(i, i ^ bit) for i in range(contexts)])  5.72 us
    pallas_call x2, Pallas kernels, project(): pl.pallas_call(functools.partial(project_kernel, first), in_specs=[vmem,...  5.13 us
  transfers between devices with their start and end apart: 19, of which 10 were waited for; matrix products, arithmetic and copies ran while one was open for 3% of the time, Pallas kernels for 35%

profile of v3, /device:TPU:0, one launch (start us, length us, event | category | flops | bytes accessed | tf_op | source)
XLA Modules:
  0.0 77.0 jit_solution(10784734691082265360)
XLA Ops:
  0.0 1.7 %shard_map.65 = (bf16[2,128,2048]{2,1,0:T(8,128)(2,1)S(1)}, bf16[3,8,2048]{2,1,0:T(8,128)(2,1)S(1)}, bf16[3,8,2048]{2,1,0:T(8,128)(2,1)S(1)}, f32[2,8,1024]{2,1,...) custom-call(s32[1]{0:T(128)} %bitcast.info, ...), custom_call_target="tpu_custom_call" | custom-call | flops 1 | bytes 1 | tf_op jit(solution)/shard_map/pallas_call | solution.py:115
  3.6 3.2 %collective-permute-start.9 = (f32[2,8,1024]{2,1,0:T(8,128)S(1)}, f32[2,8,1024]{2,1,0:T(8,128)S(1)}, u32[]{:S(2)}, u32[]{:S(2)}) collective-permute-start(f32[2,8,1024]{2,1,0:T(8,128)S(1)} %get-tuple-element.187.taps), channel_id=1, source_target_pairs={{0,2},{1,3},{2,0},{3,1},{4,6},{5,7},{6,4},{7,5},{8,10},{9,11},{10,... | collective-permute-start | bytes 196616 | tf_op jit(solution)/shard_map/ppermute | solution.py:437
  6.8 2.2 %collective-permute-done.9.taps = f32[2,8,1024]{2,1,0:T(8,128)S(1)} collective-permute-done((f32[2,8,1024]{2,1,0:T(8,128)S(1)}, f32[2,8,1024]{2,1,0:T(8,128)S(1)}, u32[]{:S(2)}, u32[]{:S(2)}) %collective-permute-start.9) | collective-permute-done | bytes 65568 | tf_op jit(solution)/shard_map/ppermute | solution.py:437
  9.1 4.1 %collective-permute-start.11 = (bf16[128,1024]{1,0:T(8,128)(2,1)S(1)}, bf16[128,1024]{1,0:T(8,128)(2,1)S(1)}, u32[]{:S(2)}, u32[]{:S(2)}) collective-permute-start(bf16[128,1024]{1,0:T(8,128)(2,1)S(1)} %get-tuple-element.193), channel_id=1, source_target_pairs={{0,1},{1,0},{2,3},{3,2},{4,5},{5,4},{6,7},{7,6},{8,9},{9,8},{10,11... | collective-permute-start | bytes 786440 | tf_op jit(solution)/shard_map/ppermute | solution.py:434
  13.2 1.5 %collective-permute-start.12 = (bf16[128,1024]{1,0:T(8,128)(2,1)S(1)}, bf16[128,1024]{1,0:T(8,128)(2,1)S(1)}, u32[]{:S(2)}, u32[]{:S(2)}) collective-permute-start(bf16[128,1024]{1,0:T(8,128)(2,1)S(1)} %get-tuple-element.194), channel_id=1, source_target_pairs={{0,2},{1,3},{2,0},{3,1},{4,6},{5,7},{6,4},{7,5},{8,10},{9,11},{10,... | collective-permute-start | bytes 786440 | tf_op jit(solution)/shard_map/ppermute | solution.py:434
  14.7 3.4 %shard_map.67 = (bf16[288,1024]{1,0:T(8,128)(2,1)S(1)}, f32[24,1024]{1,0:T(8,128)S(1)}) custom-call(s32[1]{0:T(128)} %bitcast.info, bf16[3,128,4096]{2,1,0:T(8,128)(2,1)} %bitcast.6, bf16[3,128,4096]{2,1,0:T(8,128)(2,1)} %bitcast.7, bf16[2,128,2048]{2,1,0:T(8,128)(2,1)S(1)} %collective-permute-done.6.kv_in, ...), custom_call_target="tpu_custom_call" | custom-call | flops 1 | bytes 1 | tf_op jit(solution)/shard_map/pallas_call | solution.py:191
  18.7 4.0 %shard_map.66 = (bf16[288,1024]{1,0:T(8,128)(2,1)}, f32[24,1024]{1,0:T(8,128)S(1)}) custom-call(s32[1]{0:T(128)} %bitcast.info, bf16[3,128,4096]{2,1,0:T(8,128)(2,1)} %bitcast.8, bf16[3,128,4096]{2,1,0:T(8,128)(2,1)} %bitcast.9, bf16[2,128,2048]{2,1,0:T(8,128)(2,1)S(1)} %collective-permute-done.6.kv_in, ...), custom_call_target="tpu_custom_call" | custom-call | flops 1 | bytes 1 | tf_op jit(solution)/shard_map/pallas_call | solution.py:191
  22.7 0.8 %collective-permute-done.10.rest_1_ = f32[24,1024]{1,0:T(8,128)S(1)} collective-permute-done((f32[24,1024]{1,0:T(8,128)S(1)}, f32[24,1024]{1,0:T(8,128)S(1)}, u32[]{:S(2)}, u32[]{:S(2)}) %collective-permute-start.10) | collective-permute-done | bytes 98336 | tf_op jit(solution)/shard_map/ppermute | solution.py:434
  23.6 1.6 %collective-permute-start.13 = (bf16[288,1024]{1,0:T(8,128)(2,1)S(1)}, bf16[288,1024]{1,0:T(8,128)(2,1)S(1)}, u32[]{:S(2)}, u32[]{:S(2)}) collective-permute-start(bf16[288,1024]{1,0:T(8,128)(2,1)S(1)} %get-tuple-element.197), channel_id=1, source_target_pairs={{0,2},{1,3},{2,0},{3,1},{4,6},{5,7},{6,4},{7,5},{8,10},{9,11},{10,... | collective-permute-start | bytes 1769480 | tf_op jit(solution)/shard_map/ppermute | solution.py:434
  25.2 16.0 %conditional.4 = (f32[16,1024]{1,0:T(8,128)S(1)}, bf16[8192,128]{1,0:T(8,128)(2,1)}) conditional(s32[]{:T(128)} %convert_element_type.48, f32[16,1024]{1,0:T(8,128)S(1)} %get-tuple-element.198.rest_4_, (f32[16,1024]{1,0:T(8,128)S(1)}, s32[]{:T(128)}, s32[]{:T(128)}, f32[24,1024]{1,0:T(8,128)S(1)}, f32[24,1024]{1,0:T(8,128)S(1)}, /*index=5*/s32[]{:T(128)}, ...), branch_computations={%region_0.1_spmd, %region_1.2_spmd} | conditional | flops 540727 | bytes 2359982 | solution.py:505
  25.2 1.6 %collective-permute-start = (f32[16,1024]{1,0:T(8,128)S(1)}, f32[16,1024]{1,0:T(8,128)S(1)}, u32[]{:S(2)}, u32[]{:S(2)}) collective-permute-start(f32[16,1024]{1,0:T(8,128)S(1)} %get-tuple-element.101), channel_id=1, source_target_pairs={{0,4},{4,0},{8,12},{12,8},{16,20},{20,16},{24,28},{28,24},{1,5},{5... | collective-permute-start | bytes 196616 | tf_op jit(solution)/shard_map/cond/branch_1_fun/ppermute | solution.py:440
  26.8 2.2 %branch_1_fun.5.rest_0_ = bf16[8192,128]{1,0:T(8,128)(2,1)} custom-call(f32[1,1024]{1,0:T(1,128)S(1)} %get-tuple-element.104.rate_row, f32[1,1024]{1,0:T(1,128)S(1)} %get-tuple-element.105.coef_row), custom_call_target="tpu_custom_call" | custom-call | flops 1 | bytes 1 | tf_op jit(solution)/shard_map/cond/branch_1_fun/pallas_call | solution.py:227
  29.0 1.1 %collective-permute-done = f32[16,1024]{1,0:T(8,128)S(1)} collective-permute-done((f32[16,1024]{1,0:T(8,128)S(1)}, f32[16,1024]{1,0:T(8,128)S(1)}, u32[]{:S(2)}, u32[]{:S(2)}) %collective-permute-start) | collective-permute-done | bytes 65568 | tf_op jit(solution)/shard_map/cond/branch_1_fun/ppermute | solution.py:440
  30.2 1.4 %collective-permute-start.1 = (f32[16,1024]{1,0:T(8,128)S(1)}, f32[16,1024]{1,0:T(8,128)S(1)}, u32[]{:S(2)}, u32[]{:S(2)}) collective-permute-start(f32[16,1024]{1,0:T(8,128)S(1)} %add_select_fusion.1), channel_id=1, source_target_pairs={{0,8},{4,12},{8,0},{12,4},{16,24},{20,28},{24,16},{28,20},{1,9},{5... | collective-permute-start | bytes 196616 | tf_op jit(solution)/shard_map/cond/branch_1_fun/ppermute | solution.py:440
  31.6 2.2 %branch_1_fun.6 = bf16[8192,128]{1,0:T(8,128)(2,1)} custom-call(f32[1,1024]{1,0:T(1,128)S(1)} %get-tuple-element.104.rate_row, f32[1,1024]{1,0:T(1,128)S(1)} %get-tuple-element.105.coef_row, bf16[8192,128]{1,0:T(8,128)(2,1)} %branch_1_fun.5.rest_0_), custom_call_target="tpu_custom_call", output_to_operand_aliasing={{}: (2, {})} | custom-call | flops 1 | bytes 1 | tf_op jit(solution)/shard_map/cond/branch_1_fun/pallas_call | solution.py:227
  34.5 2.8 %collective-permute-start.2 = (f32[16,1024]{1,0:T(8,128)S(1)}, f32[16,1024]{1,0:T(8,128)S(1)}, u32[]{:S(2)}, u32[]{:S(2)}) collective-permute-start(f32[16,1024]{1,0:T(8,128)S(1)} %add_select_fusion), channel_id=1, source_target_pairs={{0,16},{4,20},{8,24},{12,28},{16,0},{20,4},{24,8},{28,12},{1,17},{... | collective-permute-start | bytes 196616 | tf_op jit(solution)/shard_map/cond/branch_1_fun/ppermute | solution.py:440
  37.3 3.9 %collective-permute-done.2 = f32[16,1024]{1,0:T(8,128)S(1)} collective-permute-done((f32[16,1024]{1,0:T(8,128)S(1)}, f32[16,1024]{1,0:T(8,128)S(1)}, u32[]{:S(2)}, u32[]{:S(2)}) %collective-permute-start.2) | collective-permute-done | bytes 65568 | tf_op jit(solution)/shard_map/cond/branch_1_fun/ppermute | solution.py:440
  41.2 1.6 %collective-permute-done.14.q0 = bf16[128,1024]{1,0:T(8,128)(2,1)S(1)} collective-permute-done((bf16[128,1024]{1,0:T(8,128)(2,1)S(1)}, bf16[128,1024]{1,0:T(8,128)(2,1)S(1)}, u32[]{:S(2)}, u32[]{:S(2)}) %collective-permute-start.14) | collective-permute-done | bytes 262176 | tf_op jit(solution)/shard_map/ppermute | solution.py:434
  42.8 4.5 %shard_map.68 = (bf16[256,1024]{1,0:T(8,128)(2,1)S(1)}, bf16[128,1024]{1,0:T(8,128)(2,1)S(1)}, bf16[128,1024]{1,0:T(8,128)(2,1)S(1)}) custom-call(s32[1]{0:T(128)} %bitcast.info, bf16[288,1024]{1,0:T(8,128)(2,1)S(1)} %collective-permute-done.13.prod, bf16[8192,128]{1,0:T(8,128)(2,1)} %get-tuple-element.203.toep, ...), custom_call_target="tpu_custom_call" | custom-call | flops 1 | bytes 1 | tf_op jit(solution)/shard_map/pallas_call | solution.py:333
  47.2 0.8 %collective-permute-start.15 = (bf16[128,1024]{1,0:T(8,128)(2,1)S(1)}, bf16[128,1024]{1,0:T(8,128)(2,1)S(1)}, u32[]{:S(2)}, u32[]{:S(2)}) collective-permute-start(bf16[128,1024]{1,0:T(8,128)(2,1)S(1)} %get-tuple-element.209), channel_id=1, source_target_pairs={{0,1},{1,0},{2,3},{3,2},{4,5},{5,4},{6,7},{7,6},{8,9},{9,8},{10,11... | collective-permute-start | bytes 786440 | tf_op jit(solution)/shard_map/ppermute | solution.py:434
  48.1 1.2 %collective-permute-done.15 = bf16[128,1024]{1,0:T(8,128)(2,1)S(1)} collective-permute-done((bf16[128,1024]{1,0:T(8,128)(2,1)S(1)}, bf16[128,1024]{1,0:T(8,128)(2,1)S(1)}, u32[]{:S(2)}, u32[]{:S(2)}) %collective-permute-start.15) | collective-permute-done | bytes 262176 | tf_op jit(solution)/shard_map/ppermute | solution.py:434
  49.3 1.6 %collective-permute-start.16 = (bf16[128,1024]{1,0:T(8,128)(2,1)S(1)}, bf16[128,1024]{1,0:T(8,128)(2,1)S(1)}, u32[]{:S(2)}, u32[]{:S(2)}) collective-permute-start(bf16[128,1024]{1,0:T(8,128)(2,1)S(1)} %add_convert_fusion.2), channel_id=1, source_target_pairs={{0,2},{1,3},{2,0},{3,1},{4,6},{5,7},{6,4},{7,5},{8,10},{9,11},{10,... | collective-permute-start | bytes 786440 | tf_op jit(solution)/shard_map/ppermute | solution.py:437
  50.9 5.2 %conditional.5 = (bf16[128,1536]{1,0:T(8,128)(2,1)}) conditional(s32[]{:T(128)} %convert_element_type.48, () %tuple.56, (bf16[256,1024]{1,0:T(8,128)(2,1)S(1)}, bf16[1024,4096]{1,0:T(8,128)(2,1)}) %tuple.57), branch_computations={%region_2.3_spmd, %region_3.4_spmd} | conditional | flops 786433 | bytes 2752561 | solution.py:541
  50.9 2.6 %branch_1_fun.7 = (bf16[128,1536]{1,0:T(8,128)(2,1)S(1)}, bf16[128,1536]{1,0:T(8,128)(2,1)S(1)}) custom-call(bf16[256,1024]{1,0:T(8,128)(2,1)S(1)} %get-tuple-element.112.gated, bf16[1024,4096]{1,0:T(8,128)(2,1)} %get-tuple-element.113.weights), custom_call_target="tpu_custom_call" | custom-call | flops 1 | bytes 1 | tf_op jit(solution)/shard_map/cond/branch_1_fun/pallas_call | solution.py:372
  53.6 1.6 %collective-permute-done.3 = bf16[128,1536]{1,0:T(8,128)(2,1)S(1)} collective-permute-done((bf16[128,1536]{1,0:T(8,128)(2,1)S(1)}, bf16[128,1536]{1,0:T(8,128)(2,1)S(1)}, u32[]{:S(2)}, u32[]{:S(2)}) %collective-permute-start.3) | collective-permute-done | bytes 393248 | tf_op jit(solution)/shard_map/cond/branch_1_fun/ppermute | solution.py:434
  56.6 5.2 %conditional.6 = (bf16[128,1536]{1,0:T(8,128)(2,1)}) conditional(s32[]{:T(128)} %convert_element_type.48, () %tuple.53, (bf16[256,1024]{1,0:T(8,128)(2,1)S(1)}, bf16[1024,4096]{1,0:T(8,128)(2,1)}) %tuple.59), branch_computations={%region_4.5_spmd, %region_5.6_spmd} | conditional | flops 786433 | bytes 2752561 | solution.py:541
  56.6 2.6 %branch_1_fun.8 = (bf16[128,1536]{1,0:T(8,128)(2,1)S(1)}, bf16[128,1536]{1,0:T(8,128)(2,1)S(1)}) custom-call(bf16[256,1024]{1,0:T(8,128)(2,1)S(1)} %get-tuple-element.116.gated, bf16[1024,4096]{1,0:T(8,128)(2,1)} %get-tuple-element.117.weights), custom_call_target="tpu_custom_call" | custom-call | flops 1 | bytes 1 | tf_op jit(solution)/shard_map/cond/branch_1_fun/pallas_call | solution.py:372
  59.3 1.7 %collective-permute-done.4 = bf16[128,1536]{1,0:T(8,128)(2,1)S(1)} collective-permute-done((bf16[128,1536]{1,0:T(8,128)(2,1)S(1)}, bf16[128,1536]{1,0:T(8,128)(2,1)S(1)}, u32[]{:S(2)}, u32[]{:S(2)}) %collective-permute-start.4) | collective-permute-done | bytes 393248 | tf_op jit(solution)/shard_map/cond/branch_1_fun/ppermute | solution.py:434
  61.8 1.5 %collective-permute-start.17 = (bf16[128,1536]{1,0:T(8,128)(2,1)}, bf16[128,1536]{1,0:T(8,128)(2,1)S(1)}, u32[]{:S(2)}, u32[]{:S(2)}) collective-permute-start(bf16[128,1536]{1,0:T(8,128)(2,1)} %get-tuple-element.233), channel_id=1, source_target_pairs={{0,2},{1,3},{2,0},{3,1},{4,6},{5,7},{6,4},{7,5},{8,10},{9,11},{10,... | collective-permute-start | bytes 1179656 | tf_op jit(solution)/shard_map/ppermute | solution.py:437
  63.3 11.3 %conditional.7 = (f32[128,4096]{1,0:T(8,128)S(1)}) conditional(s32[]{:T(128)} %convert_element_type.48, () %tuple.50, (bf16[128,4096]{1,0:T(8,128)(2,1)}, s32[1]{0:T(128)}, bf16[288,1024]{1,0:T(8,128)(2,1)}, bf16[8192,128]{1,0:T(8,128)(2,1)}, bf16[128,1024]{1,0:T(8,128)(2,1)S(1)}, /*index=5*/bf16[3,128,4096]{2,1,0:T(8,128)(2,1)}, ...), branch_computations={%region_6.7_spmd, %region_7.8_spmd} | conditional | flops 2621441 | bytes 13631565 | solution.py:544
  63.4 8.1 %branch_1_fun.9 = (bf16[256,1024]{1,0:T(8,128)(2,1)}, bf16[128,4096]{1,0:T(8,128)(2,1)S(1)}, bf16[128,4096]{1,0:T(8,128)(2,1)S(1)}) custom-call(s32[1]{0:T(128)} %get-tuple-element.121.info, bf16[288,1024]{1,0:T(8,128)(2,1)} %get-tuple-element.122.prod, bf16[8192,128]{1,0:T(8,128)(2,1)} %get-tuple-element.123.toep, ...), custom_call_target="tpu_custom_call" | custom-call | flops 1 | bytes 1 | tf_op jit(solution)/shard_map/cond/branch_1_fun/pallas_call | solution.py:333
  71.6 2.6 %collective-permute-done.5 = bf16[128,4096]{1,0:T(8,128)(2,1)S(1)} collective-permute-done((bf16[128,4096]{1,0:T(8,128)(2,1)S(1)}, bf16[128,4096]{1,0:T(8,128)(2,1)S(1)}, u32[]{:S(2)}, u32[]{:S(2)}) %collective-permute-start.5) | collective-permute-done | bytes 1048608 | tf_op jit(solution)/shard_map/cond/branch_1_fun/ppermute | solution.py:434
  (36 shorter events, 8.6 us)
Async XLA Ops:
  1.7 7.3 %collective-permute-start.6 = (bf16[2,128,2048]{2,1,0:T(8,128)(2,1)S(1)}, bf16[2,128,2048]{2,1,0:T(8,128)(2,1)S(1)}, u32[]{:S(2)}, u32[]{:S(2)}) collective-permute-start(bf16[2,128,2048]{2,1,0:T(8,128)(2,1)S(1)} %get-tuple-element.177), channel_id=1, source_target_pairs={{0,1},{1,0},{2,3},{3,2},{4,5},{5,4},{6,7},{7,6},{8,9},{9,8},{10,11... | collective-permute-start | bytes 3145736 | tf_op jit(solution)/shard_map/ppermute | solution.py:434
  2.3 6.8 %collective-permute-start.7 = (bf16[3,8,2048]{2,1,0:T(8,128)(2,1)S(1)}, bf16[3,8,2048]{2,1,0:T(8,128)(2,1)S(1)}, u32[]{:S(2)}, u32[]{:S(2)}) collective-permute-start(bf16[3,8,2048]{2,1,0:T(8,128)(2,1)S(1)} %get-tuple-element.178), channel_id=1, source_target_pairs={{1,2},{3,4},{5,6},{7,8},{9,10},{11,12},{13,14},{15,16},{17,18},{19... | collective-permute-start | bytes 294920 | tf_op jit(solution)/shard_map/ppermute | solution.py:456
  2.9 6.2 %collective-permute-start.8 = (bf16[3,8,2048]{2,1,0:T(8,128)(2,1)S(1)}, bf16[3,8,2048]{2,1,0:T(8,128)(2,1)S(1)}, u32[]{:S(2)}, u32[]{:S(2)}) collective-permute-start(bf16[3,8,2048]{2,1,0:T(8,128)(2,1)S(1)} %get-tuple-element.179), channel_id=1, source_target_pairs={{1,3},{3,5},{5,7},{7,9},{9,11},{11,13},{13,15},{15,17},{17,19},{19... | collective-permute-start | bytes 294920 | tf_op jit(solution)/shard_map/ppermute | solution.py:456
  3.6 5.5 %collective-permute-start.9 = (f32[2,8,1024]{2,1,0:T(8,128)S(1)}, f32[2,8,1024]{2,1,0:T(8,128)S(1)}, u32[]{:S(2)}, u32[]{:S(2)}) collective-permute-start(f32[2,8,1024]{2,1,0:T(8,128)S(1)} %get-tuple-element.187.taps), channel_id=1, source_target_pairs={{0,2},{1,3},{2,0},{3,1},{4,6},{5,7},{6,4},{7,5},{8,10},{9,11},{10,... | collective-permute-start | bytes 196616 | tf_op jit(solution)/shard_map/ppermute | solution.py:437
  9.1 14.5 %collective-permute-start.11 = (bf16[128,1024]{1,0:T(8,128)(2,1)S(1)}, bf16[128,1024]{1,0:T(8,128)(2,1)S(1)}, u32[]{:S(2)}, u32[]{:S(2)}) collective-permute-start(bf16[128,1024]{1,0:T(8,128)(2,1)S(1)} %get-tuple-element.193), channel_id=1, source_target_pairs={{0,1},{1,0},{2,3},{3,2},{4,5},{5,4},{6,7},{7,6},{8,9},{9,8},{10,11... | collective-permute-start | bytes 786440 | tf_op jit(solution)/shard_map/ppermute | solution.py:434
  13.2 10.4 %collective-permute-start.12 = (bf16[128,1024]{1,0:T(8,128)(2,1)S(1)}, bf16[128,1024]{1,0:T(8,128)(2,1)S(1)}, u32[]{:S(2)}, u32[]{:S(2)}) collective-permute-start(bf16[128,1024]{1,0:T(8,128)(2,1)S(1)} %get-tuple-element.194), channel_id=1, source_target_pairs={{0,2},{1,3},{2,0},{3,1},{4,6},{5,7},{6,4},{7,5},{8,10},{9,11},{10,... | collective-permute-start | bytes 786440 | tf_op jit(solution)/shard_map/ppermute | solution.py:434
  18.1 5.5 %collective-permute-start.10 = (f32[24,1024]{1,0:T(8,128)S(1)}, f32[24,1024]{1,0:T(8,128)S(1)}, u32[]{:S(2)}, u32[]{:S(2)}) collective-permute-start(f32[24,1024]{1,0:T(8,128)S(1)} %get-tuple-element.190), channel_id=1, source_target_pairs={{0,2},{1,3},{2,0},{3,1},{4,6},{5,7},{6,4},{7,5},{8,10},{9,11},{10,... | collective-permute-start | bytes 294920 | tf_op jit(solution)/shard_map/ppermute | solution.py:434
  23.6 1.6 %copy-start.1 = (bf16[128,1024]{1,0:T(8,128)(2,1)}, bf16[128,1024]{1,0:T(8,128)(2,1)S(1)}, u32[]{:S(2)}) copy-start(bf16[128,1024]{1,0:T(8,128)(2,1)S(1)} %collective-permute-done.11) | copy-start | bytes 786436
  23.6 19.2 %collective-permute-start.13 = (bf16[288,1024]{1,0:T(8,128)(2,1)S(1)}, bf16[288,1024]{1,0:T(8,128)(2,1)S(1)}, u32[]{:S(2)}, u32[]{:S(2)}) collective-permute-start(bf16[288,1024]{1,0:T(8,128)(2,1)S(1)} %get-tuple-element.197), channel_id=1, source_target_pairs={{0,2},{1,3},{2,0},{3,1},{4,6},{5,7},{6,4},{7,5},{8,10},{9,11},{10,... | collective-permute-start | bytes 1769480 | tf_op jit(solution)/shard_map/ppermute | solution.py:434
  25.1 17.6 %collective-permute-start.14 = (bf16[128,1024]{1,0:T(8,128)(2,1)S(1)}, bf16[128,1024]{1,0:T(8,128)(2,1)S(1)}, u32[]{:S(2)}, u32[]{:S(2)}) collective-permute-start(bf16[128,1024]{1,0:T(8,128)(2,1)S(1)} %get-tuple-element.204), channel_id=1, source_target_pairs={{0,3},{1,2},{2,1},{3,0},{4,7},{5,6},{6,5},{7,4},{8,11},{9,10},{10,... | collective-permute-start | bytes 786440 | tf_op jit(solution)/shard_map/ppermute | solution.py:434
  25.2 4.9 %collective-permute-start = (f32[16,1024]{1,0:T(8,128)S(1)}, f32[16,1024]{1,0:T(8,128)S(1)}, u32[]{:S(2)}, u32[]{:S(2)}) collective-permute-start(f32[16,1024]{1,0:T(8,128)S(1)} %get-tuple-element.101), channel_id=1, source_target_pairs={{0,4},{4,0},{8,12},{12,8},{16,20},{20,16},{24,28},{28,24},{1,5},{5... | collective-permute-start | bytes 196616 | tf_op jit(solution)/shard_map/cond/branch_1_fun/ppermute | solution.py:440
  30.2 4.3 %collective-permute-start.1 = (f32[16,1024]{1,0:T(8,128)S(1)}, f32[16,1024]{1,0:T(8,128)S(1)}, u32[]{:S(2)}, u32[]{:S(2)}) collective-permute-start(f32[16,1024]{1,0:T(8,128)S(1)} %add_select_fusion.1), channel_id=1, source_target_pairs={{0,8},{4,12},{8,0},{12,4},{16,24},{20,28},{24,16},{28,20},{1,9},{5... | collective-permute-start | bytes 196616 | tf_op jit(solution)/shard_map/cond/branch_1_fun/ppermute | solution.py:440
  34.5 6.6 %collective-permute-start.2 = (f32[16,1024]{1,0:T(8,128)S(1)}, f32[16,1024]{1,0:T(8,128)S(1)}, u32[]{:S(2)}, u32[]{:S(2)}) collective-permute-start(f32[16,1024]{1,0:T(8,128)S(1)} %add_select_fusion), channel_id=1, source_target_pairs={{0,16},{4,20},{8,24},{12,28},{16,0},{20,4},{24,8},{28,12},{1,17},{... | collective-permute-start | bytes 196616 | tf_op jit(solution)/shard_map/cond/branch_1_fun/ppermute | solution.py:440
  47.2 2.0 %collective-permute-start.15 = (bf16[128,1024]{1,0:T(8,128)(2,1)S(1)}, bf16[128,1024]{1,0:T(8,128)(2,1)S(1)}, u32[]{:S(2)}, u32[]{:S(2)}) collective-permute-start(bf16[128,1024]{1,0:T(8,128)(2,1)S(1)} %get-tuple-element.209), channel_id=1, source_target_pairs={{0,1},{1,0},{2,3},{3,2},{4,5},{5,4},{6,7},{7,6},{8,9},{9,8},{10,11... | collective-permute-start | bytes 786440 | tf_op jit(solution)/shard_map/ppermute | solution.py:434
  49.3 12.5 %collective-permute-start.16 = (bf16[128,1024]{1,0:T(8,128)(2,1)S(1)}, bf16[128,1024]{1,0:T(8,128)(2,1)S(1)}, u32[]{:S(2)}, u32[]{:S(2)}) collective-permute-start(bf16[128,1024]{1,0:T(8,128)(2,1)S(1)} %add_convert_fusion.2), channel_id=1, source_target_pairs={{0,2},{1,3},{2,0},{3,1},{4,6},{5,7},{6,4},{7,5},{8,10},{9,11},{10,... | collective-permute-start | bytes 786440 | tf_op jit(solution)/shard_map/ppermute | solution.py:437
  53.5 1.8 %collective-permute-start.3 = (bf16[128,1536]{1,0:T(8,128)(2,1)S(1)}, bf16[128,1536]{1,0:T(8,128)(2,1)S(1)}, u32[]{:S(2)}, u32[]{:S(2)}) collective-permute-start(bf16[128,1536]{1,0:T(8,128)(2,1)S(1)} %get-tuple-element.115), channel_id=1, source_target_pairs={{0,1},{1,0},{2,3},{3,2},{4,5},{5,4},{6,7},{7,6},{8,9},{9,8},{10,11... | collective-permute-start | bytes 1179656 | tf_op jit(solution)/shard_map/cond/branch_1_fun/ppermute | solution.py:434
  56.1 7.2 %copy-start.2 = (bf16[128,1024]{1,0:T(8,128)(2,1)S(1)}, bf16[128,1024]{1,0:T(8,128)(2,1)}, u32[]{:S(2)}) copy-start(bf16[128,1024]{1,0:T(8,128)(2,1)} %copy-done.1) | copy-start | bytes 786436
  56.1 19.3 %collective-permute-start.18 = (bf16[128,1536]{1,0:T(8,128)(2,1)}, bf16[128,1536]{1,0:T(8,128)(2,1)S(1)}, u32[]{:S(2)}, u32[]{:S(2)}) collective-permute-start(bf16[128,1536]{1,0:T(8,128)(2,1)} %get-tuple-element.232), channel_id=1, source_target_pairs={{0,2},{1,3},{2,0},{3,1},{4,6},{5,7},{6,4},{7,5},{8,10},{9,11},{10,... | collective-permute-start | bytes 1179656 | tf_op jit(solution)/shard_map/ppermute | solution.py:437
  59.2 1.8 %collective-permute-start.4 = (bf16[128,1536]{1,0:T(8,128)(2,1)S(1)}, bf16[128,1536]{1,0:T(8,128)(2,1)S(1)}, u32[]{:S(2)}, u32[]{:S(2)}) collective-permute-start(bf16[128,1536]{1,0:T(8,128)(2,1)S(1)} %get-tuple-element.119), channel_id=1, source_target_pairs={{0,1},{1,0},{2,3},{3,2},{4,5},{5,4},{6,7},{7,6},{8,9},{9,8},{10,11... | collective-permute-start | bytes 1179656 | tf_op jit(solution)/shard_map/cond/branch_1_fun/ppermute | solution.py:434
  61.8 14.4 %collective-permute-start.17 = (bf16[128,1536]{1,0:T(8,128)(2,1)}, bf16[128,1536]{1,0:T(8,128)(2,1)S(1)}, u32[]{:S(2)}, u32[]{:S(2)}) collective-permute-start(bf16[128,1536]{1,0:T(8,128)(2,1)} %get-tuple-element.233), channel_id=1, source_target_pairs={{0,2},{1,3},{2,0},{3,1},{4,6},{5,7},{6,4},{7,5},{8,10},{9,11},{10,... | collective-permute-start | bytes 1179656 | tf_op jit(solution)/shard_map/ppermute | solution.py:437
  63.3 10.9 %copy-start = (bf16[128,4096]{1,0:T(8,128)(2,1)S(1)}, bf16[128,4096]{1,0:T(8,128)(2,1)}, u32[]{:S(2)}) copy-start(bf16[128,4096]{1,0:T(8,128)(2,1)} %get-tuple-element.221) | copy-start | bytes 3145732 | tf_op jit(solution)/shard_map/cond
  71.5 2.7 %collective-permute-start.5 = (bf16[128,4096]{1,0:T(8,128)(2,1)S(1)}, bf16[128,4096]{1,0:T(8,128)(2,1)S(1)}, u32[]{:S(2)}, u32[]{:S(2)}) collective-permute-start(bf16[128,4096]{1,0:T(8,128)(2,1)S(1)} %get-tuple-element.135), channel_id=1, source_target_pairs={{0,1},{1,0},{2,3},{3,2},{4,5},{5,4},{6,7},{7,6},{8,9},{9,8},{10,11... | collective-permute-start | bytes 3145736 | tf_op jit(solution)/shard_map/cond/branch_1_fun/ppermute | solution.py:434

commit v4 on v3

--- a/solution.py
+++ b/solution.py
@@ -1,5 +1,4 @@
 import functools
-import math
 
 import jax
 import jax.numpy as jnp
@@ -235,6 +234,38 @@
     )(rate_row, coef_row, *made)
 
 
+def local_kernel(prod, toep, out):
+    rows, width = out.shape[0] // 2, out.shape[1]
+    lane_group = iota((rows, LANES), 1) // GROUP_CH
+    for w in range(width // LANES):
+        lanes = slice(w * LANES, (w + 1) * LANES)
+        beside = jnp.concatenate([prod[:rows, lanes], prod[rows : 2 * rows, lanes]], axis=1)
+        local = dot(toep[w * PER_TILE * rows : (w + 1) * PER_TILE * rows, :], beside)
+        for i in range(2):
+            cols = slice(i * LANES, (i + 1) * LANES)
+            kept = local[:rows, cols]
+            for g in range(1, PER_TILE):
+                kept = jnp.where(lane_group == g, local[g * rows : (g + 1) * rows, cols], kept)
+            out[i * rows : (i + 1) * rows, lanes] = kept
+
+
+def local(prod, toep):
+    rows, width = toep.shape[1], prod.shape[1]
+    block = min(512, width)
+    return pl.pallas_call(
+        local_kernel,
+        grid=(width // block,),
+        in_specs=[
+            pl.BlockSpec((prod.shape[0], block), lambda i: (0, i)),
+            pl.BlockSpec((block // GROUP_CH * rows, rows), lambda i: (i, 0)),
+        ],
+        out_specs=pl.BlockSpec((2 * rows, block), lambda i: (0, i)),
+        out_shape=jax.ShapeDtypeStruct((2 * rows, width), F32),
+        compiler_params=pltpu.CompilerParams(vmem_limit_bytes=12 << 20),
+        cost_estimate=BRIEF,
+    )(prod, toep)
+
+
 def weight_copies(weights, first, held, sems):
     share = held.shape[2]
     return [
@@ -252,7 +283,7 @@
         mine[:, j * share : (j + 1) * share] = product[rows:].astype(BF16)
 
 
-def gate_kernel(d, chips, info, prod, toep, q0, q1, *rest):
+def gate_kernel(d, chips, info, long_in, second, q0, q1, *rest):
     states, rest = rest[:chips], rest[chips:]
     taps, before, wide_rates, rate_row, coef_row, weights, out, theirs, mine, pad, gated, held, sems = rest
     rows, width = q0.shape[-2:]
@@ -284,15 +315,16 @@
         state = before[:, lanes]
         for y in range(chips - 1):
             state = jnp.where(y < places[0] // 2, fade * state + by_chip[y][:ORDER], state)
-        inner = prod[2 * rows :, lanes].astype(F32)
+        inner = (long_in[2 * rows :, lanes] if d == 0 else second[:, lanes]).astype(F32)
         halfway = inner[:ORDER] + inner[ORDER:]
         halfway = jnp.exp(-rate * float(rows)) * state + halfway
         entering = [jnp.where(place % 2 == 0, state, halfway) for place in places]
         entering = [jnp.where(mask, jnp.concatenate([value] * PER_TILE, axis=0), 0.0) for value in entering]
         state_high, state_low = halves(jnp.concatenate(entering, axis=1))
         carried = dot(into_high, state_high) + dot(into_high, state_low) + dot(into_low, state_high)
-        beside = jnp.concatenate([prod[pl.ds(at, rows), lanes] for at in begins], axis=1)
-        local = dot(toep[w * PER_TILE * rows : (w + 1) * PER_TILE * rows, :], beside)
+        if d == 0:
+            beside = jnp.concatenate([long_in[pl.ds(at, rows), lanes] for at in begins], axis=1)
+            local = dot(second[w * PER_TILE * rows : (w + 1) * PER_TILE * rows, :], beside)
         tap = taps[0, :, lanes]
         for i, (q, place) in enumerate(zip((q0, q1), places)):
             other = (q1, q0)[i]
@@ -301,9 +333,13 @@
             pad[w, i, EDGE:, :] = (q[0, :, lanes] if d == 0 and i == 1 else q[:, lanes]).astype(F32)
             cols_of = slice(i * LANES, (i + 1) * LANES)
             for start in range(0, rows, step):
-                long = local[start : start + step, cols_of]
-                for g in range(1, PER_TILE):
-                    long = jnp.where(lane_group == g, local[g * rows + start : g * rows + start + step, cols_of], long)
+                if d > 0:
+                    long = long_in[pl.ds(begins[i] + start, step), lanes]
+                else:
+                    long = local[start : start + step, cols_of]
+                    for g in range(1, PER_TILE):
+                        at = g * rows + start
+                        long = jnp.where(lane_group == g, local[at : at + step, cols_of], long)
                 long = long + carried[start : start + step, cols_of]
                 value = convolve(pad.at[w, i], tap, start, step) * long
                 at = i * rows + start
@@ -335,7 +371,11 @@
         grid_spec=pltpu.PrefetchScalarGridSpec(
             num_scalar_prefetch=1,
             grid=(per,),
-            in_specs=[spec(2 * rows + 2 * ORDER), pl.BlockSpec((block // GROUP_CH * rows, rows), lambda i, info: (i, 0))]
+            in_specs=(
+                [spec(2 * rows), pl.BlockSpec((2 * ORDER, block), lambda i, info: (rows // ORDER, i))]
+                if d > 0
+                else [spec(2 * rows + 2 * ORDER), pl.BlockSpec((block // GROUP_CH * rows, rows), lambda i, info: (i, 0))]
+            )
             + [spec(rows), spec(rows) if d > 0 else pl.BlockSpec((1, rows, block), lambda i, info: (0, 0, info[0] * per + i))]
             + [spec(ORDER + EDGE)] * chips
             + [spec(3, TAPS), spec(ORDER), spec(ORDER), spec(1), spec(1)]
@@ -355,7 +395,7 @@
         ],
         compiler_params=pltpu.CompilerParams(vmem_limit_bytes=24 << 20),
         cost_estimate=BRIEF,
-    )(info, prod, toep, *pair, *states, taps, before, wide_rates, rate_row, coef_row, weights)
+    )(info, *((local(prod, toep), prod) if d > 0 else (prod, toep)), *pair, *states, taps, before, wide_rates, rate_row, coef_row, weights)
 
 
 def project_kernel(first, gated, weights, theirs, mine, held, sems):
@@ -380,43 +420,37 @@
     )(gated, weights)
 
 
-def finish_kernel(first, blocks, count, *rest):
-    bases, terms, (out, ready, sems) = rest[:blocks], rest[blocks : blocks + count], rest[-3:]
-    rows, cols = ready.shape
+def finish_kernel(parts, base, *rest):
+    terms, (out, ready, sems) = rest[:-3], rest[-3:]
+    rows = base.shape[0]
     step = min(32, rows)
+    each = len(terms) // len(parts)
     copies = []
     for i in range(rows // step):
         span = slice(i * step, (i + 1) * step)
-        total = jnp.concatenate([base[span, :] for base in bases], axis=1)
-        for term in terms:
-            total = total + term[span, :].astype(F32)
-        ready[span, :] = total.astype(BF16)
-        here = ready.at[pl.ds(i * step, step), :]
-        copies.append(pltpu.make_async_copy(here, out.at[pl.ds(i * step, step), pl.ds(first, cols)], sems.at[i]))
+        for p, (first, cols) in enumerate(parts):
+            total = base[span, first : first + cols]
+            for term in terms[p * each : (p + 1) * each]:
+                total = total + term[span, :].astype(F32)
+            ready[span, first : first + cols] = total.astype(BF16)
+        here = pl.ds(i * step, step)
+        copies.append(pltpu.make_async_copy(ready.at[here, :], out.at[here, :], sems.at[i]))
         copies[-1].start()
     for copy in copies:
         copy.wait()
 
 
-def finish(first, cols, base, terms, out):
+def finish(parts, base, terms):
     rows, depth = base.shape
-    before = [] if out is None else [out]
-    block = math.gcd(first, cols)
-    vmem = pl.BlockSpec(memory_space=pltpu.VMEM)
-    hbm = pl.BlockSpec(memory_space=pltpu.HBM)
     return pl.pallas_call(
-        functools.partial(finish_kernel, first, cols // block, len(terms)),
-        grid=(1,),
-        in_specs=[pl.BlockSpec((rows, block), lambda i, at=first // block + j: (0, at)) for j in range(cols // block)]
-        + [vmem] * len(terms)
-        + [hbm] * len(before),
-        out_specs=hbm,
+        functools.partial(finish_kernel, parts),
+        in_specs=[pl.BlockSpec(memory_space=pltpu.VMEM)] * (1 + len(terms)),
+        out_specs=pl.BlockSpec(memory_space=pltpu.HBM),
         out_shape=jax.ShapeDtypeStruct((rows, depth), BF16),
-        scratch_shapes=[pltpu.VMEM((rows, cols), BF16), pltpu.SemaphoreType.DMA((rows // min(32, rows),))],
-        input_output_aliases={cols // block + len(terms): 0} if before else {},
+        scratch_shapes=[pltpu.VMEM((rows, depth), BF16), pltpu.SemaphoreType.DMA((rows // min(32, rows),))],
         compiler_params=pltpu.CompilerParams(vmem_limit_bytes=12 << 20),
         cost_estimate=BRIEF,
-    )(*[base] * (cols // block), *terms, *before)
+    )(base, *terms)
 
 
 def body(chips, contexts, features, residual, short_weight, rates, residues, out_weight):
@@ -517,8 +551,10 @@
         return mine.astype(F32) + send(theirs, 1).astype(F32)
 
     def own(prod):
-        _, theirs, mine = gated_rows(0, prod, depth)
-        return residual.astype(F32) + summed(theirs, mine)
+        half = depth // 2
+        gated, *first_half = gated_rows(0, prod, half)
+        sums = [summed(*first_half), summed(*project(gated, weights, half, half))]
+        return residual.astype(F32) + jnp.concatenate(sums, axis=1)
 
     def no_own(prod):
         return jnp.zeros((rows, depth), F32)
@@ -542,10 +578,7 @@
     prods[0], wholes, arriving[0] = lax.optimization_barrier((prods[0], wholes, arriving[0]))
     arriving.append([send_back(whole, 2 * d) for d, whole in enumerate(wholes, 1)])
     base = lax.cond(always, own, no_own, prods[0])
-    out = None
-    for (first_col, cols), terms in zip(parts, arriving):
-        out = finish(first_col, cols, base, terms, out)
-    return out
+    return finish(parts, base, [term for terms in arriving for term in terms])
 
 
 def solution(mesh):

time: 77.2 us -> 76.2 us (0.987)
  starting transfers between devices: 23.4 us -> 22.3 us
  waiting for transfers between devices: 17.6 us -> 16.6 us
  Pallas kernels: 33.6 us -> 34.4 us
    pallas_call x2, Pallas kernels: 12.6 us -> 8.94 us  [gate(): pl.pallas_call(functools.partial(gate_kernel, d, chips), grid_spec=pltpu....]
    pallas_call x2 -> x3, Pallas kernels: 5.13 us -> 8.15 us  [project(): pl.pallas_call(functools.partial(project_kernel, first), in_specs=[vmem,...]
    ppermute x10 -> x11, waiting for transfers between devices: 9.59 us -> 7.13 us  [send(): lax.ppermute(value, 'tp', [(i, target(i, e, chips)) for i in range(steps)])]
    ppermute x4, waiting for transfers between devices: 2.25 us -> 3.71 us  [send_back(): lax.ppermute(value, 'tp', [(i, source(i, e, chips)) for i in range(steps)])]
    pallas_call x3 -> x2, Pallas kernels: 2.33 us -> 3.77 us  [the longest x1 2.73 us: local(): pl.pallas_call(local_kernel, grid=(width // block,), in_specs=[pl.BlockSp...]
    ppermute x4, starting transfers between devices: 6.85 us -> 6.06 us  [send_back(): lax.ppermute(value, 'tp', [(i, source(i, e, chips)) for i in range(steps)])]
    ppermute x10 -> x11, starting transfers between devices: 9.39 us -> 9.18 us  [send(): lax.ppermute(value, 'tp', [(i, target(i, e, chips)) for i in range(steps)])]
  transfers between devices with their start and end apart: 19 -> 20, of which waited for: 10 -> 10; matrix products, arithmetic and copies ran while one was open for 3% -> 3% of each run, Pallas kernels for 35% -> 37%
where the time goes in v4:
time: 76.2 us; the launch traced here: 75.9 us
  Pallas kernels  34.4 us (45%)
  starting transfers between devices  22.3 us (29%)
  waiting for transfers between devices  16.6 us (22%)
  other arithmetic  2.35 us (3%)
    ppermute x11, starting transfers between devices, send(): lax.ppermute(value, 'tp', [(i, target(i, e, chips)) for i in range(steps)])  9.18 us
    pallas_call x2, Pallas kernels, gate(): pl.pallas_call(functools.partial(gate_kernel, d, chips), grid_spec=pltpu....  8.94 us
    pallas_call x3, Pallas kernels, project(): pl.pallas_call(functools.partial(project_kernel, first), in_specs=[vmem,...  8.15 us
    pallas_call x2, Pallas kernels, front(): pl.pallas_call(front_kernel, grid_spec=pltpu.PrefetchScalarGridSpec(num_s...  7.46 us
    ppermute x11, waiting for transfers between devices, send(): lax.ppermute(value, 'tp', [(i, target(i, e, chips)) for i in range(steps)])  7.13 us
    ppermute x4, starting transfers between devices, send_back(): lax.ppermute(value, 'tp', [(i, source(i, e, chips)) for i in range(steps)])  6.06 us
    ppermute x3, starting transfers between devices, with_context(): return lax.ppermute(value, 'ctx', [(i, i ^ bit) for i in range(contexts)])  5.78 us
    ppermute x3, waiting for transfers between devices, with_context(): return lax.ppermute(value, 'ctx', [(i, i ^ bit) for i in range(contexts)])  5.75 us
  transfers between devices with their start and end apart: 20, of which 10 were waited for; matrix products, arithmetic and copies ran while one was open for 3% of the time, Pallas kernels for 37%

profile of v4, /device:TPU:0, one launch (start us, length us, event | category | flops | bytes accessed | tf_op | source)
XLA Modules:
  0.0 75.9 jit_solution(15952131356697709044)
XLA Ops:
  0.0 1.7 %shard_map.65 = (bf16[2,128,2048]{2,1,0:T(8,128)(2,1)S(1)}, bf16[3,8,2048]{2,1,0:T(8,128)(2,1)S(1)}, bf16[3,8,2048]{2,1,0:T(8,128)(2,1)S(1)}, f32[2,8,1024]{2,1,...) custom-call(s32[1]{0:T(128)} %bitcast.info, ...), custom_call_target="tpu_custom_call" | custom-call | flops 1 | bytes 1 | tf_op jit(solution)/shard_map/pallas_call | solution.py:114
  3.6 3.2 %collective-permute-start.10 = (f32[2,8,1024]{2,1,0:T(8,128)S(1)}, f32[2,8,1024]{2,1,0:T(8,128)S(1)}, u32[]{:S(2)}, u32[]{:S(2)}) collective-permute-start(f32[2,8,1024]{2,1,0:T(8,128)S(1)} %get-tuple-element.190.taps), channel_id=1, source_target_pairs={{0,2},{1,3},{2,0},{3,1},{4,6},{5,7},{6,4},{7,5},{8,10},{9,11},{10,... | collective-permute-start | bytes 196616 | tf_op jit(solution)/shard_map/ppermute | solution.py:471
  6.8 2.2 %collective-permute-done.10.taps = f32[2,8,1024]{2,1,0:T(8,128)S(1)} collective-permute-done((f32[2,8,1024]{2,1,0:T(8,128)S(1)}, f32[2,8,1024]{2,1,0:T(8,128)S(1)}, u32[]{:S(2)}, u32[]{:S(2)}) %collective-permute-start.10) | collective-permute-done | bytes 65568 | tf_op jit(solution)/shard_map/ppermute | solution.py:471
  9.1 4.1 %collective-permute-start.12 = (bf16[128,1024]{1,0:T(8,128)(2,1)S(1)}, bf16[128,1024]{1,0:T(8,128)(2,1)S(1)}, u32[]{:S(2)}, u32[]{:S(2)}) collective-permute-start(bf16[128,1024]{1,0:T(8,128)(2,1)S(1)} %get-tuple-element.196), channel_id=1, source_target_pairs={{0,1},{1,0},{2,3},{3,2},{4,5},{5,4},{6,7},{7,6},{8,9},{9,8},{10,11... | collective-permute-start | bytes 786440 | tf_op jit(solution)/shard_map/ppermute | solution.py:468
  13.2 1.5 %collective-permute-start.13 = (bf16[128,1024]{1,0:T(8,128)(2,1)S(1)}, bf16[128,1024]{1,0:T(8,128)(2,1)S(1)}, u32[]{:S(2)}, u32[]{:S(2)}) collective-permute-start(bf16[128,1024]{1,0:T(8,128)(2,1)S(1)} %get-tuple-element.197), channel_id=1, source_target_pairs={{0,2},{1,3},{2,0},{3,1},{4,6},{5,7},{6,4},{7,5},{8,10},{9,11},{10,... | collective-permute-start | bytes 786440 | tf_op jit(solution)/shard_map/ppermute | solution.py:468
  14.7 3.4 %shard_map.67 = (bf16[288,1024]{1,0:T(8,128)(2,1)S(1)}, f32[24,1024]{1,0:T(8,128)S(1)}) custom-call(s32[1]{0:T(128)} %bitcast.info, bf16[3,128,4096]{2,1,0:T(8,128)(2,1)} %bitcast.6, bf16[3,128,4096]{2,1,0:T(8,128)(2,1)} %bitcast.7, bf16[2,128,2048]{2,1,0:T(8,128)(2,1)S(1)} %collective-permute-done.7.kv_in, ...), custom_call_target="tpu_custom_call" | custom-call | flops 1 | bytes 1 | tf_op jit(solution)/shard_map/pallas_call | solution.py:190
  18.7 4.0 %shard_map.66 = (bf16[288,1024]{1,0:T(8,128)(2,1)}, f32[24,1024]{1,0:T(8,128)S(1)}) custom-call(s32[1]{0:T(128)} %bitcast.info, bf16[3,128,4096]{2,1,0:T(8,128)(2,1)} %bitcast.8, bf16[3,128,4096]{2,1,0:T(8,128)(2,1)} %bitcast.9, bf16[2,128,2048]{2,1,0:T(8,128)(2,1)S(1)} %collective-permute-done.7.kv_in, ...), custom_call_target="tpu_custom_call" | custom-call | flops 1 | bytes 1 | tf_op jit(solution)/shard_map/pallas_call | solution.py:190
  23.6 1.6 %collective-permute-start.14 = (bf16[288,1024]{1,0:T(8,128)(2,1)S(1)}, bf16[288,1024]{1,0:T(8,128)(2,1)S(1)}, u32[]{:S(2)}, u32[]{:S(2)}) collective-permute-start(bf16[288,1024]{1,0:T(8,128)(2,1)S(1)} %get-tuple-element.200), channel_id=1, source_target_pairs={{0,2},{1,3},{2,0},{3,1},{4,6},{5,7},{6,4},{7,5},{8,10},{9,11},{10,... | collective-permute-start | bytes 1769480 | tf_op jit(solution)/shard_map/ppermute | solution.py:468
  25.2 16.0 %conditional.4 = (f32[16,1024]{1,0:T(8,128)S(1)}, bf16[8192,128]{1,0:T(8,128)(2,1)}) conditional(s32[]{:T(128)} %convert_element_type.54, f32[16,1024]{1,0:T(8,128)S(1)} %get-tuple-element.201.rest_4_, (f32[16,1024]{1,0:T(8,128)S(1)}, s32[]{:T(128)}, s32[]{:T(128)}, f32[24,1024]{1,0:T(8,128)S(1)}, f32[24,1024]{1,0:T(8,128)S(1)}, /*index=5*/s32[]{:T(128)}, ...), branch_computations={%region_0.1_spmd, %region_1.2_spmd} | conditional | flops 540727 | bytes 2359982 | solution.py:539
  25.2 1.6 %collective-permute-start = (f32[16,1024]{1,0:T(8,128)S(1)}, f32[16,1024]{1,0:T(8,128)S(1)}, u32[]{:S(2)}, u32[]{:S(2)}) collective-permute-start(f32[16,1024]{1,0:T(8,128)S(1)} %get-tuple-element.101), channel_id=1, source_target_pairs={{0,4},{4,0},{8,12},{12,8},{16,20},{20,16},{24,28},{28,24},{1,5},{5... | collective-permute-start | bytes 196616 | tf_op jit(solution)/shard_map/cond/branch_1_fun/ppermute | solution.py:474
  26.8 2.2 %branch_1_fun.6.rest_0_ = bf16[8192,128]{1,0:T(8,128)(2,1)} custom-call(f32[1,1024]{1,0:T(1,128)S(1)} %get-tuple-element.104.rate_row, f32[1,1024]{1,0:T(1,128)S(1)} %get-tuple-element.105.coef_row), custom_call_target="tpu_custom_call" | custom-call | flops 1 | bytes 1 | tf_op jit(solution)/shard_map/cond/branch_1_fun/pallas_call | solution.py:226
  29.0 1.1 %collective-permute-done = f32[16,1024]{1,0:T(8,128)S(1)} collective-permute-done((f32[16,1024]{1,0:T(8,128)S(1)}, f32[16,1024]{1,0:T(8,128)S(1)}, u32[]{:S(2)}, u32[]{:S(2)}) %collective-permute-start) | collective-permute-done | bytes 65568 | tf_op jit(solution)/shard_map/cond/branch_1_fun/ppermute | solution.py:474
  30.2 1.4 %collective-permute-start.1 = (f32[16,1024]{1,0:T(8,128)S(1)}, f32[16,1024]{1,0:T(8,128)S(1)}, u32[]{:S(2)}, u32[]{:S(2)}) collective-permute-start(f32[16,1024]{1,0:T(8,128)S(1)} %add_select_fusion.1), channel_id=1, source_target_pairs={{0,8},{4,12},{8,0},{12,4},{16,24},{20,28},{24,16},{28,20},{1,9},{5... | collective-permute-start | bytes 196616 | tf_op jit(solution)/shard_map/cond/branch_1_fun/ppermute | solution.py:474
  31.6 2.2 %branch_1_fun.7 = bf16[8192,128]{1,0:T(8,128)(2,1)} custom-call(f32[1,1024]{1,0:T(1,128)S(1)} %get-tuple-element.104.rate_row, f32[1,1024]{1,0:T(1,128)S(1)} %get-tuple-element.105.coef_row, bf16[8192,128]{1,0:T(8,128)(2,1)} %branch_1_fun.6.rest_0_), custom_call_target="tpu_custom_call", output_to_operand_aliasing={{}: (2, {})} | custom-call | flops 1 | bytes 1 | tf_op jit(solution)/shard_map/cond/branch_1_fun/pallas_call | solution.py:226
  34.5 2.8 %collective-permute-start.2 = (f32[16,1024]{1,0:T(8,128)S(1)}, f32[16,1024]{1,0:T(8,128)S(1)}, u32[]{:S(2)}, u32[]{:S(2)}) collective-permute-start(f32[16,1024]{1,0:T(8,128)S(1)} %add_select_fusion), channel_id=1, source_target_pairs={{0,16},{4,20},{8,24},{12,28},{16,0},{20,4},{24,8},{28,12},{1,17},{... | collective-permute-start | bytes 196616 | tf_op jit(solution)/shard_map/cond/branch_1_fun/ppermute | solution.py:474
  37.3 3.9 %collective-permute-done.2 = f32[16,1024]{1,0:T(8,128)S(1)} collective-permute-done((f32[16,1024]{1,0:T(8,128)S(1)}, f32[16,1024]{1,0:T(8,128)S(1)}, u32[]{:S(2)}, u32[]{:S(2)}) %collective-permute-start.2) | collective-permute-done | bytes 65568 | tf_op jit(solution)/shard_map/cond/branch_1_fun/ppermute | solution.py:474
  41.2 2.7 %shard_map.68.long_in = f32[256,1024]{1,0:T(8,128)S(1)} custom-call(bf16[288,1024]{1,0:T(8,128)(2,1)S(1)} %collective-permute-done.14.prod.second, bf16[8192,128]{1,0:T(8,128)(2,1)} %get-tuple-element.206.toep), custom_call_target="tpu_custom_call" | custom-call | flops 1 | bytes 1 | tf_op jit(solution)/shard_map/pallas_call | solution.py:255
  43.9 3.4 %shard_map.69 = (bf16[256,1024]{1,0:T(8,128)(2,1)S(1)}, bf16[128,1024]{1,0:T(8,128)(2,1)S(1)}, bf16[128,1024]{1,0:T(8,128)(2,1)S(1)}) custom-call(s32[1]{0:T(128)} %bitcast.info, f32[256,1024]{1,0:T(8,128)S(1)} %shard_map.68.long_in, bf16[288,1024]{1,0:T(8,128)(2,1)S(1)} %collective-permute-done.14.prod.second, ...), custom_call_target="tpu_custom_call" | custom-call | flops 1 | bytes 1 | tf_op jit(solution)/shard_map/pallas_call | solution.py:369
  47.5 1.5 %collective-permute-done.16 = bf16[128,1024]{1,0:T(8,128)(2,1)S(1)} collective-permute-done((bf16[128,1024]{1,0:T(8,128)(2,1)S(1)}, bf16[128,1024]{1,0:T(8,128)(2,1)S(1)}, u32[]{:S(2)}, u32[]{:S(2)}) %collective-permute-start.16) | collective-permute-done | bytes 262176 | tf_op jit(solution)/shard_map/ppermute | solution.py:468
  49.8 5.2 %conditional.5 = (bf16[128,1536]{1,0:T(8,128)(2,1)}) conditional(s32[]{:T(128)} %convert_element_type.54, () %tuple.56, (bf16[256,1024]{1,0:T(8,128)(2,1)S(1)}, bf16[1024,4096]{1,0:T(8,128)(2,1)}) %tuple.57), branch_computations={%region_2.3_spmd, %region_3.4_spmd} | conditional | flops 786433 | bytes 2752561 | solution.py:577
  49.8 2.6 %branch_1_fun.8 = (bf16[128,1536]{1,0:T(8,128)(2,1)S(1)}, bf16[128,1536]{1,0:T(8,128)(2,1)S(1)}) custom-call(bf16[256,1024]{1,0:T(8,128)(2,1)S(1)} %get-tuple-element.112.gated, bf16[1024,4096]{1,0:T(8,128)(2,1)} %get-tuple-element.113.weights), custom_call_target="tpu_custom_call" | custom-call | flops 1 | bytes 1 | tf_op jit(solution)/shard_map/cond/branch_1_fun/pallas_call | solution.py:412
  52.6 1.6 %collective-permute-done.3 = bf16[128,1536]{1,0:T(8,128)(2,1)S(1)} collective-permute-done((bf16[128,1536]{1,0:T(8,128)(2,1)S(1)}, bf16[128,1536]{1,0:T(8,128)(2,1)S(1)}, u32[]{:S(2)}, u32[]{:S(2)}) %collective-permute-start.3) | collective-permute-done | bytes 393248 | tf_op jit(solution)/shard_map/cond/branch_1_fun/ppermute | solution.py:468
  55.1 1.3 %collective-permute-start.18 = (bf16[128,1536]{1,0:T(8,128)(2,1)}, bf16[128,1536]{1,0:T(8,128)(2,1)S(1)}, u32[]{:S(2)}, u32[]{:S(2)}) collective-permute-start(bf16[128,1536]{1,0:T(8,128)(2,1)} %get-tuple-element.235), channel_id=1, source_target_pairs={{0,2},{1,3},{2,0},{3,1},{4,6},{5,7},{6,4},{7,5},{8,10},{9,11},{10,... | collective-permute-start | bytes 1179656 | tf_op jit(solution)/shard_map/ppermute | solution.py:471
  56.4 5.2 %conditional.6 = (bf16[128,1536]{1,0:T(8,128)(2,1)}) conditional(s32[]{:T(128)} %convert_element_type.54, () %tuple.53, (bf16[256,1024]{1,0:T(8,128)(2,1)S(1)}, bf16[1024,4096]{1,0:T(8,128)(2,1)}) %tuple.59), branch_computations={%region_4.5_spmd, %region_5.6_spmd} | conditional | flops 786433 | bytes 2752561 | solution.py:577
  56.4 2.6 %branch_1_fun.9 = (bf16[128,1536]{1,0:T(8,128)(2,1)S(1)}, bf16[128,1536]{1,0:T(8,128)(2,1)S(1)}) custom-call(bf16[256,1024]{1,0:T(8,128)(2,1)S(1)} %get-tuple-element.116.gated, bf16[1024,4096]{1,0:T(8,128)(2,1)} %get-tuple-element.117.weights), custom_call_target="tpu_custom_call" | custom-call | flops 1 | bytes 1 | tf_op jit(solution)/shard_map/cond/branch_1_fun/pallas_call | solution.py:412
  59.0 1.7 %collective-permute-done.4 = bf16[128,1536]{1,0:T(8,128)(2,1)S(1)} collective-permute-done((bf16[128,1536]{1,0:T(8,128)(2,1)S(1)}, bf16[128,1536]{1,0:T(8,128)(2,1)S(1)}, u32[]{:S(2)}, u32[]{:S(2)}) %collective-permute-start.4) | collective-permute-done | bytes 393248 | tf_op jit(solution)/shard_map/cond/branch_1_fun/ppermute | solution.py:468
  62.3 11.1 %conditional.7 = (f32[128,4096]{1,0:T(8,128)S(1)}) conditional(s32[]{:T(128)} %convert_element_type.54, () %tuple.50, (bf16[128,4096]{1,0:T(8,128)(2,1)}, s32[1]{0:T(128)}, bf16[288,1024]{1,0:T(8,128)(2,1)}, bf16[8192,128]{1,0:T(8,128)(2,1)}, bf16[128,1024]{1,0:T(8,128)(2,1)}, /*index=5*/bf16[3,128,4096]{2,1,0:T(8,128)(2,1)}, ...), branch_computations={%region_6.7_spmd, %region_7.8_spmd} | conditional | flops 3145730 | bytes 17825910 | solution.py:580
  62.3 5.5 %branch_1_fun.10 = (bf16[256,1024]{1,0:T(8,128)(2,1)S(1)}, bf16[128,2048]{1,0:T(8,128)(2,1)S(1)}, bf16[128,2048]{1,0:T(8,128)(2,1)S(1)}) custom-call(s32[1]{0:T(128)} %get-tuple-element.121.info, bf16[288,1024]{1,0:T(8,128)(2,1)} %get-tuple-element.122.long_in, bf16[8192,128]{1,0:T(8,128)(2,1)} %get-tuple-element.123.second, ...), custom_call_target="tpu_custom_call" | custom-call | flops 1 | bytes 1 | tf_op jit(solution)/shard_map/cond/branch_1_fun/pallas_call | solution.py:369
  67.9 3.0 %branch_1_fun.11 = (bf16[128,2048]{1,0:T(8,128)(2,1)S(1)}, bf16[128,2048]{1,0:T(8,128)(2,1)S(1)}) custom-call(bf16[256,1024]{1,0:T(8,128)(2,1)S(1)} %get-tuple-element.136.gated, bf16[1024,4096]{1,0:T(8,128)(2,1)} %get-tuple-element.133.rest_7_.weights), custom_call_target="tpu_custom_call" | custom-call | flops 1 | bytes 1 | tf_op jit(solution)/shard_map/cond/branch_1_fun/pallas_call | solution.py:412
  71.6 1.4 %collective-permute-done.6 = bf16[128,2048]{1,0:T(8,128)(2,1)S(1)} collective-permute-done((bf16[128,2048]{1,0:T(8,128)(2,1)S(1)}, bf16[128,2048]{1,0:T(8,128)(2,1)S(1)}, u32[]{:S(2)}, u32[]{:S(2)}) %collective-permute-start.6) | collective-permute-done | bytes 524320 | tf_op jit(solution)/shard_map/cond/branch_1_fun/ppermute | solution.py:468
  73.4 1.5 %collective-permute-done.19.rest_2_ = bf16[128,1536]{1,0:T(8,128)(2,1)S(1)} collective-permute-done((bf16[128,1536]{1,0:T(8,128)(2,1)}, bf16[128,1536]{1,0:T(8,128)(2,1)S(1)}, u32[]{:S(2)}, u32[]{:S(2)}) %collective-permute-start.19) | collective-permute-done | bytes 393248 | tf_op jit(solution)/shard_map/ppermute | solution.py:471
  74.9 1.0 %shard_map.70 = bf16[128,4096]{1,0:T(8,128)(2,1)} custom-call(f32[128,4096]{1,0:T(8,128)S(1)} %get-tuple-element.237.base, bf16[128,1024]{1,0:T(8,128)(2,1)S(1)} %collective-permute-done.17.rest_0_, bf16[128,1536]{1,0:T(8,128)(2,1)S(1)} %collective-permute-done.18.rest_1_, bf16[128,1536]{1,0:T(8,128)(2,1)S(1)} %collective-permute-done.19.rest_2_), custom_call_target="tpu_custom_call" | custom-call | flops 1 | bytes 1 | tf_op jit(solution)/shard_map/pallas_call | solution.py:445
  (38 shorter events, 8.8 us)
Async XLA Ops:
  1.7 7.3 %collective-permute-start.7 = (bf16[2,128,2048]{2,1,0:T(8,128)(2,1)S(1)}, bf16[2,128,2048]{2,1,0:T(8,128)(2,1)S(1)}, u32[]{:S(2)}, u32[]{:S(2)}) collective-permute-start(bf16[2,128,2048]{2,1,0:T(8,128)(2,1)S(1)} %get-tuple-element.180), channel_id=1, source_target_pairs={{0,1},{1,0},{2,3},{3,2},{4,5},{5,4},{6,7},{7,6},{8,9},{9,8},{10,11... | collective-permute-start | bytes 3145736 | tf_op jit(solution)/shard_map/ppermute | solution.py:468
  2.3 6.8 %collective-permute-start.8 = (bf16[3,8,2048]{2,1,0:T(8,128)(2,1)S(1)}, bf16[3,8,2048]{2,1,0:T(8,128)(2,1)S(1)}, u32[]{:S(2)}, u32[]{:S(2)}) collective-permute-start(bf16[3,8,2048]{2,1,0:T(8,128)(2,1)S(1)} %get-tuple-element.181), channel_id=1, source_target_pairs={{1,2},{3,4},{5,6},{7,8},{9,10},{11,12},{13,14},{15,16},{17,18},{19... | collective-permute-start | bytes 294920 | tf_op jit(solution)/shard_map/ppermute | solution.py:490
  2.9 6.2 %collective-permute-start.9 = (bf16[3,8,2048]{2,1,0:T(8,128)(2,1)S(1)}, bf16[3,8,2048]{2,1,0:T(8,128)(2,1)S(1)}, u32[]{:S(2)}, u32[]{:S(2)}) collective-permute-start(bf16[3,8,2048]{2,1,0:T(8,128)(2,1)S(1)} %get-tuple-element.182), channel_id=1, source_target_pairs={{1,3},{3,5},{5,7},{7,9},{9,11},{11,13},{13,15},{15,17},{17,19},{19... | collective-permute-start | bytes 294920 | tf_op jit(solution)/shard_map/ppermute | solution.py:490
  3.6 5.5 %collective-permute-start.10 = (f32[2,8,1024]{2,1,0:T(8,128)S(1)}, f32[2,8,1024]{2,1,0:T(8,128)S(1)}, u32[]{:S(2)}, u32[]{:S(2)}) collective-permute-start(f32[2,8,1024]{2,1,0:T(8,128)S(1)} %get-tuple-element.190.taps), channel_id=1, source_target_pairs={{0,2},{1,3},{2,0},{3,1},{4,6},{5,7},{6,4},{7,5},{8,10},{9,11},{10,... | collective-permute-start | bytes 196616 | tf_op jit(solution)/shard_map/ppermute | solution.py:471
  9.1 14.5 %collective-permute-start.12 = (bf16[128,1024]{1,0:T(8,128)(2,1)S(1)}, bf16[128,1024]{1,0:T(8,128)(2,1)S(1)}, u32[]{:S(2)}, u32[]{:S(2)}) collective-permute-start(bf16[128,1024]{1,0:T(8,128)(2,1)S(1)} %get-tuple-element.196), channel_id=1, source_target_pairs={{0,1},{1,0},{2,3},{3,2},{4,5},{5,4},{6,7},{7,6},{8,9},{9,8},{10,11... | collective-permute-start | bytes 786440 | tf_op jit(solution)/shard_map/ppermute | solution.py:468
  13.2 10.4 %collective-permute-start.13 = (bf16[128,1024]{1,0:T(8,128)(2,1)S(1)}, bf16[128,1024]{1,0:T(8,128)(2,1)S(1)}, u32[]{:S(2)}, u32[]{:S(2)}) collective-permute-start(bf16[128,1024]{1,0:T(8,128)(2,1)S(1)} %get-tuple-element.197), channel_id=1, source_target_pairs={{0,2},{1,3},{2,0},{3,1},{4,6},{5,7},{6,4},{7,5},{8,10},{9,11},{10,... | collective-permute-start | bytes 786440 | tf_op jit(solution)/shard_map/ppermute | solution.py:468
  18.1 5.5 %collective-permute-start.11 = (f32[24,1024]{1,0:T(8,128)S(1)}, f32[24,1024]{1,0:T(8,128)S(1)}, u32[]{:S(2)}, u32[]{:S(2)}) collective-permute-start(f32[24,1024]{1,0:T(8,128)S(1)} %get-tuple-element.193), channel_id=1, source_target_pairs={{0,2},{1,3},{2,0},{3,1},{4,6},{5,7},{6,4},{7,5},{8,10},{9,11},{10,... | collective-permute-start | bytes 294920 | tf_op jit(solution)/shard_map/ppermute | solution.py:468
  23.6 1.6 %copy-start.1 = (bf16[128,1024]{1,0:T(8,128)(2,1)}, bf16[128,1024]{1,0:T(8,128)(2,1)S(1)}, u32[]{:S(2)}) copy-start(bf16[128,1024]{1,0:T(8,128)(2,1)S(1)} %collective-permute-done.12) | copy-start | bytes 786436
  23.6 17.6 %collective-permute-start.14 = (bf16[288,1024]{1,0:T(8,128)(2,1)S(1)}, bf16[288,1024]{1,0:T(8,128)(2,1)S(1)}, u32[]{:S(2)}, u32[]{:S(2)}) collective-permute-start(bf16[288,1024]{1,0:T(8,128)(2,1)S(1)} %get-tuple-element.200), channel_id=1, source_target_pairs={{0,2},{1,3},{2,0},{3,1},{4,6},{5,7},{6,4},{7,5},{8,10},{9,11},{10,... | collective-permute-start | bytes 1769480 | tf_op jit(solution)/shard_map/ppermute | solution.py:468
  25.1 18.8 %collective-permute-start.15 = (bf16[128,1024]{1,0:T(8,128)(2,1)S(1)}, bf16[128,1024]{1,0:T(8,128)(2,1)S(1)}, u32[]{:S(2)}, u32[]{:S(2)}) collective-permute-start(bf16[128,1024]{1,0:T(8,128)(2,1)S(1)} %get-tuple-element.207), channel_id=1, source_target_pairs={{0,3},{1,2},{2,1},{3,0},{4,7},{5,6},{6,5},{7,4},{8,11},{9,10},{10,... | collective-permute-start | bytes 786440 | tf_op jit(solution)/shard_map/ppermute | solution.py:468
  25.2 4.9 %collective-permute-start = (f32[16,1024]{1,0:T(8,128)S(1)}, f32[16,1024]{1,0:T(8,128)S(1)}, u32[]{:S(2)}, u32[]{:S(2)}) collective-permute-start(f32[16,1024]{1,0:T(8,128)S(1)} %get-tuple-element.101), channel_id=1, source_target_pairs={{0,4},{4,0},{8,12},{12,8},{16,20},{20,16},{24,28},{28,24},{1,5},{5... | collective-permute-start | bytes 196616 | tf_op jit(solution)/shard_map/cond/branch_1_fun/ppermute | solution.py:474
  30.2 4.3 %collective-permute-start.1 = (f32[16,1024]{1,0:T(8,128)S(1)}, f32[16,1024]{1,0:T(8,128)S(1)}, u32[]{:S(2)}, u32[]{:S(2)}) collective-permute-start(f32[16,1024]{1,0:T(8,128)S(1)} %add_select_fusion.1), channel_id=1, source_target_pairs={{0,8},{4,12},{8,0},{12,4},{16,24},{20,28},{24,16},{28,20},{1,9},{5... | collective-permute-start | bytes 196616 | tf_op jit(solution)/shard_map/cond/branch_1_fun/ppermute | solution.py:474
  34.5 6.6 %collective-permute-start.2 = (f32[16,1024]{1,0:T(8,128)S(1)}, f32[16,1024]{1,0:T(8,128)S(1)}, u32[]{:S(2)}, u32[]{:S(2)}) collective-permute-start(f32[16,1024]{1,0:T(8,128)S(1)} %add_select_fusion), channel_id=1, source_target_pairs={{0,16},{4,20},{8,24},{12,28},{16,0},{20,4},{24,8},{28,12},{1,17},{... | collective-permute-start | bytes 196616 | tf_op jit(solution)/shard_map/cond/branch_1_fun/ppermute | solution.py:474
  47.4 1.6 %collective-permute-start.16 = (bf16[128,1024]{1,0:T(8,128)(2,1)S(1)}, bf16[128,1024]{1,0:T(8,128)(2,1)S(1)}, u32[]{:S(2)}, u32[]{:S(2)}) collective-permute-start(bf16[128,1024]{1,0:T(8,128)(2,1)S(1)} %get-tuple-element.212), channel_id=1, source_target_pairs={{0,1},{1,0},{2,3},{3,2},{4,5},{5,4},{6,7},{7,6},{8,9},{9,8},{10,11... | collective-permute-start | bytes 786440 | tf_op jit(solution)/shard_map/ppermute | solution.py:468
  49.0 12.5 %collective-permute-start.17 = (bf16[128,1024]{1,0:T(8,128)(2,1)S(1)}, bf16[128,1024]{1,0:T(8,128)(2,1)S(1)}, u32[]{:S(2)}, u32[]{:S(2)}) collective-permute-start(bf16[128,1024]{1,0:T(8,128)(2,1)S(1)} %add_convert_fusion.2), channel_id=1, source_target_pairs={{0,2},{1,3},{2,0},{3,1},{4,6},{5,7},{6,4},{7,5},{8,10},{9,11},{10,... | collective-permute-start | bytes 786440 | tf_op jit(solution)/shard_map/ppermute | solution.py:471
  52.4 1.8 %collective-permute-start.3 = (bf16[128,1536]{1,0:T(8,128)(2,1)S(1)}, bf16[128,1536]{1,0:T(8,128)(2,1)S(1)}, u32[]{:S(2)}, u32[]{:S(2)}) collective-permute-start(bf16[128,1536]{1,0:T(8,128)(2,1)S(1)} %get-tuple-element.115), channel_id=1, source_target_pairs={{0,1},{1,0},{2,3},{3,2},{4,5},{5,4},{6,7},{7,6},{8,9},{9,8},{10,11... | collective-permute-start | bytes 1179656 | tf_op jit(solution)/shard_map/cond/branch_1_fun/ppermute | solution.py:468
  55.1 18.3 %collective-permute-start.18 = (bf16[128,1536]{1,0:T(8,128)(2,1)}, bf16[128,1536]{1,0:T(8,128)(2,1)S(1)}, u32[]{:S(2)}, u32[]{:S(2)}) collective-permute-start(bf16[128,1536]{1,0:T(8,128)(2,1)} %get-tuple-element.235), channel_id=1, source_target_pairs={{0,2},{1,3},{2,0},{3,1},{4,6},{5,7},{6,4},{7,5},{8,10},{9,11},{10,... | collective-permute-start | bytes 1179656 | tf_op jit(solution)/shard_map/ppermute | solution.py:471
  58.9 1.8 %collective-permute-start.4 = (bf16[128,1536]{1,0:T(8,128)(2,1)S(1)}, bf16[128,1536]{1,0:T(8,128)(2,1)S(1)}, u32[]{:S(2)}, u32[]{:S(2)}) collective-permute-start(bf16[128,1536]{1,0:T(8,128)(2,1)S(1)} %get-tuple-element.119), channel_id=1, source_target_pairs={{0,1},{1,0},{2,3},{3,2},{4,5},{5,4},{6,7},{7,6},{8,9},{9,8},{10,11... | collective-permute-start | bytes 1179656 | tf_op jit(solution)/shard_map/cond/branch_1_fun/ppermute | solution.py:468
  61.6 13.3 %collective-permute-start.19 = (bf16[128,1536]{1,0:T(8,128)(2,1)}, bf16[128,1536]{1,0:T(8,128)(2,1)S(1)}, u32[]{:S(2)}, u32[]{:S(2)}) collective-permute-start(bf16[128,1536]{1,0:T(8,128)(2,1)} %get-tuple-element.236), channel_id=1, source_target_pairs={{0,2},{1,3},{2,0},{3,1},{4,6},{5,7},{6,4},{7,5},{8,10},{9,11},{10,... | collective-permute-start | bytes 1179656 | tf_op jit(solution)/shard_map/ppermute | solution.py:471
  67.8 3.7 %collective-permute-start.5 = (bf16[128,2048]{1,0:T(8,128)(2,1)S(1)}, bf16[128,2048]{1,0:T(8,128)(2,1)S(1)}, u32[]{:S(2)}, u32[]{:S(2)}) collective-permute-start(bf16[128,2048]{1,0:T(8,128)(2,1)S(1)} %get-tuple-element.135), channel_id=1, source_target_pairs={{0,1},{1,0},{2,3},{3,2},{4,5},{5,4},{6,7},{7,6},{8,9},{9,8},{10,11... | collective-permute-start | bytes 1572872 | tf_op jit(solution)/shard_map/cond/branch_1_fun/ppermute | solution.py:468
  70.9 2.1 %collective-permute-start.6 = (bf16[128,2048]{1,0:T(8,128)(2,1)S(1)}, bf16[128,2048]{1,0:T(8,128)(2,1)S(1)}, u32[]{:S(2)}, u32[]{:S(2)}) collective-permute-start(bf16[128,2048]{1,0:T(8,128)(2,1)S(1)} %get-tuple-element.138), channel_id=1, source_target_pairs={{0,1},{1,0},{2,3},{3,2},{4,5},{5,4},{6,7},{7,6},{8,9},{9,8},{10,11... | collective-permute-start | bytes 1572872 | tf_op jit(solution)/shard_map/cond/branch_1_fun/ppermute | solution.py:468
  71.5 1.7 %copy-start = (bf16[128,4096]{1,0:T(8,128)(2,1)S(1)}, bf16[128,4096]{1,0:T(8,128)(2,1)}, u32[]{:S(2)}) copy-start(bf16[128,4096]{1,0:T(8,128)(2,1)} %get-tuple-element.224) | copy-start | bytes 3145732 | tf_op jit(solution)/shard_map/cond

commit v5 on v4

--- a/solution.py
+++ b/solution.py
@@ -538,7 +538,7 @@
 
     before, toep = lax.cond(always, relay, no_relay, states)
 
-    parts = [(0, depth // 4), (depth // 4, 3 * depth // 8), (5 * depth // 8, 3 * depth // 8)]
+    parts = [(0, 3 * depth // 8), (3 * depth // 8, 3 * depth // 8), (3 * depth // 4, depth // 4)]
     weights = in_hbm(out_weight)
 
     def gated_rows(d, prod, cols):
@@ -550,13 +550,13 @@
     def summed(theirs, mine):
         return mine.astype(F32) + send(theirs, 1).astype(F32)
 
-    def own(prod):
-        half = depth // 2
-        gated, *first_half = gated_rows(0, prod, half)
-        sums = [summed(*first_half), summed(*project(gated, weights, half, half))]
+    half = depth // 2
+
+    def own(gated, theirs, mine):
+        sums = [summed(theirs, mine), summed(*project(gated, weights, half, half))]
         return residual.astype(F32) + jnp.concatenate(sums, axis=1)
 
-    def no_own(prod):
+    def no_own(gated, theirs, mine):
         return jnp.zeros((rows, depth), F32)
 
     gateds, wholes, arriving = [], [], []
@@ -566,18 +566,23 @@
         wholes.append(summed(*first_part).astype(BF16))
     for part in parts[1:]:
 
-        def others(gateds, part=part):
-            return [summed(*project(gated, weights, *part)).astype(BF16) for gated in gateds]
-
-        def no_others(gateds, part=part):
-            return [jnp.zeros((rows, part[1]), BF16) for _ in gateds]
+        def others(gateds, prod, part=part):
+            pairs = [project(gated, weights, *part) for gated in gateds]
+            came = [send(theirs, 1) for theirs, _ in pairs]
+            mine = list(gated_rows(0, prod, half)) if part == parts[-1] else []
+            came, mine = lax.optimization_barrier((came, mine))
+            return [(own.astype(F32) + got.astype(F32)).astype(BF16) for (_, own), got in zip(pairs, came)], mine
+
+        def no_others(gateds, prod, part=part):
+            blank = [jnp.zeros((2 * rows, width), BF16)] + [jnp.zeros((rows, half), BF16)] * 2
+            return [jnp.zeros((rows, part[1]), BF16) for _ in gateds], blank if part == parts[-1] else []
 
         gateds, wholes = lax.optimization_barrier((gateds, wholes))
         arriving.append([send_back(whole, 2 * d) for d, whole in enumerate(wholes, 1)])
-        wholes = lax.cond(always, others, no_others, gateds)
-    prods[0], wholes, arriving[0] = lax.optimization_barrier((prods[0], wholes, arriving[0]))
+        wholes, mine = lax.cond(always, others, no_others, gateds, prods[0])
+    mine, wholes, arriving[0] = lax.optimization_barrier((mine, wholes, arriving[0]))
     arriving.append([send_back(whole, 2 * d) for d, whole in enumerate(wholes, 1)])
-    base = lax.cond(always, own, no_own, prods[0])
+    base = lax.cond(always, own, no_own, *mine)
     return finish(parts, base, [term for terms in arriving for term in terms])
 
 

time: 76.2 us -> 78.8 us (1.034)
  other arithmetic: 2.35 us -> 4.44 us
  Pallas kernels: 34.4 us -> 35.3 us
    pallas_call x1, Pallas kernels: 1.04 us -> 2.63 us  [finish(): pl.pallas_call(functools.partial(finish_kernel, parts), in_specs=[pl.Bloc...]
    add x1, other arithmetic: 0.22 us -> 1.6 us  [own(): return residual.astype(F32) + jnp.concatenate(sums, axis=1)]
    ppermute x11, waiting for transfers between devices: 7.13 us -> 6.26 us  [send(): lax.ppermute(value, 'tp', [(i, target(i, e, chips)) for i in range(steps)])]
  transfers between devices with their start and end apart: 20 -> 20, of which waited for: 10 -> 9; matrix products, arithmetic and copies ran while one was open for 3% -> 5% of each run, Pallas kernels for 37% -> 35%
where the time goes in v5:
time: 78.8 us; the launch traced here: 78.5 us
  Pallas kernels  35.3 us (45%)
  starting transfers between devices  22.3 us (28%)
  waiting for transfers between devices  16.2 us (21%)
  other arithmetic  4.44 us (6%)
    pallas_call x2, Pallas kernels, gate(): pl.pallas_call(functools.partial(gate_kernel, d, chips), grid_spec=pltpu....  9.31 us
    ppermute x11, starting transfers between devices, send(): lax.ppermute(value, 'tp', [(i, target(i, e, chips)) for i in range(steps)])  9.12 us
    pallas_call x3, Pallas kernels, project(): pl.pallas_call(functools.partial(project_kernel, first), in_specs=[vmem,...  7.74 us
    pallas_call x2, Pallas kernels, front(): pl.pallas_call(front_kernel, grid_spec=pltpu.PrefetchScalarGridSpec(num_s...  6.84 us
    ppermute x11, waiting for transfers between devices, send(): lax.ppermute(value, 'tp', [(i, target(i, e, chips)) for i in range(steps)])  6.26 us
    ppermute x4, starting transfers between devices, send_back(): lax.ppermute(value, 'tp', [(i, source(i, e, chips)) for i in range(steps)])  6 us
    ppermute x3, starting transfers between devices, with_context(): return lax.ppermute(value, 'ctx', [(i, i ^ bit) for i in range(contexts)])  5.87 us
    ppermute x3, waiting for transfers between devices, with_context(): return lax.ppermute(value, 'ctx', [(i, i ^ bit) for i in range(contexts)])  5.65 us
  transfers between devices with their start and end apart: 20, of which 9 were waited for; matrix products, arithmetic and copies ran while one was open for 5% of the time, Pallas kernels for 35%

profile of v5, /device:TPU:0, one launch (start us, length us, event | category | flops | bytes accessed | tf_op | source)
XLA Modules:
  0.0 78.5 jit_solution(816678475153011791)
XLA Ops:
  0.0 1.7 %shard_map.65 = (bf16[2,128,2048]{2,1,0:T(8,128)(2,1)S(1)}, bf16[3,8,2048]{2,1,0:T(8,128)(2,1)S(1)}, bf16[3,8,2048]{2,1,0:T(8,128)(2,1)S(1)}, f32[2,8,1024]{2,1,...) custom-call(s32[1]{0:T(128)} %bitcast.info, ...), custom_call_target="tpu_custom_call" | custom-call | flops 1 | bytes 1 | tf_op jit(solution)/shard_map/pallas_call | solution.py:114
  3.6 3.2 %collective-permute-start.10 = (f32[2,8,1024]{2,1,0:T(8,128)S(1)}, f32[2,8,1024]{2,1,0:T(8,128)S(1)}, u32[]{:S(2)}, u32[]{:S(2)}) collective-permute-start(f32[2,8,1024]{2,1,0:T(8,128)S(1)} %get-tuple-element.206.taps), channel_id=1, source_target_pairs={{0,2},{1,3},{2,0},{3,1},{4,6},{5,7},{6,4},{7,5},{8,10},{9,11},{10,... | collective-permute-start | bytes 196616 | tf_op jit(solution)/shard_map/ppermute | solution.py:471
  6.8 2.2 %collective-permute-done.10.taps = f32[2,8,1024]{2,1,0:T(8,128)S(1)} collective-permute-done((f32[2,8,1024]{2,1,0:T(8,128)S(1)}, f32[2,8,1024]{2,1,0:T(8,128)S(1)}, u32[]{:S(2)}, u32[]{:S(2)}) %collective-permute-start.10) | collective-permute-done | bytes 65568 | tf_op jit(solution)/shard_map/ppermute | solution.py:471
  9.1 4.1 %collective-permute-start.12 = (bf16[128,1024]{1,0:T(8,128)(2,1)S(1)}, bf16[128,1024]{1,0:T(8,128)(2,1)S(1)}, u32[]{:S(2)}, u32[]{:S(2)}) collective-permute-start(bf16[128,1024]{1,0:T(8,128)(2,1)S(1)} %get-tuple-element.212), channel_id=1, source_target_pairs={{0,1},{1,0},{2,3},{3,2},{4,5},{5,4},{6,7},{7,6},{8,9},{9,8},{10,11... | collective-permute-start | bytes 786440 | tf_op jit(solution)/shard_map/ppermute | solution.py:468
  13.2 1.5 %collective-permute-start.13 = (bf16[128,1024]{1,0:T(8,128)(2,1)S(1)}, bf16[128,1024]{1,0:T(8,128)(2,1)S(1)}, u32[]{:S(2)}, u32[]{:S(2)}) collective-permute-start(bf16[128,1024]{1,0:T(8,128)(2,1)S(1)} %get-tuple-element.213), channel_id=1, source_target_pairs={{0,2},{1,3},{2,0},{3,1},{4,6},{5,7},{6,4},{7,5},{8,10},{9,11},{10,... | collective-permute-start | bytes 786440 | tf_op jit(solution)/shard_map/ppermute | solution.py:468
  14.7 3.4 %shard_map.67 = (bf16[288,1024]{1,0:T(8,128)(2,1)S(1)}, f32[24,1024]{1,0:T(8,128)S(1)}) custom-call(s32[1]{0:T(128)} %bitcast.info, bf16[3,128,4096]{2,1,0:T(8,128)(2,1)} %bitcast.6, bf16[3,128,4096]{2,1,0:T(8,128)(2,1)} %bitcast.7, bf16[2,128,2048]{2,1,0:T(8,128)(2,1)S(1)} %collective-permute-done.7.kv_in, ...), custom_call_target="tpu_custom_call" | custom-call | flops 1 | bytes 1 | tf_op jit(solution)/shard_map/pallas_call | solution.py:190
  18.7 3.4 %shard_map.66 = (bf16[288,1024]{1,0:T(8,128)(2,1)S(1)}, f32[24,1024]{1,0:T(8,128)S(1)}) custom-call(s32[1]{0:T(128)} %bitcast.info, bf16[3,128,4096]{2,1,0:T(8,128)(2,1)} %bitcast.8, bf16[3,128,4096]{2,1,0:T(8,128)(2,1)} %bitcast.9, bf16[2,128,2048]{2,1,0:T(8,128)(2,1)S(1)} %collective-permute-done.7.kv_in, ...), custom_call_target="tpu_custom_call" | custom-call | flops 1 | bytes 1 | tf_op jit(solution)/shard_map/pallas_call | solution.py:190
  22.1 1.4 %collective-permute-done.11.rest_1_ = f32[24,1024]{1,0:T(8,128)S(1)} collective-permute-done((f32[24,1024]{1,0:T(8,128)S(1)}, f32[24,1024]{1,0:T(8,128)S(1)}, u32[]{:S(2)}, u32[]{:S(2)}) %collective-permute-start.11) | collective-permute-done | bytes 98336 | tf_op jit(solution)/shard_map/ppermute | solution.py:468
  23.6 1.6 %collective-permute-start.14 = (bf16[288,1024]{1,0:T(8,128)(2,1)S(1)}, bf16[288,1024]{1,0:T(8,128)(2,1)S(1)}, u32[]{:S(2)}, u32[]{:S(2)}) collective-permute-start(bf16[288,1024]{1,0:T(8,128)(2,1)S(1)} %get-tuple-element.215), channel_id=1, source_target_pairs={{0,2},{1,3},{2,0},{3,1},{4,6},{5,7},{6,4},{7,5},{8,10},{9,11},{10,... | collective-permute-start | bytes 1769480 | tf_op jit(solution)/shard_map/ppermute | solution.py:468
  25.2 16.0 %conditional.4 = (f32[16,1024]{1,0:T(8,128)S(1)}, bf16[8192,128]{1,0:T(8,128)(2,1)}) conditional(s32[]{:T(128)} %convert_element_type.54, f32[16,1024]{1,0:T(8,128)S(1)} %get-tuple-element.216.rest_4_, (f32[16,1024]{1,0:T(8,128)S(1)}, s32[]{:T(128)}, s32[]{:T(128)}, f32[24,1024]{1,0:T(8,128)S(1)}, f32[24,1024]{1,0:T(8,128)S(1)}, /*index=5*/s32[]{:T(128)}, ...), branch_computations={%region_0.1_spmd, %region_1.2_spmd} | conditional | flops 540727 | bytes 2359982 | solution.py:539
  25.2 1.6 %collective-permute-start = (f32[16,1024]{1,0:T(8,128)S(1)}, f32[16,1024]{1,0:T(8,128)S(1)}, u32[]{:S(2)}, u32[]{:S(2)}) collective-permute-start(f32[16,1024]{1,0:T(8,128)S(1)} %get-tuple-element.104), channel_id=1, source_target_pairs={{0,4},{4,0},{8,12},{12,8},{16,20},{20,16},{24,28},{28,24},{1,5},{5... | collective-permute-start | bytes 196616 | tf_op jit(solution)/shard_map/cond/branch_1_fun/ppermute | solution.py:474
  26.8 2.2 %branch_1_fun.6.rest_0_ = bf16[8192,128]{1,0:T(8,128)(2,1)} custom-call(f32[1,1024]{1,0:T(1,128)S(1)} %get-tuple-element.107.rate_row, f32[1,1024]{1,0:T(1,128)S(1)} %get-tuple-element.108.coef_row), custom_call_target="tpu_custom_call" | custom-call | flops 1 | bytes 1 | tf_op jit(solution)/shard_map/cond/branch_1_fun/pallas_call | solution.py:226
  30.2 1.5 %collective-permute-start.1 = (f32[16,1024]{1,0:T(8,128)S(1)}, f32[16,1024]{1,0:T(8,128)S(1)}, u32[]{:S(2)}, u32[]{:S(2)}) collective-permute-start(f32[16,1024]{1,0:T(8,128)S(1)} %add_select_fusion.1), channel_id=1, source_target_pairs={{0,8},{4,12},{8,0},{12,4},{16,24},{20,28},{24,16},{28,20},{1,9},{5... | collective-permute-start | bytes 196616 | tf_op jit(solution)/shard_map/cond/branch_1_fun/ppermute | solution.py:474
  31.6 2.2 %branch_1_fun.7 = bf16[8192,128]{1,0:T(8,128)(2,1)} custom-call(f32[1,1024]{1,0:T(1,128)S(1)} %get-tuple-element.107.rate_row, f32[1,1024]{1,0:T(1,128)S(1)} %get-tuple-element.108.coef_row, bf16[8192,128]{1,0:T(8,128)(2,1)} %branch_1_fun.6.rest_0_), custom_call_target="tpu_custom_call", output_to_operand_aliasing={{}: (2, {})} | custom-call | flops 1 | bytes 1 | tf_op jit(solution)/shard_map/cond/branch_1_fun/pallas_call | solution.py:226
  34.5 2.8 %collective-permute-start.2 = (f32[16,1024]{1,0:T(8,128)S(1)}, f32[16,1024]{1,0:T(8,128)S(1)}, u32[]{:S(2)}, u32[]{:S(2)}) collective-permute-start(f32[16,1024]{1,0:T(8,128)S(1)} %add_select_fusion), channel_id=1, source_target_pairs={{0,16},{4,20},{8,24},{12,28},{16,0},{20,4},{24,8},{28,12},{1,17},{... | collective-permute-start | bytes 196616 | tf_op jit(solution)/shard_map/cond/branch_1_fun/ppermute | solution.py:474
  37.3 3.8 %collective-permute-done.2 = f32[16,1024]{1,0:T(8,128)S(1)} collective-permute-done((f32[16,1024]{1,0:T(8,128)S(1)}, f32[16,1024]{1,0:T(8,128)S(1)}, u32[]{:S(2)}, u32[]{:S(2)}) %collective-permute-start.2) | collective-permute-done | bytes 65568 | tf_op jit(solution)/shard_map/cond/branch_1_fun/ppermute | solution.py:474
  41.2 2.7 %shard_map.68.long_in = f32[256,1024]{1,0:T(8,128)S(1)} custom-call(bf16[288,1024]{1,0:T(8,128)(2,1)S(1)} %collective-permute-done.14.prod.second, bf16[8192,128]{1,0:T(8,128)(2,1)} %get-tuple-element.221.toep), custom_call_target="tpu_custom_call" | custom-call | flops 1 | bytes 1 | tf_op jit(solution)/shard_map/pallas_call | solution.py:255
  43.9 3.9 %shard_map.69 = (bf16[256,1024]{1,0:T(8,128)(2,1)S(1)}, bf16[128,1536]{1,0:T(8,128)(2,1)S(1)}, bf16[128,1536]{1,0:T(8,128)(2,1)S(1)}) custom-call(s32[1]{0:T(128)} %bitcast.info, f32[256,1024]{1,0:T(8,128)S(1)} %shard_map.68.long_in, bf16[288,1024]{1,0:T(8,128)(2,1)S(1)} %collective-permute-done.14.prod.second, ...), custom_call_target="tpu_custom_call" | custom-call | flops 1 | bytes 1 | tf_op jit(solution)/shard_map/pallas_call | solution.py:369
  47.9 1.7 %collective-permute-done.16 = bf16[128,1536]{1,0:T(8,128)(2,1)S(1)} collective-permute-done((bf16[128,1536]{1,0:T(8,128)(2,1)S(1)}, bf16[128,1536]{1,0:T(8,128)(2,1)S(1)}, u32[]{:S(2)}, u32[]{:S(2)}) %collective-permute-start.16) | collective-permute-done | bytes 393248 | tf_op jit(solution)/shard_map/ppermute | solution.py:468
  51.2 5.2 %conditional.5 = (bf16[128,1536]{1,0:T(8,128)(2,1)}) conditional(s32[]{:T(128)} %convert_element_type.54, () %tuple.59, (bf16[256,1024]{1,0:T(8,128)(2,1)S(1)}, bf16[1024,4096]{1,0:T(8,128)(2,1)}) %tuple.60), branch_computations={%region_2.3_spmd, %region_3.4_spmd} | conditional | flops 786433 | bytes 2752561 | solution.py:582
  51.2 2.6 %branch_1_fun.8 = (bf16[128,1536]{1,0:T(8,128)(2,1)S(1)}, bf16[128,1536]{1,0:T(8,128)(2,1)S(1)}) custom-call(bf16[256,1024]{1,0:T(8,128)(2,1)S(1)} %get-tuple-element.115.gated, bf16[1024,4096]{1,0:T(8,128)(2,1)} %get-tuple-element.116.weights), custom_call_target="tpu_custom_call" | custom-call | flops 1 | bytes 1 | tf_op jit(solution)/shard_map/cond/branch_1_fun/pallas_call | solution.py:412
  53.9 1.6 %collective-permute-done.3 = bf16[128,1536]{1,0:T(8,128)(2,1)S(1)} collective-permute-done((bf16[128,1536]{1,0:T(8,128)(2,1)S(1)}, bf16[128,1536]{1,0:T(8,128)(2,1)S(1)}, u32[]{:S(2)}, u32[]{:S(2)}) %collective-permute-start.3) | collective-permute-done | bytes 393248 | tf_op jit(solution)/shard_map/cond/branch_1_fun/ppermute | solution.py:468
  56.4 1.3 %collective-permute-start.18 = (bf16[128,1536]{1,0:T(8,128)(2,1)}, bf16[128,1536]{1,0:T(8,128)(2,1)S(1)}, u32[]{:S(2)}, u32[]{:S(2)}) collective-permute-start(bf16[128,1536]{1,0:T(8,128)(2,1)} %get-tuple-element.265), channel_id=1, source_target_pairs={{0,2},{1,3},{2,0},{3,1},{4,6},{5,7},{6,4},{7,5},{8,10},{9,11},{10,... | collective-permute-start | bytes 1179656 | tf_op jit(solution)/shard_map/ppermute | solution.py:471
  57.7 8.5 %conditional.6 = (bf16[128,1024]{1,0:T(8,128)(2,1)}, bf16[256,1024]{1,0:T(8,128)(2,1)S(1)}, bf16[128,2048]{1,0:T(8,128)(2,1)S(1)}, bf16[128,2048]{1,0:T(8,128)(2,1)S(1)}) conditional(s32[]{:T(128)} %convert_element_type.54, () %tuple.54, (bf16[256,1024]{1,0:T(8,128)(2,1)S(1)}, bf16[1024,4096]{1,0:T(8,128)(2,1)}, s32[1]{0:T(128)}, ...), branch_computations={%region_4.5_spmd, %region_5.6_spmd} | conditional | flops 524290 | bytes 2883686 | solution.py:582
  57.7 2.2 %branch_1_fun.9 = (bf16[128,1024]{1,0:T(8,128)(2,1)S(1)}, bf16[128,1024]{1,0:T(8,128)(2,1)S(1)}) custom-call(bf16[256,1024]{1,0:T(8,128)(2,1)S(1)} %get-tuple-element.119.gated, bf16[1024,4096]{1,0:T(8,128)(2,1)} %get-tuple-element.120.weights.rest_7_), custom_call_target="tpu_custom_call" | custom-call | flops 1 | bytes 1 | tf_op jit(solution)/shard_map/cond/branch_1_fun/pallas_call | solution.py:412
  59.9 5.4 %branch_1_fun.10 = (bf16[256,1024]{1,0:T(8,128)(2,1)S(1)}, bf16[128,2048]{1,0:T(8,128)(2,1)S(1)}, bf16[128,2048]{1,0:T(8,128)(2,1)S(1)}) custom-call(s32[1]{0:T(128)} %get-tuple-element.123.info, bf16[288,1024]{1,0:T(8,128)(2,1)S(1)} %get-tuple-element.124.long_in, bf16[8192,128]{1,0:T(8,128)(2,1)} %get-tuple-element.125.second, ...), custom_call_target="tpu_custom_call" | custom-call | flops 1 | bytes 1 | tf_op jit(solution)/shard_map/cond/branch_1_fun/pallas_call | solution.py:369
  66.9 6.9 %conditional.7 = (f32[128,4096]{1,0:T(8,128)}) conditional(s32[]{:T(128)} %convert_element_type.54, () %tuple.53, (bf16[128,4096]{1,0:T(8,128)(2,1)}, bf16[128,2048]{1,0:T(8,128)(2,1)S(1)}, bf16[128,2048]{1,0:T(8,128)(2,1)S(1)}, bf16[256,1024]{1,0:T(8,128)(2,1)S(1)}, bf16[1024,4096]{1,0:T(8,128)(2,1)}) %tuple.64), branch_computations={%region_6.7_spmd, %region_7.8_spmd} | conditional | flops 3145729 | bytes 17825908 | solution.py:585
  67.1 3.0 %branch_1_fun.11 = (bf16[128,2048]{1,0:T(8,128)(2,1)S(1)}, bf16[128,2048]{1,0:T(8,128)(2,1)S(1)}) custom-call(bf16[256,1024]{1,0:T(8,128)(2,1)S(1)} %get-tuple-element.145.gated, bf16[1024,4096]{1,0:T(8,128)(2,1)} %get-tuple-element.146.weights), custom_call_target="tpu_custom_call" | custom-call | flops 1 | bytes 1 | tf_op jit(solution)/shard_map/cond/branch_1_fun/pallas_call | solution.py:412
  70.6 1.4 %collective-permute-done.6 = bf16[128,2048]{1,0:T(8,128)(2,1)S(1)} collective-permute-done((bf16[128,2048]{1,0:T(8,128)(2,1)S(1)}, bf16[128,2048]{1,0:T(8,128)(2,1)S(1)}, u32[]{:S(2)}, u32[]{:S(2)}) %collective-permute-start.6) | collective-permute-done | bytes 524320 | tf_op jit(solution)/shard_map/cond/branch_1_fun/ppermute | solution.py:468
  72.2 1.6 %maximum_add_fusion = f32[128,4096]{1,0:T(8,128)} fusion(f32[128,2048]{1,0:T(8,128)S(1)} %convert_add_fusion, f32[128,2048]{1,0:T(8,128)S(1)} %convert_add_fusion.1, bf16[128,4096]{1,0:T(8,128)(2,1)S(1)} %copy-done), kind=kLoop, calls=%fused_computation.11 | loop fusion | flops 1572864 | bytes 5242880 | tf_op jit(solution)/shard_map/cond/branch_1_fun/add | solution.py:557
  73.8 2.0 %collective-permute-done.19.rest_2_ = bf16[128,1024]{1,0:T(8,128)(2,1)S(1)} collective-permute-done((bf16[128,1024]{1,0:T(8,128)(2,1)}, bf16[128,1024]{1,0:T(8,128)(2,1)S(1)}, u32[]{:S(2)}, u32[]{:S(2)}) %collective-permute-start.19) | collective-permute-done | bytes 262176 | tf_op jit(solution)/shard_map/ppermute | solution.py:471
  75.8 2.6 %shard_map.70 = bf16[128,4096]{1,0:T(8,128)(2,1)} custom-call(f32[128,4096]{1,0:T(8,128)} %get-tuple-element.266.base, bf16[128,1536]{1,0:T(8,128)(2,1)S(1)} %collective-permute-done.17.rest_0_, bf16[128,1536]{1,0:T(8,128)(2,1)S(1)} %collective-permute-done.18.rest_1_, bf16[128,1024]{1,0:T(8,128)(2,1)S(1)} %collective-permute-done.19.rest_2_), custom_call_target="tpu_custom_call" | custom-call | flops 1 | bytes 1 | tf_op jit(solution)/shard_map/pallas_call | solution.py:445
  (40 shorter events, 9.4 us)
Async XLA Ops:
  1.7 7.3 %collective-permute-start.7 = (bf16[2,128,2048]{2,1,0:T(8,128)(2,1)S(1)}, bf16[2,128,2048]{2,1,0:T(8,128)(2,1)S(1)}, u32[]{:S(2)}, u32[]{:S(2)}) collective-permute-start(bf16[2,128,2048]{2,1,0:T(8,128)(2,1)S(1)} %get-tuple-element.196), channel_id=1, source_target_pairs={{0,1},{1,0},{2,3},{3,2},{4,5},{5,4},{6,7},{7,6},{8,9},{9,8},{10,11... | collective-permute-start | bytes 3145736 | tf_op jit(solution)/shard_map/ppermute | solution.py:468
  2.3 6.8 %collective-permute-start.8 = (bf16[3,8,2048]{2,1,0:T(8,128)(2,1)S(1)}, bf16[3,8,2048]{2,1,0:T(8,128)(2,1)S(1)}, u32[]{:S(2)}, u32[]{:S(2)}) collective-permute-start(bf16[3,8,2048]{2,1,0:T(8,128)(2,1)S(1)} %get-tuple-element.197), channel_id=1, source_target_pairs={{1,2},{3,4},{5,6},{7,8},{9,10},{11,12},{13,14},{15,16},{17,18},{19... | collective-permute-start | bytes 294920 | tf_op jit(solution)/shard_map/ppermute | solution.py:490
  2.9 6.2 %collective-permute-start.9 = (bf16[3,8,2048]{2,1,0:T(8,128)(2,1)S(1)}, bf16[3,8,2048]{2,1,0:T(8,128)(2,1)S(1)}, u32[]{:S(2)}, u32[]{:S(2)}) collective-permute-start(bf16[3,8,2048]{2,1,0:T(8,128)(2,1)S(1)} %get-tuple-element.198), channel_id=1, source_target_pairs={{1,3},{3,5},{5,7},{7,9},{9,11},{11,13},{13,15},{15,17},{17,19},{19... | collective-permute-start | bytes 294920 | tf_op jit(solution)/shard_map/ppermute | solution.py:490
  3.6 5.5 %collective-permute-start.10 = (f32[2,8,1024]{2,1,0:T(8,128)S(1)}, f32[2,8,1024]{2,1,0:T(8,128)S(1)}, u32[]{:S(2)}, u32[]{:S(2)}) collective-permute-start(f32[2,8,1024]{2,1,0:T(8,128)S(1)} %get-tuple-element.206.taps), channel_id=1, source_target_pairs={{0,2},{1,3},{2,0},{3,1},{4,6},{5,7},{6,4},{7,5},{8,10},{9,11},{10,... | collective-permute-start | bytes 196616 | tf_op jit(solution)/shard_map/ppermute | solution.py:471
  9.1 14.5 %collective-permute-start.12 = (bf16[128,1024]{1,0:T(8,128)(2,1)S(1)}, bf16[128,1024]{1,0:T(8,128)(2,1)S(1)}, u32[]{:S(2)}, u32[]{:S(2)}) collective-permute-start(bf16[128,1024]{1,0:T(8,128)(2,1)S(1)} %get-tuple-element.212), channel_id=1, source_target_pairs={{0,1},{1,0},{2,3},{3,2},{4,5},{5,4},{6,7},{7,6},{8,9},{9,8},{10,11... | collective-permute-start | bytes 786440 | tf_op jit(solution)/shard_map/ppermute | solution.py:468
  13.2 10.4 %collective-permute-start.13 = (bf16[128,1024]{1,0:T(8,128)(2,1)S(1)}, bf16[128,1024]{1,0:T(8,128)(2,1)S(1)}, u32[]{:S(2)}, u32[]{:S(2)}) collective-permute-start(bf16[128,1024]{1,0:T(8,128)(2,1)S(1)} %get-tuple-element.213), channel_id=1, source_target_pairs={{0,2},{1,3},{2,0},{3,1},{4,6},{5,7},{6,4},{7,5},{8,10},{9,11},{10,... | collective-permute-start | bytes 786440 | tf_op jit(solution)/shard_map/ppermute | solution.py:468
  18.1 5.5 %collective-permute-start.11 = (f32[24,1024]{1,0:T(8,128)S(1)}, f32[24,1024]{1,0:T(8,128)S(1)}, u32[]{:S(2)}, u32[]{:S(2)}) collective-permute-start(f32[24,1024]{1,0:T(8,128)S(1)} %get-tuple-element.209), channel_id=1, source_target_pairs={{0,2},{1,3},{2,0},{3,1},{4,6},{5,7},{6,4},{7,5},{8,10},{9,11},{10,... | collective-permute-start | bytes 294920 | tf_op jit(solution)/shard_map/ppermute | solution.py:468
  23.6 1.6 %copy-start.1 = (bf16[128,1024]{1,0:T(8,128)(2,1)}, bf16[128,1024]{1,0:T(8,128)(2,1)S(1)}, u32[]{:S(2)}) copy-start(bf16[128,1024]{1,0:T(8,128)(2,1)S(1)} %collective-permute-done.12) | copy-start | bytes 786436
  23.6 17.6 %collective-permute-start.14 = (bf16[288,1024]{1,0:T(8,128)(2,1)S(1)}, bf16[288,1024]{1,0:T(8,128)(2,1)S(1)}, u32[]{:S(2)}, u32[]{:S(2)}) collective-permute-start(bf16[288,1024]{1,0:T(8,128)(2,1)S(1)} %get-tuple-element.215), channel_id=1, source_target_pairs={{0,2},{1,3},{2,0},{3,1},{4,6},{5,7},{6,4},{7,5},{8,10},{9,11},{10,... | collective-permute-start | bytes 1769480 | tf_op jit(solution)/shard_map/ppermute | solution.py:468
  25.1 18.8 %collective-permute-start.15 = (bf16[128,1024]{1,0:T(8,128)(2,1)S(1)}, bf16[128,1024]{1,0:T(8,128)(2,1)S(1)}, u32[]{:S(2)}, u32[]{:S(2)}) collective-permute-start(bf16[128,1024]{1,0:T(8,128)(2,1)S(1)} %get-tuple-element.222), channel_id=1, source_target_pairs={{0,3},{1,2},{2,1},{3,0},{4,7},{5,6},{6,5},{7,4},{8,11},{9,10},{10,... | collective-permute-start | bytes 786440 | tf_op jit(solution)/shard_map/ppermute | solution.py:468
  25.2 4.9 %collective-permute-start = (f32[16,1024]{1,0:T(8,128)S(1)}, f32[16,1024]{1,0:T(8,128)S(1)}, u32[]{:S(2)}, u32[]{:S(2)}) collective-permute-start(f32[16,1024]{1,0:T(8,128)S(1)} %get-tuple-element.104), channel_id=1, source_target_pairs={{0,4},{4,0},{8,12},{12,8},{16,20},{20,16},{24,28},{28,24},{1,5},{5... | collective-permute-start | bytes 196616 | tf_op jit(solution)/shard_map/cond/branch_1_fun/ppermute | solution.py:474
  30.2 4.3 %collective-permute-start.1 = (f32[16,1024]{1,0:T(8,128)S(1)}, f32[16,1024]{1,0:T(8,128)S(1)}, u32[]{:S(2)}, u32[]{:S(2)}) collective-permute-start(f32[16,1024]{1,0:T(8,128)S(1)} %add_select_fusion.1), channel_id=1, source_target_pairs={{0,8},{4,12},{8,0},{12,4},{16,24},{20,28},{24,16},{28,20},{1,9},{5... | collective-permute-start | bytes 196616 | tf_op jit(solution)/shard_map/cond/branch_1_fun/ppermute | solution.py:474
  34.5 6.6 %collective-permute-start.2 = (f32[16,1024]{1,0:T(8,128)S(1)}, f32[16,1024]{1,0:T(8,128)S(1)}, u32[]{:S(2)}, u32[]{:S(2)}) collective-permute-start(f32[16,1024]{1,0:T(8,128)S(1)} %add_select_fusion), channel_id=1, source_target_pairs={{0,16},{4,20},{8,24},{12,28},{16,0},{20,4},{24,8},{28,12},{1,17},{... | collective-permute-start | bytes 196616 | tf_op jit(solution)/shard_map/cond/branch_1_fun/ppermute | solution.py:474
  47.8 1.8 %collective-permute-start.16 = (bf16[128,1536]{1,0:T(8,128)(2,1)S(1)}, bf16[128,1536]{1,0:T(8,128)(2,1)S(1)}, u32[]{:S(2)}, u32[]{:S(2)}) collective-permute-start(bf16[128,1536]{1,0:T(8,128)(2,1)S(1)} %get-tuple-element.227), channel_id=1, source_target_pairs={{0,1},{1,0},{2,3},{3,2},{4,5},{5,4},{6,7},{7,6},{8,9},{9,8},{10,11... | collective-permute-start | bytes 1179656 | tf_op jit(solution)/shard_map/ppermute | solution.py:468
  50.4 15.7 %collective-permute-start.17 = (bf16[128,1536]{1,0:T(8,128)(2,1)}, bf16[128,1536]{1,0:T(8,128)(2,1)S(1)}, u32[]{:S(2)}, u32[]{:S(2)}) collective-permute-start(bf16[128,1536]{1,0:T(8,128)(2,1)} %add_convert_fusion.2), channel_id=1, source_target_pairs={{0,2},{1,3},{2,0},{3,1},{4,6},{5,7},{6,4},{7,5},{8,10},{9,11},{10,... | collective-permute-start | bytes 1179656 | tf_op jit(solution)/shard_map/ppermute | solution.py:471
  53.8 1.8 %collective-permute-start.3 = (bf16[128,1536]{1,0:T(8,128)(2,1)S(1)}, bf16[128,1536]{1,0:T(8,128)(2,1)S(1)}, u32[]{:S(2)}, u32[]{:S(2)}) collective-permute-start(bf16[128,1536]{1,0:T(8,128)(2,1)S(1)} %get-tuple-element.118), channel_id=1, source_target_pairs={{0,1},{1,0},{2,3},{3,2},{4,5},{5,4},{6,7},{7,6},{8,9},{9,8},{10,11... | collective-permute-start | bytes 1179656 | tf_op jit(solution)/shard_map/cond/branch_1_fun/ppermute | solution.py:468
  56.4 17.4 %collective-permute-start.18 = (bf16[128,1536]{1,0:T(8,128)(2,1)}, bf16[128,1536]{1,0:T(8,128)(2,1)S(1)}, u32[]{:S(2)}, u32[]{:S(2)}) collective-permute-start(bf16[128,1536]{1,0:T(8,128)(2,1)} %get-tuple-element.265), channel_id=1, source_target_pairs={{0,2},{1,3},{2,0},{3,1},{4,6},{5,7},{6,4},{7,5},{8,10},{9,11},{10,... | collective-permute-start | bytes 1179656 | tf_op jit(solution)/shard_map/ppermute | solution.py:471
  57.7 2.3 %copy-start.2 = (bf16[128,1024]{1,0:T(8,128)(2,1)S(1)}, bf16[128,1024]{1,0:T(8,128)(2,1)}, u32[]{:S(2)}) copy-start(bf16[128,1024]{1,0:T(8,128)(2,1)} %get-tuple-element.126.q0) | copy-start | bytes 786436 | tf_op jit(solution)/shard_map/cond
  59.8 5.5 %collective-permute-start.4 = (bf16[128,1024]{1,0:T(8,128)(2,1)S(1)}, bf16[128,1024]{1,0:T(8,128)(2,1)S(1)}, u32[]{:S(2)}, u32[]{:S(2)}) collective-permute-start(bf16[128,1024]{1,0:T(8,128)(2,1)S(1)} %get-tuple-element.122), channel_id=1, source_target_pairs={{0,1},{1,0},{2,3},{3,2},{4,5},{5,4},{6,7},{7,6},{8,9},{9,8},{10,11... | collective-permute-start | bytes 786440 | tf_op jit(solution)/shard_map/cond/branch_1_fun/ppermute | solution.py:468
  66.2 9.7 %collective-permute-start.19 = (bf16[128,1024]{1,0:T(8,128)(2,1)}, bf16[128,1024]{1,0:T(8,128)(2,1)S(1)}, u32[]{:S(2)}, u32[]{:S(2)}) collective-permute-start(bf16[128,1024]{1,0:T(8,128)(2,1)} %get-tuple-element.242), channel_id=1, source_target_pairs={{0,2},{1,3},{2,0},{3,1},{4,6},{5,7},{6,4},{7,5},{8,10},{9,11},{10,... | collective-permute-start | bytes 786440 | tf_op jit(solution)/shard_map/ppermute | solution.py:471
  66.9 3.6 %collective-permute-start.5 = (bf16[128,2048]{1,0:T(8,128)(2,1)S(1)}, bf16[128,2048]{1,0:T(8,128)(2,1)S(1)}, u32[]{:S(2)}, u32[]{:S(2)}) collective-permute-start(bf16[128,2048]{1,0:T(8,128)(2,1)S(1)} %get-tuple-element.144), channel_id=1, source_target_pairs={{0,1},{1,0},{2,3},{3,2},{4,5},{5,4},{6,7},{7,6},{8,9},{9,8},{10,11... | collective-permute-start | bytes 1572872 | tf_op jit(solution)/shard_map/cond/branch_1_fun/ppermute | solution.py:468
  70.1 2.0 %collective-permute-start.6 = (bf16[128,2048]{1,0:T(8,128)(2,1)S(1)}, bf16[128,2048]{1,0:T(8,128)(2,1)S(1)}, u32[]{:S(2)}, u32[]{:S(2)}) collective-permute-start(bf16[128,2048]{1,0:T(8,128)(2,1)S(1)} %get-tuple-element.148), channel_id=1, source_target_pairs={{0,1},{1,0},{2,3},{3,2},{4,5},{5,4},{6,7},{7,6},{8,9},{9,8},{10,11... | collective-permute-start | bytes 1572872 | tf_op jit(solution)/shard_map/cond/branch_1_fun/ppermute | solution.py:468
  70.5 1.7 %copy-start = (bf16[128,4096]{1,0:T(8,128)(2,1)S(1)}, bf16[128,4096]{1,0:T(8,128)(2,1)}, u32[]{:S(2)}) copy-start(bf16[128,4096]{1,0:T(8,128)(2,1)} %get-tuple-element.246) | copy-start | bytes 3145732 | tf_op jit(solution)/shard_map/cond

commit v6 on v4

--- a/solution.py
+++ b/solution.py
@@ -538,7 +538,7 @@
 
     before, toep = lax.cond(always, relay, no_relay, states)
 
-    parts = [(0, depth // 4), (depth // 4, 3 * depth // 8), (5 * depth // 8, 3 * depth // 8)]
+    parts = [(0, 3 * depth // 8), (3 * depth // 8, 3 * depth // 8), (3 * depth // 4, depth // 4)]
     weights = in_hbm(out_weight)
 
     def gated_rows(d, prod, cols):

time: 76.2 us -> 76.3 us (level)
  transfers between devices with their start and end apart: 20 -> 20, of which waited for: 10 -> 11; matrix products, arithmetic and copies ran while one was open for 3% -> 3% of each run, Pallas kernels for 37% -> 37%
where the time goes in v6:
time: 76.3 us; the launch traced here: 76 us
  Pallas kernels  34.4 us (45%)
  starting transfers between devices  22.4 us (29%)
  waiting for transfers between devices  16.7 us (22%)
  other arithmetic  2.3 us (3%)
    pallas_call x2, Pallas kernels, gate(): pl.pallas_call(functools.partial(gate_kernel, d, chips), grid_spec=pltpu....  9.39 us
    ppermute x11, starting transfers between devices, send(): lax.ppermute(value, 'tp', [(i, target(i, e, chips)) for i in range(steps)])  9.17 us
    pallas_call x3, Pallas kernels, project(): pl.pallas_call(functools.partial(project_kernel, first), in_specs=[vmem,...  7.7 us
    pallas_call x2, Pallas kernels, front(): pl.pallas_call(front_kernel, grid_spec=pltpu.PrefetchScalarGridSpec(num_s...  7.46 us
    ppermute x11, waiting for transfers between devices, send(): lax.ppermute(value, 'tp', [(i, target(i, e, chips)) for i in range(steps)])  7.13 us
    ppermute x4, starting transfers between devices, send_back(): lax.ppermute(value, 'tp', [(i, source(i, e, chips)) for i in range(steps)])  6.04 us
    ppermute x3, starting transfers between devices, with_context(): return lax.ppermute(value, 'ctx', [(i, i ^ bit) for i in range(contexts)])  5.87 us
    ppermute x3, waiting for transfers between devices, with_context(): return lax.ppermute(value, 'ctx', [(i, i ^ bit) for i in range(contexts)])  5.66 us
  transfers between devices with their start and end apart: 20, of which 11 were waited for; matrix products, arithmetic and copies ran while one was open for 3% of the time, Pallas kernels for 37%

profile of v6, /device:TPU:0, one launch (start us, length us, event | category | flops | bytes accessed | tf_op | source)
XLA Modules:
  0.0 76.0 jit_solution(14402667885110170846)
XLA Ops:
  0.0 1.7 %shard_map.65 = (bf16[2,128,2048]{2,1,0:T(8,128)(2,1)S(1)}, bf16[3,8,2048]{2,1,0:T(8,128)(2,1)S(1)}, bf16[3,8,2048]{2,1,0:T(8,128)(2,1)S(1)}, f32[2,8,1024]{2,1,...) custom-call(s32[1]{0:T(128)} %bitcast.info, ...), custom_call_target="tpu_custom_call" | custom-call | flops 1 | bytes 1 | tf_op jit(solution)/shard_map/pallas_call | solution.py:114
  3.6 3.2 %collective-permute-start.10 = (f32[2,8,1024]{2,1,0:T(8,128)S(1)}, f32[2,8,1024]{2,1,0:T(8,128)S(1)}, u32[]{:S(2)}, u32[]{:S(2)}) collective-permute-start(f32[2,8,1024]{2,1,0:T(8,128)S(1)} %get-tuple-element.190.taps), channel_id=1, source_target_pairs={{0,2},{1,3},{2,0},{3,1},{4,6},{5,7},{6,4},{7,5},{8,10},{9,11},{10,... | collective-permute-start | bytes 196616 | tf_op jit(solution)/shard_map/ppermute | solution.py:471
  6.8 2.2 %collective-permute-done.10.taps = f32[2,8,1024]{2,1,0:T(8,128)S(1)} collective-permute-done((f32[2,8,1024]{2,1,0:T(8,128)S(1)}, f32[2,8,1024]{2,1,0:T(8,128)S(1)}, u32[]{:S(2)}, u32[]{:S(2)}) %collective-permute-start.10) | collective-permute-done | bytes 65568 | tf_op jit(solution)/shard_map/ppermute | solution.py:471
  9.1 4.1 %collective-permute-start.12 = (bf16[128,1024]{1,0:T(8,128)(2,1)S(1)}, bf16[128,1024]{1,0:T(8,128)(2,1)S(1)}, u32[]{:S(2)}, u32[]{:S(2)}) collective-permute-start(bf16[128,1024]{1,0:T(8,128)(2,1)S(1)} %get-tuple-element.196), channel_id=1, source_target_pairs={{0,1},{1,0},{2,3},{3,2},{4,5},{5,4},{6,7},{7,6},{8,9},{9,8},{10,11... | collective-permute-start | bytes 786440 | tf_op jit(solution)/shard_map/ppermute | solution.py:468
  13.2 1.5 %collective-permute-start.13 = (bf16[128,1024]{1,0:T(8,128)(2,1)S(1)}, bf16[128,1024]{1,0:T(8,128)(2,1)S(1)}, u32[]{:S(2)}, u32[]{:S(2)}) collective-permute-start(bf16[128,1024]{1,0:T(8,128)(2,1)S(1)} %get-tuple-element.197), channel_id=1, source_target_pairs={{0,2},{1,3},{2,0},{3,1},{4,6},{5,7},{6,4},{7,5},{8,10},{9,11},{10,... | collective-permute-start | bytes 786440 | tf_op jit(solution)/shard_map/ppermute | solution.py:468
  14.7 3.4 %shard_map.67 = (bf16[288,1024]{1,0:T(8,128)(2,1)S(1)}, f32[24,1024]{1,0:T(8,128)S(1)}) custom-call(s32[1]{0:T(128)} %bitcast.info, bf16[3,128,4096]{2,1,0:T(8,128)(2,1)} %bitcast.6, bf16[3,128,4096]{2,1,0:T(8,128)(2,1)} %bitcast.7, bf16[2,128,2048]{2,1,0:T(8,128)(2,1)S(1)} %collective-permute-done.7.kv_in, ...), custom_call_target="tpu_custom_call" | custom-call | flops 1 | bytes 1 | tf_op jit(solution)/shard_map/pallas_call | solution.py:190
  18.7 4.0 %shard_map.66 = (bf16[288,1024]{1,0:T(8,128)(2,1)}, f32[24,1024]{1,0:T(8,128)S(1)}) custom-call(s32[1]{0:T(128)} %bitcast.info, bf16[3,128,4096]{2,1,0:T(8,128)(2,1)} %bitcast.8, bf16[3,128,4096]{2,1,0:T(8,128)(2,1)} %bitcast.9, bf16[2,128,2048]{2,1,0:T(8,128)(2,1)S(1)} %collective-permute-done.7.kv_in, ...), custom_call_target="tpu_custom_call" | custom-call | flops 1 | bytes 1 | tf_op jit(solution)/shard_map/pallas_call | solution.py:190
  23.6 1.6 %collective-permute-start.14 = (bf16[288,1024]{1,0:T(8,128)(2,1)S(1)}, bf16[288,1024]{1,0:T(8,128)(2,1)S(1)}, u32[]{:S(2)}, u32[]{:S(2)}) collective-permute-start(bf16[288,1024]{1,0:T(8,128)(2,1)S(1)} %get-tuple-element.200), channel_id=1, source_target_pairs={{0,2},{1,3},{2,0},{3,1},{4,6},{5,7},{6,4},{7,5},{8,10},{9,11},{10,... | collective-permute-start | bytes 1769480 | tf_op jit(solution)/shard_map/ppermute | solution.py:468
  25.2 16.0 %conditional.4 = (f32[16,1024]{1,0:T(8,128)S(1)}, bf16[8192,128]{1,0:T(8,128)(2,1)}) conditional(s32[]{:T(128)} %convert_element_type.54, f32[16,1024]{1,0:T(8,128)S(1)} %get-tuple-element.201.rest_4_, (f32[16,1024]{1,0:T(8,128)S(1)}, s32[]{:T(128)}, s32[]{:T(128)}, f32[24,1024]{1,0:T(8,128)S(1)}, f32[24,1024]{1,0:T(8,128)S(1)}, /*index=5*/s32[]{:T(128)}, ...), branch_computations={%region_0.1_spmd, %region_1.2_spmd} | conditional | flops 540727 | bytes 2359982 | solution.py:539
  25.2 1.6 %collective-permute-start = (f32[16,1024]{1,0:T(8,128)S(1)}, f32[16,1024]{1,0:T(8,128)S(1)}, u32[]{:S(2)}, u32[]{:S(2)}) collective-permute-start(f32[16,1024]{1,0:T(8,128)S(1)} %get-tuple-element.101), channel_id=1, source_target_pairs={{0,4},{4,0},{8,12},{12,8},{16,20},{20,16},{24,28},{28,24},{1,5},{5... | collective-permute-start | bytes 196616 | tf_op jit(solution)/shard_map/cond/branch_1_fun/ppermute | solution.py:474
  26.8 2.2 %branch_1_fun.6.rest_0_ = bf16[8192,128]{1,0:T(8,128)(2,1)} custom-call(f32[1,1024]{1,0:T(1,128)S(1)} %get-tuple-element.104.rate_row, f32[1,1024]{1,0:T(1,128)S(1)} %get-tuple-element.105.coef_row), custom_call_target="tpu_custom_call" | custom-call | flops 1 | bytes 1 | tf_op jit(solution)/shard_map/cond/branch_1_fun/pallas_call | solution.py:226
  29.0 1.1 %collective-permute-done = f32[16,1024]{1,0:T(8,128)S(1)} collective-permute-done((f32[16,1024]{1,0:T(8,128)S(1)}, f32[16,1024]{1,0:T(8,128)S(1)}, u32[]{:S(2)}, u32[]{:S(2)}) %collective-permute-start) | collective-permute-done | bytes 65568 | tf_op jit(solution)/shard_map/cond/branch_1_fun/ppermute | solution.py:474
  30.2 1.5 %collective-permute-start.1 = (f32[16,1024]{1,0:T(8,128)S(1)}, f32[16,1024]{1,0:T(8,128)S(1)}, u32[]{:S(2)}, u32[]{:S(2)}) collective-permute-start(f32[16,1024]{1,0:T(8,128)S(1)} %add_select_fusion.1), channel_id=1, source_target_pairs={{0,8},{4,12},{8,0},{12,4},{16,24},{20,28},{24,16},{28,20},{1,9},{5... | collective-permute-start | bytes 196616 | tf_op jit(solution)/shard_map/cond/branch_1_fun/ppermute | solution.py:474
  31.6 2.2 %branch_1_fun.7 = bf16[8192,128]{1,0:T(8,128)(2,1)} custom-call(f32[1,1024]{1,0:T(1,128)S(1)} %get-tuple-element.104.rate_row, f32[1,1024]{1,0:T(1,128)S(1)} %get-tuple-element.105.coef_row, bf16[8192,128]{1,0:T(8,128)(2,1)} %branch_1_fun.6.rest_0_), custom_call_target="tpu_custom_call", output_to_operand_aliasing={{}: (2, {})} | custom-call | flops 1 | bytes 1 | tf_op jit(solution)/shard_map/cond/branch_1_fun/pallas_call | solution.py:226
  34.5 2.8 %collective-permute-start.2 = (f32[16,1024]{1,0:T(8,128)S(1)}, f32[16,1024]{1,0:T(8,128)S(1)}, u32[]{:S(2)}, u32[]{:S(2)}) collective-permute-start(f32[16,1024]{1,0:T(8,128)S(1)} %add_select_fusion), channel_id=1, source_target_pairs={{0,16},{4,20},{8,24},{12,28},{16,0},{20,4},{24,8},{28,12},{1,17},{... | collective-permute-start | bytes 196616 | tf_op jit(solution)/shard_map/cond/branch_1_fun/ppermute | solution.py:474
  37.3 3.8 %collective-permute-done.2 = f32[16,1024]{1,0:T(8,128)S(1)} collective-permute-done((f32[16,1024]{1,0:T(8,128)S(1)}, f32[16,1024]{1,0:T(8,128)S(1)}, u32[]{:S(2)}, u32[]{:S(2)}) %collective-permute-start.2) | collective-permute-done | bytes 65568 | tf_op jit(solution)/shard_map/cond/branch_1_fun/ppermute | solution.py:474
  41.2 2.7 %shard_map.68.long_in = f32[256,1024]{1,0:T(8,128)S(1)} custom-call(bf16[288,1024]{1,0:T(8,128)(2,1)S(1)} %collective-permute-done.14.prod.second, bf16[8192,128]{1,0:T(8,128)(2,1)} %get-tuple-element.206.toep), custom_call_target="tpu_custom_call" | custom-call | flops 1 | bytes 1 | tf_op jit(solution)/shard_map/pallas_call | solution.py:255
  43.9 3.9 %shard_map.69 = (bf16[256,1024]{1,0:T(8,128)(2,1)S(1)}, bf16[128,1536]{1,0:T(8,128)(2,1)S(1)}, bf16[128,1536]{1,0:T(8,128)(2,1)S(1)}) custom-call(s32[1]{0:T(128)} %bitcast.info, f32[256,1024]{1,0:T(8,128)S(1)} %shard_map.68.long_in, bf16[288,1024]{1,0:T(8,128)(2,1)S(1)} %collective-permute-done.14.prod.second, ...), custom_call_target="tpu_custom_call" | custom-call | flops 1 | bytes 1 | tf_op jit(solution)/shard_map/pallas_call | solution.py:369
  47.9 1.7 %collective-permute-done.16 = bf16[128,1536]{1,0:T(8,128)(2,1)S(1)} collective-permute-done((bf16[128,1536]{1,0:T(8,128)(2,1)S(1)}, bf16[128,1536]{1,0:T(8,128)(2,1)S(1)}, u32[]{:S(2)}, u32[]{:S(2)}) %collective-permute-start.16) | collective-permute-done | bytes 393248 | tf_op jit(solution)/shard_map/ppermute | solution.py:468
  50.5 5.2 %conditional.5 = (bf16[128,1536]{1,0:T(8,128)(2,1)}) conditional(s32[]{:T(128)} %convert_element_type.54, () %tuple.56, (bf16[256,1024]{1,0:T(8,128)(2,1)S(1)}, bf16[1024,4096]{1,0:T(8,128)(2,1)}) %tuple.57), branch_computations={%region_2.3_spmd, %region_3.4_spmd} | conditional | flops 786433 | bytes 2752561 | solution.py:577
  50.5 2.6 %branch_1_fun.8 = (bf16[128,1536]{1,0:T(8,128)(2,1)S(1)}, bf16[128,1536]{1,0:T(8,128)(2,1)S(1)}) custom-call(bf16[256,1024]{1,0:T(8,128)(2,1)S(1)} %get-tuple-element.112.gated, bf16[1024,4096]{1,0:T(8,128)(2,1)} %get-tuple-element.113.weights), custom_call_target="tpu_custom_call" | custom-call | flops 1 | bytes 1 | tf_op jit(solution)/shard_map/cond/branch_1_fun/pallas_call | solution.py:412
  53.2 1.6 %collective-permute-done.3 = bf16[128,1536]{1,0:T(8,128)(2,1)S(1)} collective-permute-done((bf16[128,1536]{1,0:T(8,128)(2,1)S(1)}, bf16[128,1536]{1,0:T(8,128)(2,1)S(1)}, u32[]{:S(2)}, u32[]{:S(2)}) %collective-permute-start.3) | collective-permute-done | bytes 393248 | tf_op jit(solution)/shard_map/cond/branch_1_fun/ppermute | solution.py:468
  55.7 1.3 %collective-permute-start.18 = (bf16[128,1536]{1,0:T(8,128)(2,1)}, bf16[128,1536]{1,0:T(8,128)(2,1)S(1)}, u32[]{:S(2)}, u32[]{:S(2)}) collective-permute-start(bf16[128,1536]{1,0:T(8,128)(2,1)} %get-tuple-element.235), channel_id=1, source_target_pairs={{0,2},{1,3},{2,0},{3,1},{4,6},{5,7},{6,4},{7,5},{8,10},{9,11},{10,... | collective-permute-start | bytes 1179656 | tf_op jit(solution)/shard_map/ppermute | solution.py:471
  57.0 4.5 %conditional.6 = (bf16[128,1024]{1,0:T(8,128)(2,1)}) conditional(s32[]{:T(128)} %convert_element_type.54, () %tuple.53, (bf16[256,1024]{1,0:T(8,128)(2,1)S(1)}, bf16[1024,4096]{1,0:T(8,128)(2,1)}) %tuple.59), branch_computations={%region_4.5_spmd, %region_5.6_spmd} | conditional | flops 524289 | bytes 1835057 | solution.py:577
  57.0 2.1 %branch_1_fun.9 = (bf16[128,1024]{1,0:T(8,128)(2,1)S(1)}, bf16[128,1024]{1,0:T(8,128)(2,1)S(1)}) custom-call(bf16[256,1024]{1,0:T(8,128)(2,1)S(1)} %get-tuple-element.116.gated, bf16[1024,4096]{1,0:T(8,128)(2,1)} %get-tuple-element.117.weights), custom_call_target="tpu_custom_call" | custom-call | flops 1 | bytes 1 | tf_op jit(solution)/shard_map/cond/branch_1_fun/pallas_call | solution.py:412
  59.2 1.5 %collective-permute-done.4 = bf16[128,1024]{1,0:T(8,128)(2,1)S(1)} collective-permute-done((bf16[128,1024]{1,0:T(8,128)(2,1)S(1)}, bf16[128,1024]{1,0:T(8,128)(2,1)S(1)}, u32[]{:S(2)}, u32[]{:S(2)}) %collective-permute-start.4) | collective-permute-done | bytes 262176 | tf_op jit(solution)/shard_map/cond/branch_1_fun/ppermute | solution.py:468
  62.4 11.1 %conditional.7 = (f32[128,4096]{1,0:T(8,128)S(1)}) conditional(s32[]{:T(128)} %convert_element_type.54, () %tuple.50, (bf16[128,4096]{1,0:T(8,128)(2,1)}, s32[1]{0:T(128)}, bf16[288,1024]{1,0:T(8,128)(2,1)}, bf16[8192,128]{1,0:T(8,128)(2,1)}, bf16[128,1024]{1,0:T(8,128)(2,1)}, /*index=5*/bf16[3,128,4096]{2,1,0:T(8,128)(2,1)}, ...), branch_computations={%region_6.7_spmd, %region_7.8_spmd} | conditional | flops 3145730 | bytes 17825910 | solution.py:580
  62.4 5.5 %branch_1_fun.10 = (bf16[256,1024]{1,0:T(8,128)(2,1)S(1)}, bf16[128,2048]{1,0:T(8,128)(2,1)S(1)}, bf16[128,2048]{1,0:T(8,128)(2,1)S(1)}) custom-call(s32[1]{0:T(128)} %get-tuple-element.121.info, bf16[288,1024]{1,0:T(8,128)(2,1)} %get-tuple-element.122.long_in, bf16[8192,128]{1,0:T(8,128)(2,1)} %get-tuple-element.123.second, ...), custom_call_target="tpu_custom_call" | custom-call | flops 1 | bytes 1 | tf_op jit(solution)/shard_map/cond/branch_1_fun/pallas_call | solution.py:369
  68.0 3.0 %branch_1_fun.11 = (bf16[128,2048]{1,0:T(8,128)(2,1)S(1)}, bf16[128,2048]{1,0:T(8,128)(2,1)S(1)}) custom-call(bf16[256,1024]{1,0:T(8,128)(2,1)S(1)} %get-tuple-element.136.gated, bf16[1024,4096]{1,0:T(8,128)(2,1)} %get-tuple-element.133.rest_7_.weights), custom_call_target="tpu_custom_call" | custom-call | flops 1 | bytes 1 | tf_op jit(solution)/shard_map/cond/branch_1_fun/pallas_call | solution.py:412
  71.8 1.4 %collective-permute-done.6 = bf16[128,2048]{1,0:T(8,128)(2,1)S(1)} collective-permute-done((bf16[128,2048]{1,0:T(8,128)(2,1)S(1)}, bf16[128,2048]{1,0:T(8,128)(2,1)S(1)}, u32[]{:S(2)}, u32[]{:S(2)}) %collective-permute-start.6) | collective-permute-done | bytes 524320 | tf_op jit(solution)/shard_map/cond/branch_1_fun/ppermute | solution.py:468
  73.5 1.4 %collective-permute-done.19.rest_2_ = bf16[128,1024]{1,0:T(8,128)(2,1)S(1)} collective-permute-done((bf16[128,1024]{1,0:T(8,128)(2,1)}, bf16[128,1024]{1,0:T(8,128)(2,1)S(1)}, u32[]{:S(2)}, u32[]{:S(2)}) %collective-permute-start.19) | collective-permute-done | bytes 262176 | tf_op jit(solution)/shard_map/ppermute | solution.py:471
  75.0 1.0 %shard_map.70 = bf16[128,4096]{1,0:T(8,128)(2,1)} custom-call(f32[128,4096]{1,0:T(8,128)S(1)} %get-tuple-element.237.base, bf16[128,1536]{1,0:T(8,128)(2,1)S(1)} %collective-permute-done.17.rest_0_, bf16[128,1536]{1,0:T(8,128)(2,1)S(1)} %collective-permute-done.18.rest_1_, bf16[128,1024]{1,0:T(8,128)(2,1)S(1)} %collective-permute-done.19.rest_2_), custom_call_target="tpu_custom_call" | custom-call | flops 1 | bytes 1 | tf_op jit(solution)/shard_map/pallas_call | solution.py:445
  (38 shorter events, 8.9 us)
Async XLA Ops:
  1.7 7.3 %collective-permute-start.7 = (bf16[2,128,2048]{2,1,0:T(8,128)(2,1)S(1)}, bf16[2,128,2048]{2,1,0:T(8,128)(2,1)S(1)}, u32[]{:S(2)}, u32[]{:S(2)}) collective-permute-start(bf16[2,128,2048]{2,1,0:T(8,128)(2,1)S(1)} %get-tuple-element.180), channel_id=1, source_target_pairs={{0,1},{1,0},{2,3},{3,2},{4,5},{5,4},{6,7},{7,6},{8,9},{9,8},{10,11... | collective-permute-start | bytes 3145736 | tf_op jit(solution)/shard_map/ppermute | solution.py:468
  2.3 6.8 %collective-permute-start.8 = (bf16[3,8,2048]{2,1,0:T(8,128)(2,1)S(1)}, bf16[3,8,2048]{2,1,0:T(8,128)(2,1)S(1)}, u32[]{:S(2)}, u32[]{:S(2)}) collective-permute-start(bf16[3,8,2048]{2,1,0:T(8,128)(2,1)S(1)} %get-tuple-element.181), channel_id=1, source_target_pairs={{1,2},{3,4},{5,6},{7,8},{9,10},{11,12},{13,14},{15,16},{17,18},{19... | collective-permute-start | bytes 294920 | tf_op jit(solution)/shard_map/ppermute | solution.py:490
  2.9 6.2 %collective-permute-start.9 = (bf16[3,8,2048]{2,1,0:T(8,128)(2,1)S(1)}, bf16[3,8,2048]{2,1,0:T(8,128)(2,1)S(1)}, u32[]{:S(2)}, u32[]{:S(2)}) collective-permute-start(bf16[3,8,2048]{2,1,0:T(8,128)(2,1)S(1)} %get-tuple-element.182), channel_id=1, source_target_pairs={{1,3},{3,5},{5,7},{7,9},{9,11},{11,13},{13,15},{15,17},{17,19},{19... | collective-permute-start | bytes 294920 | tf_op jit(solution)/shard_map/ppermute | solution.py:490
  3.6 5.5 %collective-permute-start.10 = (f32[2,8,1024]{2,1,0:T(8,128)S(1)}, f32[2,8,1024]{2,1,0:T(8,128)S(1)}, u32[]{:S(2)}, u32[]{:S(2)}) collective-permute-start(f32[2,8,1024]{2,1,0:T(8,128)S(1)} %get-tuple-element.190.taps), channel_id=1, source_target_pairs={{0,2},{1,3},{2,0},{3,1},{4,6},{5,7},{6,4},{7,5},{8,10},{9,11},{10,... | collective-permute-start | bytes 196616 | tf_op jit(solution)/shard_map/ppermute | solution.py:471
  9.1 14.5 %collective-permute-start.12 = (bf16[128,1024]{1,0:T(8,128)(2,1)S(1)}, bf16[128,1024]{1,0:T(8,128)(2,1)S(1)}, u32[]{:S(2)}, u32[]{:S(2)}) collective-permute-start(bf16[128,1024]{1,0:T(8,128)(2,1)S(1)} %get-tuple-element.196), channel_id=1, source_target_pairs={{0,1},{1,0},{2,3},{3,2},{4,5},{5,4},{6,7},{7,6},{8,9},{9,8},{10,11... | collective-permute-start | bytes 786440 | tf_op jit(solution)/shard_map/ppermute | solution.py:468
  13.2 10.4 %collective-permute-start.13 = (bf16[128,1024]{1,0:T(8,128)(2,1)S(1)}, bf16[128,1024]{1,0:T(8,128)(2,1)S(1)}, u32[]{:S(2)}, u32[]{:S(2)}) collective-permute-start(bf16[128,1024]{1,0:T(8,128)(2,1)S(1)} %get-tuple-element.197), channel_id=1, source_target_pairs={{0,2},{1,3},{2,0},{3,1},{4,6},{5,7},{6,4},{7,5},{8,10},{9,11},{10,... | collective-permute-start | bytes 786440 | tf_op jit(solution)/shard_map/ppermute | solution.py:468
  18.1 5.5 %collective-permute-start.11 = (f32[24,1024]{1,0:T(8,128)S(1)}, f32[24,1024]{1,0:T(8,128)S(1)}, u32[]{:S(2)}, u32[]{:S(2)}) collective-permute-start(f32[24,1024]{1,0:T(8,128)S(1)} %get-tuple-element.193), channel_id=1, source_target_pairs={{0,2},{1,3},{2,0},{3,1},{4,6},{5,7},{6,4},{7,5},{8,10},{9,11},{10,... | collective-permute-start | bytes 294920 | tf_op jit(solution)/shard_map/ppermute | solution.py:468
  23.6 1.6 %copy-start.1 = (bf16[128,1024]{1,0:T(8,128)(2,1)}, bf16[128,1024]{1,0:T(8,128)(2,1)S(1)}, u32[]{:S(2)}) copy-start(bf16[128,1024]{1,0:T(8,128)(2,1)S(1)} %collective-permute-done.12) | copy-start | bytes 786436
  23.6 17.6 %collective-permute-start.14 = (bf16[288,1024]{1,0:T(8,128)(2,1)S(1)}, bf16[288,1024]{1,0:T(8,128)(2,1)S(1)}, u32[]{:S(2)}, u32[]{:S(2)}) collective-permute-start(bf16[288,1024]{1,0:T(8,128)(2,1)S(1)} %get-tuple-element.200), channel_id=1, source_target_pairs={{0,2},{1,3},{2,0},{3,1},{4,6},{5,7},{6,4},{7,5},{8,10},{9,11},{10,... | collective-permute-start | bytes 1769480 | tf_op jit(solution)/shard_map/ppermute | solution.py:468
  25.1 18.8 %collective-permute-start.15 = (bf16[128,1024]{1,0:T(8,128)(2,1)S(1)}, bf16[128,1024]{1,0:T(8,128)(2,1)S(1)}, u32[]{:S(2)}, u32[]{:S(2)}) collective-permute-start(bf16[128,1024]{1,0:T(8,128)(2,1)S(1)} %get-tuple-element.207), channel_id=1, source_target_pairs={{0,3},{1,2},{2,1},{3,0},{4,7},{5,6},{6,5},{7,4},{8,11},{9,10},{10,... | collective-permute-start | bytes 786440 | tf_op jit(solution)/shard_map/ppermute | solution.py:468
  25.2 4.9 %collective-permute-start = (f32[16,1024]{1,0:T(8,128)S(1)}, f32[16,1024]{1,0:T(8,128)S(1)}, u32[]{:S(2)}, u32[]{:S(2)}) collective-permute-start(f32[16,1024]{1,0:T(8,128)S(1)} %get-tuple-element.101), channel_id=1, source_target_pairs={{0,4},{4,0},{8,12},{12,8},{16,20},{20,16},{24,28},{28,24},{1,5},{5... | collective-permute-start | bytes 196616 | tf_op jit(solution)/shard_map/cond/branch_1_fun/ppermute | solution.py:474
  30.2 4.3 %collective-permute-start.1 = (f32[16,1024]{1,0:T(8,128)S(1)}, f32[16,1024]{1,0:T(8,128)S(1)}, u32[]{:S(2)}, u32[]{:S(2)}) collective-permute-start(f32[16,1024]{1,0:T(8,128)S(1)} %add_select_fusion.1), channel_id=1, source_target_pairs={{0,8},{4,12},{8,0},{12,4},{16,24},{20,28},{24,16},{28,20},{1,9},{5... | collective-permute-start | bytes 196616 | tf_op jit(solution)/shard_map/cond/branch_1_fun/ppermute | solution.py:474
  34.5 6.6 %collective-permute-start.2 = (f32[16,1024]{1,0:T(8,128)S(1)}, f32[16,1024]{1,0:T(8,128)S(1)}, u32[]{:S(2)}, u32[]{:S(2)}) collective-permute-start(f32[16,1024]{1,0:T(8,128)S(1)} %add_select_fusion), channel_id=1, source_target_pairs={{0,16},{4,20},{8,24},{12,28},{16,0},{20,4},{24,8},{28,12},{1,17},{... | collective-permute-start | bytes 196616 | tf_op jit(solution)/shard_map/cond/branch_1_fun/ppermute | solution.py:474
  47.8 1.8 %collective-permute-start.16 = (bf16[128,1536]{1,0:T(8,128)(2,1)S(1)}, bf16[128,1536]{1,0:T(8,128)(2,1)S(1)}, u32[]{:S(2)}, u32[]{:S(2)}) collective-permute-start(bf16[128,1536]{1,0:T(8,128)(2,1)S(1)} %get-tuple-element.212), channel_id=1, source_target_pairs={{0,1},{1,0},{2,3},{3,2},{4,5},{5,4},{6,7},{7,6},{8,9},{9,8},{10,11... | collective-permute-start | bytes 1179656 | tf_op jit(solution)/shard_map/ppermute | solution.py:468
  49.7 12.0 %collective-permute-start.17 = (bf16[128,1536]{1,0:T(8,128)(2,1)S(1)}, bf16[128,1536]{1,0:T(8,128)(2,1)S(1)}, u32[]{:S(2)}, u32[]{:S(2)}) collective-permute-start(bf16[128,1536]{1,0:T(8,128)(2,1)S(1)} %add_convert_fusion.2), channel_id=1, source_target_pairs={{0,2},{1,3},{2,0},{3,1},{4,6},{5,7},{6,4},{7,5},{8,10},{9,11},{10,... | collective-permute-start | bytes 1179656 | tf_op jit(solution)/shard_map/ppermute | solution.py:471
  53.1 1.8 %collective-permute-start.3 = (bf16[128,1536]{1,0:T(8,128)(2,1)S(1)}, bf16[128,1536]{1,0:T(8,128)(2,1)S(1)}, u32[]{:S(2)}, u32[]{:S(2)}) collective-permute-start(bf16[128,1536]{1,0:T(8,128)(2,1)S(1)} %get-tuple-element.115), channel_id=1, source_target_pairs={{0,1},{1,0},{2,3},{3,2},{4,5},{5,4},{6,7},{7,6},{8,9},{9,8},{10,11... | collective-permute-start | bytes 1179656 | tf_op jit(solution)/shard_map/cond/branch_1_fun/ppermute | solution.py:468
  55.7 17.8 %collective-permute-start.18 = (bf16[128,1536]{1,0:T(8,128)(2,1)}, bf16[128,1536]{1,0:T(8,128)(2,1)S(1)}, u32[]{:S(2)}, u32[]{:S(2)}) collective-permute-start(bf16[128,1536]{1,0:T(8,128)(2,1)} %get-tuple-element.235), channel_id=1, source_target_pairs={{0,2},{1,3},{2,0},{3,1},{4,6},{5,7},{6,4},{7,5},{8,10},{9,11},{10,... | collective-permute-start | bytes 1179656 | tf_op jit(solution)/shard_map/ppermute | solution.py:471
  59.1 1.6 %collective-permute-start.4 = (bf16[128,1024]{1,0:T(8,128)(2,1)S(1)}, bf16[128,1024]{1,0:T(8,128)(2,1)S(1)}, u32[]{:S(2)}, u32[]{:S(2)}) collective-permute-start(bf16[128,1024]{1,0:T(8,128)(2,1)S(1)} %get-tuple-element.119), channel_id=1, source_target_pairs={{0,1},{1,0},{2,3},{3,2},{4,5},{5,4},{6,7},{7,6},{8,9},{9,8},{10,11... | collective-permute-start | bytes 786440 | tf_op jit(solution)/shard_map/cond/branch_1_fun/ppermute | solution.py:468
  61.7 13.2 %collective-permute-start.19 = (bf16[128,1024]{1,0:T(8,128)(2,1)}, bf16[128,1024]{1,0:T(8,128)(2,1)S(1)}, u32[]{:S(2)}, u32[]{:S(2)}) collective-permute-start(bf16[128,1024]{1,0:T(8,128)(2,1)} %get-tuple-element.236), channel_id=1, source_target_pairs={{0,2},{1,3},{2,0},{3,1},{4,6},{5,7},{6,4},{7,5},{8,10},{9,11},{10,... | collective-permute-start | bytes 786440 | tf_op jit(solution)/shard_map/ppermute | solution.py:471
  68.0 3.7 %collective-permute-start.5 = (bf16[128,2048]{1,0:T(8,128)(2,1)S(1)}, bf16[128,2048]{1,0:T(8,128)(2,1)S(1)}, u32[]{:S(2)}, u32[]{:S(2)}) collective-permute-start(bf16[128,2048]{1,0:T(8,128)(2,1)S(1)} %get-tuple-element.135), channel_id=1, source_target_pairs={{0,1},{1,0},{2,3},{3,2},{4,5},{5,4},{6,7},{7,6},{8,9},{9,8},{10,11... | collective-permute-start | bytes 1572872 | tf_op jit(solution)/shard_map/cond/branch_1_fun/ppermute | solution.py:468
  71.1 2.1 %collective-permute-start.6 = (bf16[128,2048]{1,0:T(8,128)(2,1)S(1)}, bf16[128,2048]{1,0:T(8,128)(2,1)S(1)}, u32[]{:S(2)}, u32[]{:S(2)}) collective-permute-start(bf16[128,2048]{1,0:T(8,128)(2,1)S(1)} %get-tuple-element.138), channel_id=1, source_target_pairs={{0,1},{1,0},{2,3},{3,2},{4,5},{5,4},{6,7},{7,6},{8,9},{9,8},{10,11... | collective-permute-start | bytes 1572872 | tf_op jit(solution)/shard_map/cond/branch_1_fun/ppermute | solution.py:468
  71.6 1.7 %copy-start = (bf16[128,4096]{1,0:T(8,128)(2,1)S(1)}, bf16[128,4096]{1,0:T(8,128)(2,1)}, u32[]{:S(2)}) copy-start(bf16[128,4096]{1,0:T(8,128)(2,1)} %get-tuple-element.224) | copy-start | bytes 3145732 | tf_op jit(solution)/shard_map/cond
